TPU v7x, 32 devices: a whole 2x2x4 slice. The times are simulated.
32 devices in a mesh: expert: 4 (over z), ctx: 4 (over y, x), dp: 2 (over core).
Axes of the slice: x: 2, y: 2, z: 4, core: 2. Of those that a mesh axis runs over, the one named last changes fastest.
Arguments:
- tokens: bfloat16 [96, 256, 512], P(('expert', 'dp'), 'ctx'), may hold values from -6 to 6
- cotangent: bfloat16 [96, 256, 512], P(('expert', 'dp'), 'ctx'), may hold values from -6 to 6
- key_mask: int32 [96, 256], P(('expert', 'dp'), 'ctx'), may hold values from 0 to 1, as said below
- route_ids: int32 [96, 256, 2], P(('expert', 'dp'), 'ctx'), may hold values from 0 to 3, all different within a row
- priority: int32 [96, 256], P(('expert', 'dp'), 'ctx'), may hold values from 0 to 1023
- norm1_gain: float32 [512], replicated, may hold values from 0.5 to 1.5
- norm1_bias: float32 [512], replicated, may hold values from -1.75 to 1.75
- qkv_weight: bfloat16 [512, 1536], replicated, may hold values from -0.25 to 0.25
- query_bias: float32 [512], replicated, may hold values from -3 to 3
- value_bias: float32 [512], replicated, may hold values from -3 to 3
- proj_weight: bfloat16 [512, 512], replicated, may hold values from -1.5 to 1.5
- proj_bias: float32 [512], replicated, may hold values from -1.75 to 1.75
- norm2_gain: float32 [512], replicated, may hold values from 0.5 to 1.5
- norm2_bias: float32 [512], replicated, may hold values from -1.75 to 1.75
- router_weight: bfloat16 [512, 4], replicated, may hold values from -0.1875 to 0.1875
- expert_up: bfloat16 [4, 512, 2048], P('expert'), may hold values from -0.25 to 0.25
- expert_up_bias: float32 [4, 2048], P('expert'), may hold values from -1.75 to 1.75
- expert_down: bfloat16 [4, 2048, 512], P('expert'), may hold values from -0.25 to 0.25
- expert_down_bias: float32 [4, 512], P('expert'), may hold values from -0.625 to 0.625
Outputs:
- block_out: bfloat16 [96, 256, 512], P(('expert', 'dp'), 'ctx')
- input_grad: bfloat16 [96, 256, 512], P(('expert', 'dp'), 'ctx')
- grad_norm1_gain: float32 [512], P('expert')
- grad_norm1_bias: float32 [512], P('expert')
- grad_qkv: float32 [512, 1536], P('expert')
- grad_query_bias: float32 [512], P('expert')
- grad_value_bias: float32 [512], P('expert')
- grad_proj: float32 [512, 512], P('expert')
- grad_proj_bias: float32 [512], P('expert')
- grad_norm2_gain: float32 [512], P('expert')
- grad_norm2_bias: float32 [512], P('expert')
- grad_router: float32 [512, 4], P('expert')
- grad_up: float32 [4, 512, 2048], P('expert')
- grad_up_bias: float32 [4, 2048], P('expert')
- grad_down: float32 [4, 2048, 512], P('expert')
- grad_down_bias: float32 [4, 512], P('expert')
Inputs may be any that keep to these rules, and one draw needn't show every extreme that they name: `key_mask`: in each image the first few keys are 1 and the rest 0; more than 192 are 1. `route_ids`: the two routes of a token name different experts.
All inputs are finite; a program needn't handle non-finite values.
Results may differ from a plain program's by a relative error of at most 0.019.
Values may be sent and summed in bfloat16 or wider, within the bound.
No kernel may reach another device: no remote copies, remote signals or barrier semaphores. Data moves between devices by JAX's collectives and lax.ppermute only.
A program may use at most 192 MiB of HBM per device.

v0:
```python
import jax
import jax.numpy as jnp
from jax import lax
from jax.experimental import pallas as pl
from jax.experimental.pallas import tpu as pltpu
from jax.sharding import PartitionSpec as P

HEADS = 8
EPS = 1e-06
NEG = -1e30
F32 = jnp.float32
BF16 = jnp.bfloat16
I32 = jnp.int32
LANES = 128
PAD = 16
VMEM_LIMIT = 58 * 2**20
EXPERT_CALLS = 4


def dot_nn(a, b):
    return lax.dot_general(a, b, (((1,), (0,)), ((), ())), preferred_element_type=F32)


def dot_nt(a, b):
    return lax.dot_general(a, b, (((1,), (1,)), ((), ())), preferred_element_type=F32)


def iota(shape, axis):
    return lax.broadcasted_iota(I32, shape, axis)


def norm_stats(v):
    centre = v - jnp.mean(v, axis=1, keepdims=True)
    inv = lax.rsqrt(jnp.mean(centre * centre, axis=1, keepdims=True) + EPS)
    return centre * inv, inv


def norm_back(gy, xhat, inv):
    return (
        gy - jnp.mean(gy, axis=1, keepdims=True) - xhat * jnp.mean(gy * xhat, axis=1, keepdims=True)
    ) * inv


def soft_gates(logits, expert_count):
    logits = jnp.where(iota(logits.shape, 1) < expert_count, logits, NEG)
    e = jnp.exp(logits - jnp.max(logits, axis=1, keepdims=True))
    return e / jnp.sum(e, axis=1, keepdims=True)


ERF = (0.254829592, -0.284496736, 1.421413741, -1.453152027, 1.061405429)
ERF_P = 0.3275911 * 0.7071067811865476


def gelu_parts(h):
    t = 1.0 / (1.0 + ERF_P * jnp.abs(h))
    e = jnp.exp(-0.5 * h * h)
    poly = 0.5 * ERF[4]
    for c in ERF[3::-1]:
        poly = poly * t + 0.5 * c
    tail = poly * t * e
    cdf = jnp.where(h >= 0, 1.0 - tail, tail)
    return h * cdf, cdf + h * (e * 0.3989422804014327)


def params(**kw):
    return pltpu.CompilerParams(vmem_limit_bytes=VMEM_LIMIT, **kw)


def takes(us):
    return pl.CostEstimate(flops=int(us * 1.15e9), bytes_accessed=1 << 17, transcendentals=0)


ANY_SPEC = pl.BlockSpec(memory_space=pl.ANY)
SMEM_SPEC = pl.BlockSpec(memory_space=pltpu.SMEM)
VMEM_SPEC = pl.BlockSpec(memory_space=pltpu.VMEM)


def shape(dims, dtype):
    return jax.ShapeDtypeStruct(dims, dtype)


def route_call(place, ints, cotangent, expert_count, capacity):
    groups, group_rows, width = cotangent.shape
    tok = groups * group_rows
    e_rows = max(PAD, expert_count)

    def kernel(place_ref, ints_ref, cot_ref, *outs):
        row_ref, col_ref = outs[:2]
        slots = outs[2:]
        ctx, expert = place_ref[0], place_ref[1]
        vals = ints_ref[...]
        ids = (vals[0:1], vals[1:2])
        key = vals[2:3]
        keys = jnp.broadcast_to(key.astype(F32), (8, tok))
        key_col = keys.T[:, :1]
        before = (key_col < keys[:1]).astype(BF16)
        hot = [(iota((e_rows, tok), 0) == i).astype(F32) for i in ids]
        counts = dot_nn(jnp.concatenate(hot, axis=0).astype(BF16), before)
        first_total = jnp.sum(hot[0], axis=1, keepdims=True)
        ranks = (
            jnp.sum(hot[0] * counts[:e_rows], axis=0, keepdims=True),
            jnp.sum(hot[1] * (counts[e_rows:] + first_total), axis=0, keepdims=True),
        )
        dest = [
            jnp.where(r < capacity, i.astype(F32) * capacity + r, -1.0)
            for r, i in zip(ranks, ids)
        ]
        rows = jnp.concatenate(
            [dest[0], dest[1], jnp.full((6, tok), -1.0, F32)], axis=0
        )
        row_ref[...] = rows.astype(I32)
        col_ref[...] = rows.T.astype(I32)
        d0, d1 = dest[0].astype(I32), dest[1].astype(I32)
        up = jnp.concatenate([cot_ref[ctx ^ d] for d in range(groups)], axis=0)
        for e in range(expert_count):
            ids_here = iota((capacity, tok), 0) + e * capacity
            pick = ((ids_here == d0) | (ids_here == d1)).astype(F32).astype(BF16)
            slots[0][e] = dot_nn(pick, up).astype(BF16)
        slots[1][0] = slots[0][expert]

    return pl.pallas_call(
        kernel,
        in_specs=[SMEM_SPEC, VMEM_SPEC, VMEM_SPEC],
        out_specs=[VMEM_SPEC] * 4,
        out_shape=[
            shape((8, tok), I32),
            shape((tok, 8), I32),
            shape((expert_count, capacity, width), BF16),
            shape((1, capacity, width), BF16),
        ],
        compiler_params=params(),
        cost_estimate=takes(4),
        name="route",
    )(place, ints, cotangent)


def gather_image(pieces, i, rows):
    at = pl.ds(pl.multiple_of(i * rows, rows), rows)
    return jnp.concatenate([p[at, :] for p in pieces], axis=0).astype(F32)


def gather_mask(pieces, i, rows, body):
    cols = []
    for p in pieces:
        block = p[body : body + PAD, :LANES].astype(F32).T
        cols.append(
            jnp.sum(jnp.where(iota(block.shape, 1) == i, block, 0.0), axis=1, keepdims=True)[:rows]
        )
    return jnp.concatenate(cols, axis=0)


def head_pair(block, h, size):
    zero = jnp.zeros_like(block)
    return jnp.concatenate([block, zero] if h % 2 == 0 else [zero, block], axis=0)


def attend_call(pieces, gain, shift, qkv, qkv_t, query_bias, value_bias, images, rows, after):
    count = len(pieces)
    width = qkv.shape[0]
    seq = count * rows
    size = width // HEADS
    body = images * rows
    scale = size ** (-0.5)

    def kernel(*refs):
        ps = refs[:count]
        gain_ref, shift_ref, qkv_ref, qkvt_ref, qb_ref, vb_ref = refs[count : count + 6]
        outs = refs[count + 7 : 2 * count + 7]
        qt_ref, k_ref, vt_ref, lse_ref, ot = refs[2 * count + 7 :]
        i = pl.program_id(0)
        x = gather_image(ps, i, rows)
        live = gather_mask(ps, i, rows, body) > 0
        xhat, _ = norm_stats(x)
        n = (xhat * gain_ref[...] + shift_ref[...]).astype(BF16)
        qt_ref[0] = (dot_nt(qkvt_ref[:width], n) + qb_ref[...]).astype(BF16)
        k_ref[0] = dot_nn(n, qkv_ref[:, width : 2 * width]).astype(BF16)
        vt_ref[0] = (dot_nt(qkvt_ref[2 * width :], n) + vb_ref[...]).astype(BF16)
        for h in range(HEADS):
            at = slice(h * size, (h + 1) * size)
            pair = slice(h // 2 * 2 * size, (h // 2 + 1) * 2 * size)
            s = dot_nn(k_ref[0, :, pair], head_pair(qt_ref[0, at, :], h, size)) * scale
            s = jnp.where(live, s, NEG)
            top = jnp.max(s, axis=0, keepdims=True)
            e = jnp.exp(s - top)
            total = jnp.sum(e, axis=0, keepdims=True)
            lse_ref[0, h : h + 1, :] = top + jnp.log(total)
            ot[at, :] = dot_nn(vt_ref[0, at, :], (e * (1.0 / total)).astype(BF16))
        o = ot[...].T.astype(BF16)
        at = pl.ds(pl.multiple_of(i * rows, rows), rows)
        for d in range(count):
            outs[d][at, :] = o[d * rows : (d + 1) * rows]

    full = lambda a: pl.BlockSpec(a.shape, lambda i: (0,) * a.ndim)
    ins = list(pieces) + [gain, shift, qkv, qkv_t, query_bias, value_bias]
    per_image = lambda dims: pl.BlockSpec((1,) + dims, lambda i: (i, 0, 0))
    return pl.pallas_call(
        kernel,
        grid=(images,),
        in_specs=[full(a) for a in ins] + [ANY_SPEC],
        out_specs=[pl.BlockSpec((body, width), lambda i: (0, 0))] * count
        + [per_image((width, seq)), per_image((seq, width)), per_image((width, seq)), per_image((HEADS, seq))],
        out_shape=[shape((body, width), BF16)] * count
        + [
            shape((images, width, seq), BF16),
            shape((images, seq, width), BF16),
            shape((images, width, seq), BF16),
            shape((images, HEADS, seq), F32),
        ],
        scratch_shapes=[pltpu.VMEM((width, seq), F32)],
        compiler_params=params(),
        cost_estimate=takes(13),
        name="attend",
    )(*ins, after)


def middle_call(place, attended, pieces, proj, proj_bias, gain, shift, dest_rows, expert_count, capacity):
    count = len(attended)
    body, width = attended[0].shape
    tok = count * body

    def kernel(place_ref, *refs):
        att, ps = refs[:count], refs[count : 2 * count]
        proj_ref, pb_ref, gain_ref, shift_ref, dest_ref = refs[2 * count : 2 * count + 5]
        mid_ref, n_ref = refs[2 * count + 5 : 2 * count + 7]
        slots = refs[2 * count + 7 :]
        expert = place_ref[1]
        for d in range(count):
            at = slice(d * body, (d + 1) * body)
            mid = (
                ps[d][:body, :].astype(F32) + dot_nn(att[d][...], proj_ref[...]) + pb_ref[...]
            )
            mid_ref[at, :] = mid
            xhat, _ = norm_stats(mid)
            n_ref[at, :] = (xhat * gain_ref[...] + shift_ref[...]).astype(BF16)
        n = n_ref[...]
        d0, d1 = dest_ref[0:1, :], dest_ref[1:2, :]
        for d in range(expert_count):
            ids_here = iota((capacity, tok), 0) + (expert ^ d) * capacity
            pick = ((ids_here == d0) | (ids_here == d1)).astype(F32).astype(BF16)
            slots[d][...] = dot_nn(pick, n).astype(BF16)

    ins = list(attended) + list(pieces) + [proj, proj_bias, gain, shift, dest_rows]
    return pl.pallas_call(
        kernel,
        in_specs=[SMEM_SPEC] + [VMEM_SPEC] * len(ins),
        out_specs=[VMEM_SPEC] * (2 + expert_count),
        out_shape=[shape((tok, width), F32), shape((tok, width), BF16)]
        + [shape((capacity, width), BF16)] * expert_count,
        compiler_params=params(),
        cost_estimate=takes(5),
        name="middle",
    )(place, *ins)


def expert_call(
    place, xs, upstream, first, router, up, up_bias, down, down_bias, results, partial, last, expert_count, n_ctx, n_dp,
    after,
):
    blocks = len(xs)
    capacity, width = xs[0].shape
    hidden_width = up.shape[1]
    total = blocks * capacity
    chunk = width
    steps = hidden_width // chunk
    pieces = n_ctx * n_dp
    per_step = pieces // steps
    part = chunk // per_step
    piece_rows = 2 * part + PAD
    sub = min(total, 384)
    has_partial = partial is not None
    ins = list(xs) + [upstream, router, up, up_bias, down, down_bias]
    ins += [partial] * has_partial + ([] if results is None else [results])
    n_in = len(ins) + len(after)

    def kernel(place_ref, *refs):
        x_refs, u_ref = refs[:blocks], refs[blocks]
        rw, up_ref, ub_ref, dn_ref, db_ref = refs[blocks + 1 : blocks + 6]
        before = refs[blocks + 6]
        o = refs[n_in:]
        out_ref, gx_refs = o[0], o[1 : 1 + blocks]
        grad_refs = o[1 + blocks : 2 + blocks + last]
        x_all, g_all, x_t, g_t, gate, out_acc, gx_acc, act, gh_all, down_bias_sum = o[
            2 + blocks + last :
        ]
        j = pl.program_id(0)
        slots = [lax.rem(place_ref[1] ^ (first + b), blocks) for b in range(blocks)]

        @pl.when(j == 0)
        def _():
            expert = place_ref[1]
            bias = jnp.zeros((1, width), F32)
            for b in range(blocks):
                at = slice(b * capacity, (b + 1) * capacity)
                x = x_refs[b][...]
                gates = soft_gates(dot_nn(x, rw[...]), expert_count)
                mine = jnp.sum(
                    jnp.where(iota(gates.shape, 1) == expert, gates, 0.0), axis=1, keepdims=True
                )
                g = (u_ref[slots[b]].astype(F32) * mine).astype(BF16)
                x_all[at, :] = x
                g_all[at, :] = g
                gate[at, :] = jnp.broadcast_to(mine, (capacity, LANES))
                bias = bias + jnp.sum(g.astype(F32), axis=0, keepdims=True)
            x_t[...] = x_all[...].T
            g_t[...] = g_all[...].T
            out_acc[...] = jnp.zeros_like(out_acc)
            gx_acc[...] = jnp.zeros_like(gx_acc)
            down_bias_sum[...] = bias

        w_up, w_dn = up_ref[...], dn_ref[...]
        bias = jnp.zeros((1, chunk), F32)
        for r in range(total // sub):
            at = slice(r * sub, (r + 1) * sub)
            h = dot_nn(x_all[at, :], w_up) + ub_ref[...]
            a, slope = gelu_parts(h)
            a = a.astype(BF16)
            act[at, :] = a
            out_acc[at, :] += dot_nn(a, w_dn)
            gh = (dot_nt(g_all[at, :], w_dn) * slope).astype(BF16)
            gh_all[at, :] = gh
            bias = bias + jnp.sum(gh.astype(F32), axis=0, keepdims=True)
            gx_acc[at, :] += dot_nt(gh, w_up)
        g_up = dot_nn(x_t[...], gh_all[...])
        g_dn = dot_nn(g_t[...], act[...]).T
        row = iota((PAD, width), 0)
        extra = jnp.where(row == 0, bias, 0.0)
        extra = jnp.where((row == 1) & (j == 0), down_bias_sum[...], extra)
        for k in range(per_step):
            vals = (
                g_up[k * part : (k + 1) * part],
                g_dn[k * part : (k + 1) * part],
                extra if k == 0 else jnp.zeros_like(extra),
            )
            if has_partial:
                vals = tuple(
                    v + before[k, at, :].astype(F32)
                    for v, at in zip(vals, (slice(0, part), slice(part, 2 * part), slice(2 * part, None)))
                )
            vals = tuple(v.astype(BF16) for v in vals)

            def put(ref, slot):
                ref[slot, :part, :] = vals[0]
                ref[slot, part : 2 * part, :] = vals[1]
                ref[slot, 2 * part :, :] = vals[2]

            if not last:
                put(grad_refs[0], k)
            else:
                piece = j * per_step + k
                slot = lax.rem(piece, n_ctx) ^ place_ref[0]
                stay = piece // n_ctx == place_ref[2]

                @pl.when(stay)
                def _():
                    put(grad_refs[0], slot)

                @pl.when(jnp.logical_not(stay))
                def _():
                    put(grad_refs[1], slot)

        @pl.when(j == steps - 1)
        def _():
            for b in range(blocks):
                at = slice(b * capacity, (b + 1) * capacity)
                out = (out_acc[at, :] + db_ref[...]).astype(BF16).astype(F32)
                out_ref[slots[b]] = (out * gate[at, :1]).astype(BF16)
                gg = jnp.sum(out * u_ref[slots[b]].astype(F32), axis=1, keepdims=True)
                line = jnp.broadcast_to(gg, (capacity, LANES)).T[:PAD]
                high = line.astype(BF16).astype(F32)
                mean = (line - high).astype(BF16).astype(F32)
                k = iota(line.shape, 0)
                parts = jnp.where(
                    k == 0, high, jnp.where(k == 1, mean, jnp.where(k == 2, line - high - mean, 0.0))
                )
                gx_refs[b][:capacity, :] = gx_acc[at, :].astype(BF16)
                gx_refs[b][capacity:, :] = jnp.concatenate(
                    [parts, jnp.zeros((PAD, width - capacity), F32)], axis=1
                ).astype(BF16)

    full = lambda a: pl.BlockSpec(a.shape, lambda j, p: (0,) * a.ndim)
    const = lambda dims: pl.BlockSpec(dims, lambda j, p: (0,) * len(dims))
    blocks_of = pl.BlockSpec((blocks, capacity, width), lambda j, p: ((p[1] ^ first) // blocks, 0, 0))
    step_pieces = pl.BlockSpec((per_step, piece_rows, width), lambda j, p: (j, 0, 0))
    specs = (
        [full(a) for a in xs]
        + [full(upstream) if upstream.shape[0] == blocks else blocks_of]
        + [
            full(router),
            pl.BlockSpec((width, chunk), lambda j, p: (0, j)),
            pl.BlockSpec((1, chunk), lambda j, p: (0, j)),
            pl.BlockSpec((chunk, width), lambda j, p: (j, 0)),
            full(down_bias),
        ]
        + [step_pieces] * has_partial
        + [ANY_SPEC] * (results is not None)
    )
    if last:
        grad_specs = [const((n_ctx, piece_rows, width))] * n_dp
        grad_shapes = [shape((n_ctx, piece_rows, width), BF16)] * n_dp
    else:
        grad_specs = [step_pieces]
        grad_shapes = [shape((pieces, piece_rows, width), BF16)]
    return pl.pallas_call(
        kernel,
        grid_spec=pltpu.PrefetchScalarGridSpec(
            num_scalar_prefetch=1,
            grid=(steps,),
            in_specs=specs + [ANY_SPEC] * len(after),
            out_specs=[blocks_of] + [const((capacity + PAD, width))] * blocks + grad_specs,
            scratch_shapes=[
                pltpu.VMEM((total, width), BF16),
                pltpu.VMEM((total, width), BF16),
                pltpu.VMEM((width, total), BF16),
                pltpu.VMEM((width, total), BF16),
                pltpu.VMEM((total, LANES), F32),
                pltpu.VMEM((total, width), F32),
                pltpu.VMEM((total, width), F32),
                pltpu.VMEM((total, chunk), BF16),
                pltpu.VMEM((total, chunk), BF16),
                pltpu.VMEM((1, width), F32),
            ],
        ),
        out_shape=[shape((expert_count, capacity, width), BF16)]
        + [shape((capacity + PAD, width), BF16)] * blocks
        + grad_shapes,
        input_output_aliases={} if results is None else {len(ins): 0},
        compiler_params=params(),
        cost_estimate=takes(13),
        name="expert",
    )(place, *ins, *after)


def slot_match(dest_ref, at, first, capacity):
    d = dest_ref[at, :]
    lanes = iota((d.shape[0], capacity), 1) + first
    return ((lanes == d[:, 0:1]) | (lanes == d[:, 1:2])).astype(F32).astype(BF16)


def output_call(place, results, mid, dest_cols, groups):
    blocks, capacity, width = results.shape
    tok = mid.shape[0]
    body = tok // groups

    def kernel(place_ref, o_ref, mid_ref, dest_ref, out_ref):
        for g in range(groups):
            at = slice(g * body, (g + 1) * body)
            acc = mid_ref[at, :]
            for e in range(blocks):
                acc = acc + dot_nn(slot_match(dest_ref, at, e * capacity, capacity), o_ref[e])
            out_ref[place_ref[0] ^ g] = acc.astype(BF16)

    return pl.pallas_call(
        kernel,
        in_specs=[SMEM_SPEC] + [VMEM_SPEC] * 3,
        out_specs=VMEM_SPEC,
        out_shape=shape((groups, body, width), BF16),
        compiler_params=params(),
        cost_estimate=takes(5),
        name="output",
    )(place, results, mid, dest_cols)


def middle_back_call(
    place, gxs, mid, normed, cotangent, dest_cols, attended, router, gain, proj, expert_count, after
):
    blocks = len(gxs)
    groups, body, width = cotangent.shape
    capacity = gxs[0].shape[0] - PAD
    tok = groups * body
    misc = -(-(expert_count + 3) // PAD) * PAD

    def kernel(place_ref, *refs):
        gx_refs = refs[:blocks]
        mid_ref, n_ref, cot_ref, dest_ref = refs[blocks : blocks + 4]
        att = refs[blocks + 4 : blocks + 4 + groups]
        router_ref, gain_ref, proj_ref = refs[blocks + 4 + groups : blocks + 7 + groups]
        refs = refs[blocks + 7 + groups + len(after) :]
        gmid_ref, ga_refs = refs[0], refs[1 : 1 + groups]
        shared_ref, branch_t, logit_t, att_all = refs[1 + groups :]
        ctx, expert = place_ref[0], place_ref[1]
        g_gain = jnp.zeros((1, width), F32)
        g_shift = jnp.zeros((1, width), F32)
        g_proj_bias = jnp.zeros((1, width), F32)
        for g in range(groups):
            at = slice(g * body, (g + 1) * body)
            gn = jnp.zeros((body, width), F32)
            gg = jnp.zeros((body, LANES), F32)
            lane = iota((body, LANES), 1)
            for d in range(blocks):
                match = slot_match(dest_ref, at, (expert ^ d) * capacity, capacity)
                gn = gn + dot_nn(match, gx_refs[d][:capacity, :])
                parts = dot_nt(match, gx_refs[d][capacity:, :capacity])
                gg = jnp.where(
                    lane == (expert ^ d), parts[:, 0:1] + parts[:, 1:2] + parts[:, 2:3], gg
                )
            gates = soft_gates(dot_nn(n_ref[at, :], router_ref[...]), expert_count)
            logit = gates * (gg - jnp.sum(gates * gg, axis=1, keepdims=True))
            logit_t[:, at] = logit.T.astype(BF16)
            gn = gn + dot_nt(logit.astype(BF16), router_ref[...])
            xhat, inv = norm_stats(mid_ref[at, :])
            g_gain = g_gain + jnp.sum(gn * xhat, axis=0, keepdims=True)
            g_shift = g_shift + jnp.sum(gn, axis=0, keepdims=True)
            gmid = cot_ref[ctx ^ g].astype(F32) + norm_back(gn * gain_ref[...], xhat, inv)
            gmid_ref[at, :] = gmid
            branch = gmid.astype(BF16)
            g_proj_bias = g_proj_bias + jnp.sum(branch.astype(F32), axis=0, keepdims=True)
            branch_t[:, at] = branch.T
            att_all[at, :] = att[g][...]
            ga_refs[g][...] = dot_nt(branch, proj_ref[...]).astype(BF16)
        shared_ref[:width, :] = dot_nn(branch_t[...], att_all[...]).astype(BF16)
        rows = dot_nn(logit_t[...], n_ref[...])[:misc]
        k = iota((misc, width), 0)
        for s, vec in enumerate((g_gain, g_shift, g_proj_bias)):
            rows = jnp.where(k == expert_count + s, vec, rows)
        shared_ref[width:, :] = rows.astype(BF16)

    ins = (
        list(gxs) + [mid, normed, cotangent, dest_cols] + list(attended) + [router, gain, proj]
    )
    return pl.pallas_call(
        kernel,
        in_specs=[SMEM_SPEC] + [VMEM_SPEC] * len(ins) + [ANY_SPEC] * len(after),
        out_specs=[VMEM_SPEC] * (2 + groups),
        out_shape=[shape((tok, width), F32)]
        + [shape((body, width), BF16)] * groups
        + [shape((width + misc, width), BF16)],
        scratch_shapes=[
            pltpu.VMEM((width, tok), BF16),
            pltpu.VMEM((LANES, tok), BF16),
            pltpu.VMEM((tok, width), BF16),
        ],
        compiler_params=params(),
        cost_estimate=takes(11),
        name="middle_back",
    )(place, *ins, *after)


def attend_back_call(
    place, pieces, grads, saved, shared, gain, shift, qkv, qkv_t, value_bias, images, rows, n_dp, after
):
    count = len(pieces)
    width = qkv.shape[0]
    seq = count * rows
    size = width // HEADS
    body = images * rows
    scale = size ** (-0.5)
    part = (4 * width) // (n_dp * count)
    extra_rows = shared.shape[0] - width

    def kernel(place_ref, *refs):
        ps, gs = refs[:count], refs[count : 2 * count]
        qt_ref, k_ref, lse_ref, shared_ref, gain_ref, shift_ref, qkv_ref, qkvt_ref, vb_ref = refs[
            2 * count : 2 * count + 9
        ]
        refs = refs[2 * count + 9 + len(after) :]
        outs, sums = refs[:count], refs[count : count + n_dp]
        gt, w_acc, gain_acc, shift_acc, qb_acc, vb_acc = refs[count + n_dp :]
        i = pl.program_id(0)
        x = gather_image(ps, i, rows)
        live = gather_mask(ps, i, rows, body) > 0
        xhat, inv = norm_stats(x)
        n = (xhat * gain_ref[...] + shift_ref[...]).astype(BF16)
        kt = dot_nt(qkvt_ref[width : 2 * width], n).astype(BF16)
        v = (dot_nn(n, qkv_ref[:, 2 * width :]) + vb_ref[...]).astype(BF16)
        dot_ = gather_image(gs, i, rows).T.astype(BF16)
        k = k_ref[0]
        qt = qt_ref[0]
        for h in range(HEADS):
            at = slice(h * size, (h + 1) * size)
            pair = slice(h // 2 * 2 * size, (h // 2 + 1) * 2 * size)
            qh, kh, gh = qt[at], kt[at], dot_[at]
            s = dot_nn(k[:, pair], head_pair(qh, h, size)) * scale
            p = jnp.exp(jnp.where(live, s, NEG) - lse_ref[0, h : h + 1, :])
            dp = dot_nn(v[:, pair], head_pair(gh, h, size))
            ds = (p * (dp - jnp.sum(p * dp, axis=0, keepdims=True))).astype(BF16)
            gt[at, :] = (dot_nn(kh, ds) * scale).astype(BF16)
            gt[width + h * size : width + (h + 1) * size, :] = (dot_nt(qh, ds) * scale).astype(BF16)
            gt[2 * width + h * size : 2 * width + (h + 1) * size, :] = dot_nt(
                gh, p.astype(BF16)
            ).astype(BF16)
        gall = gt[...]
        gw = dot_nn(gall, n)
        gn = dot_nn(qkv_ref[...], gall).T
        qb = gall[:width].astype(F32)
        vb = gall[2 * width :].astype(F32)
        g_gain = jnp.sum(gn * xhat, axis=0, keepdims=True)
        g_shift = jnp.sum(gn, axis=0, keepdims=True)

        @pl.when(i == 0)
        def _():
            w_acc[...] = jnp.zeros_like(w_acc)
            gain_acc[...] = jnp.zeros_like(gain_acc)
            shift_acc[...] = jnp.zeros_like(shift_acc)
            qb_acc[...] = jnp.zeros_like(qb_acc)
            vb_acc[...] = jnp.zeros_like(vb_acc)

        w_acc[...] += gw
        gain_acc[...] += g_gain
        shift_acc[...] += g_shift
        qb_acc[...] += qb
        vb_acc[...] += vb
        gin = norm_back(gn * gain_ref[...], xhat, inv).astype(BF16)
        at = pl.ds(pl.multiple_of(i * rows, rows), rows)
        for d in range(count):
            outs[d][at, :] = gin[d * rows : (d + 1) * rows]

        @pl.when(i == images - 1)
        def _():
            rows_of = [
                jnp.broadcast_to(jnp.sum(a[...], axis=1, keepdims=True), (width, LANES)).T[:1]
                for a in (qb_acc, vb_acc)
            ]
            k16 = iota((PAD, width), 0)
            vecs = jnp.zeros((PAD, width), F32)
            for s, vec in enumerate((gain_acc[...], shift_acc[...], *rows_of)):
                vecs = jnp.where(k16 == s, vec, vecs)
            for p in range(n_dp * count):
                first = p * part
                if first < 3 * width:
                    block = w_acc[first : first + part, :].astype(BF16)
                else:
                    block = shared_ref[first - 3 * width : first - 3 * width + part, :]
                if p == 0:
                    extra = vecs.astype(BF16)
                elif p * PAD <= extra_rows:
                    extra = shared_ref[width + (p - 1) * PAD : width + p * PAD, :]
                else:
                    extra = jnp.zeros((PAD, width), BF16)
                slot = p % count ^ place_ref[0]

                def put(ref):
                    ref[slot, :part, :] = block
                    ref[slot, part:, :] = extra

                @pl.when(place_ref[2] == p // count)
                def _():
                    put(sums[0])

                @pl.when(place_ref[2] != p // count)
                def _():
                    put(sums[1])

    full = lambda a: pl.BlockSpec(a.shape, lambda i: (0,) * a.ndim)
    const = lambda dims: pl.BlockSpec(dims, lambda i: (0,) * len(dims))
    per_image = lambda a: pl.BlockSpec((1,) + a.shape[1:], lambda i: (i, 0, 0))
    rest = [shared, gain, shift, qkv, qkv_t, value_bias]
    return pl.pallas_call(
        kernel,
        grid=(images,),
        in_specs=[SMEM_SPEC] + [full(a) for a in pieces]
        + [full(a) for a in grads]
        + [per_image(a) for a in saved]
        + [full(a) for a in rest]
        + [ANY_SPEC] * len(after),
        out_specs=[const((body, width))] * count + [const((count, part + PAD, width))] * n_dp,
        out_shape=[shape((body, width), BF16)] * count
        + [shape((count, part + PAD, width), BF16)] * n_dp,
        scratch_shapes=[
            pltpu.VMEM((3 * width, seq), BF16),
            pltpu.VMEM((3 * width, width), F32),
            pltpu.VMEM((1, width), F32),
            pltpu.VMEM((1, width), F32),
            pltpu.VMEM((width, seq), F32),
            pltpu.VMEM((width, seq), F32),
        ],
        compiler_params=params(),
        cost_estimate=takes(20),
        name="attend_back",
    )(place, *pieces, *grads, *saved, *rest, *after)


def input_call(place, gmid, gins):
    groups = len(gins)
    body, width = gins[0].shape

    def kernel(place_ref, gmid_ref, *refs):
        ctx = place_ref[0]
        for g in range(groups):
            refs[groups][ctx ^ g] = (
                gmid_ref[g * body : (g + 1) * body, :] + refs[g][...].astype(F32)
            ).astype(BF16)

    return pl.pallas_call(
        kernel,
        in_specs=[SMEM_SPEC] + [VMEM_SPEC] * (1 + groups),
        out_specs=VMEM_SPEC,
        out_shape=shape((groups, body, width), BF16),
        compiler_params=params(),
        cost_estimate=takes(3),
        name="input",
    )(place, gmid, *gins)


def expert_grads_call(place, pieces, width, hidden_width, n_ctx, n_dp):
    count = len(pieces)
    chunk = width
    per_step = count * chunk // hidden_width
    part = chunk // per_step

    def kernel(place_ref, *refs):
        ins, (up_ref, down_ref, extra_ref) = refs[:count], refs[count:]
        q = pl.program_id(0)
        for i in range(count):

            @pl.when(q == i)
            def _():
                up_ref[...] = ins[i][:part, :].astype(F32)
                down_ref[...] = ins[i][part : 2 * part, :].astype(F32)
                extra_ref[0] = ins[i][2 * part :, :].astype(F32)

    def piece(q, p):
        return (p[2] ^ (q // n_ctx)) * n_ctx + (p[0] ^ lax.rem(q, n_ctx))

    return pl.pallas_call(
        kernel,
        grid_spec=pltpu.PrefetchScalarGridSpec(
            num_scalar_prefetch=1,
            grid=(count,),
            in_specs=[pl.BlockSpec(a.shape, lambda q, p: (0, 0)) for a in pieces],
            out_specs=[
                pl.BlockSpec(
                    (part, chunk), lambda q, p: (lax.rem(piece(q, p), per_step), piece(q, p) // per_step)
                ),
                pl.BlockSpec((part, width), lambda q, p: (piece(q, p), 0)),
                pl.BlockSpec((1, PAD, width), lambda q, p: (piece(q, p), 0, 0)),
            ],
        ),
        out_shape=[
            shape((width, hidden_width), F32),
            shape((hidden_width, width), F32),
            shape((count, PAD, width), F32),
        ],
        compiler_params=params(),
        cost_estimate=takes(7),
        name="expert_grads",
    )(place, *pieces)


def shared_grads_call(place, pieces, n_ctx, width):
    count = len(pieces)
    rows, share = pieces[0].shape
    part = rows - PAD

    def kernel(place_ref, *refs):
        ins, (qkv_ref, proj_ref, extra_ref, hold) = refs[:count], refs[count:]
        for q in range(count):
            piece = (place_ref[2] ^ (q // n_ctx)) * n_ctx + (place_ref[0] ^ (q % n_ctx))
            hold[piece] = ins[q][...].astype(F32)
        for p in range(count):
            block = hold[p, :part, :].T
            if p * part < 3 * width:
                qkv_ref[:, p * part : (p + 1) * part] = block
            else:
                proj_ref[:, p * part - 3 * width : (p + 1) * part - 3 * width] = block
            extra_ref[p * PAD : (p + 1) * PAD, :] = hold[p, part:, :]

    return pl.pallas_call(
        kernel,
        in_specs=[SMEM_SPEC] + [VMEM_SPEC] * count,
        out_specs=[VMEM_SPEC] * 3,
        out_shape=[shape((share, 3 * width), F32), shape((share, width), F32), shape((count * PAD, share), F32)],
        scratch_shapes=[pltpu.VMEM((count, rows, share), F32)],
        compiler_params=params(),
        cost_estimate=takes(3),
        name="shared_grads",
    )(place, *pieces)


def swap(x, axis, d, size, what="sums"):
    with jax.named_scope(f"{what}_{axis}_{d}"):
        return lax.ppermute(x, axis, [(i, i ^ d) for i in range(size)])


def exchange(x, axis, what):
    with jax.named_scope(what):
        return lax.all_to_all(x, axis, split_axis=0, concat_axis=0, tiled=True)


def named_permute(x, axes, pairs):
    with jax.named_scope("shared_sums"):
        return lax.ppermute(x, axes, pairs)


def pick(x, i):
    return lax.dynamic_index_in_dim(x, i, 0, keepdims=False)


def add_all(parts):
    acc = parts[0].astype(F32)
    for p in parts[1:]:
        acc = acc + p.astype(F32)
    return acc.astype(BF16)


def reduce_core(stay, go, n_dp, what):
    came = swap(go, "dp", 1, n_dp, what)
    return [add_all([stay[g], came[g]]) for g in range(stay.shape[0])]


def reduce_ctx(parts, n_ctx, what):
    return [parts[0]] + [swap(parts[d], "ctx", d, n_ctx, what) for d in range(1, n_ctx)]


def local(
    mesh_sizes,
    tokens,
    cotangent,
    key_mask,
    route_ids,
    priority,
    norm1_gain,
    norm1_bias,
    qkv_weight,
    query_bias,
    value_bias,
    proj_weight,
    proj_bias,
    norm2_gain,
    norm2_bias,
    router_weight,
    expert_up,
    expert_up_bias,
    expert_down,
    expert_down_bias,
):
    n_expert, n_ctx, n_dp = mesh_sizes
    images_all, rows, width = tokens.shape
    tok = images_all * rows
    images = images_all // n_ctx
    body = images * rows
    expert_count = router_weight.shape[1]
    capacity = max(2, 2 * tok // expert_count)
    ctx, expert, core = (lax.axis_index(a) for a in ("ctx", "expert", "dp"))
    place = jnp.stack([ctx, expert, core]).astype(I32)

    tok4 = tokens.reshape(n_ctx, body, width)
    mask4 = jnp.pad(
        key_mask.reshape(n_ctx, images, rows).astype(BF16),
        ((0, 0), (0, PAD - images), (0, width - rows)),
    )
    both = jnp.concatenate([tok4, mask4], axis=1)
    mine = [pick(both, ctx ^ d) for d in range(n_ctx)]
    pieces = [mine[0]] + [swap(mine[d], "ctx", d, n_ctx, "tokens") for d in range(1, n_ctx)]

    order = jnp.arange(tok, dtype=I32).reshape(n_ctx, body)
    ints4 = jnp.stack(
        [
            route_ids[..., 0].reshape(n_ctx, body),
            route_ids[..., 1].reshape(n_ctx, body),
            priority.reshape(n_ctx, body) * tok + order,
        ],
        axis=1,
    )
    ints = jnp.concatenate([pick(ints4, ctx ^ d) for d in range(n_ctx)], axis=1)
    ints = jnp.pad(ints, ((0, 5), (0, 0)))
    cot4 = cotangent.reshape(n_ctx, body, width)
    dest_rows, dest_cols, u_send, u_own = route_call(place, ints, cot4, expert_count, capacity)
    u_came = exchange(u_send, "expert", "upstream")

    row = lambda v: v.reshape(1, -1)
    col = lambda v: v.reshape(-1, 1)
    qkv_t = qkv_weight.T
    att = attend_call(
        pieces, row(norm1_gain), row(norm1_bias), qkv_weight, qkv_t, col(query_bias), col(value_bias),
        images, rows, dest_rows,
    )
    att_out, (q_t, k, v_t, lse) = att[:n_ctx], att[n_ctx:]
    attended = [att_out[0]] + [swap(att_out[d], "ctx", d, n_ctx, "attended") for d in range(1, n_ctx)]

    mid, normed2, *x_send = middle_call(
        place, attended, mine, proj_weight, row(proj_bias), row(norm2_gain), row(norm2_bias), dest_rows,
        expert_count, capacity,
    )
    xs = [x_send[0]] + [swap(x_send[d], "expert", d, n_expert, "rows") for d in range(1, n_expert)]

    router = jnp.pad(router_weight, ((0, 0), (0, LANES - expert_count)))
    results, gxs, grads = None, [], None
    group = max(1, n_expert // EXPERT_CALLS)
    for first in range(0, n_expert, group):
        last = first + group == n_expert
        results, *res = expert_call(
            place, xs[first : first + group], u_own if first + group == 1 else u_came, first, router, expert_up[0],
            expert_up_bias, expert_down[0], expert_down_bias, results, grads, last, expert_count, n_ctx, n_dp,
            gxs[1:2] if last else [],
        )
        gxs += [
            g if first + b == 0 else swap(g, "expert", first + b, n_expert, "rows_grad")
            for b, g in enumerate(res[:group])
        ]
        grads = res[group] if not last else res[group:]

    parts = reduce_core(*grads, n_dp, "expert_terms")

    grad_mid, *rest = middle_back_call(
        place, gxs, mid, normed2, cot4, dest_cols, attended, router, row(norm2_gain), proj_weight, expert_count,
        [],
    )
    ga_send, shared = rest[:n_ctx], rest[n_ctx]
    gas = [ga_send[0]] + [swap(ga_send[d], "ctx", d, n_ctx, "attended_grad") for d in range(1, n_ctx)]

    block_out = output_call(place, exchange(results, "expert", "results"), mid, dest_cols, n_ctx)

    mine_sum = add_all(reduce_ctx(parts, n_ctx, "expert_terms"))
    own = reduce_ctx([mine_sum] * n_ctx, n_ctx, "expert_sums")
    *gin_send, stay, go = attend_back_call(
        place, pieces, gas, (q_t, k, lse), shared, row(norm1_gain), row(norm1_bias), qkv_weight, qkv_t,
        row(value_bias), images, rows, n_dp, own[1:],
    )

    share = width // n_expert
    part = add_all(reduce_ctx(reduce_core(stay, go, n_dp, "shared"), n_ctx, "shared"))
    cut = [lax.dynamic_slice_in_dim(part, (expert ^ d) * share, share, 1) for d in range(n_expert)]
    part = add_all([cut[0]] + [swap(cut[d], "expert", d, n_expert, "shared") for d in range(1, n_expert)])
    every = [part] + [
        named_permute(
            part,
            ("ctx", "dp"),
            [(i, i ^ (q % n_ctx * n_dp + q // n_ctx)) for i in range(n_dp * n_ctx)],
        )
        for q in range(1, n_dp * n_ctx)
    ]

    gins = [gin_send[0]] + [swap(gin_send[d], "ctx", d, n_ctx, "input_grad") for d in range(1, n_ctx)]
    input_grad = input_call(place, grad_mid, gins)

    other = [swap(a, "dp", 1, n_dp, "expert_sums") for a in own]
    grad_up, grad_down, extra = expert_grads_call(
        place, own + other, width, expert_up.shape[2], n_ctx, n_dp
    )
    per_step = extra.shape[0] * width // expert_up.shape[2]
    grad_up_bias = extra[::per_step, 0].reshape(1, -1)
    grad_down_bias = extra[0, 1].reshape(1, -1)

    grad_qkv, grad_proj, extra = shared_grads_call(place, every, n_ctx, width)
    g1_gain, g1_bias, g_query_bias, g_value_bias = (extra[s] for s in range(4))
    grad_router = extra[PAD : PAD + expert_count].T
    g2_gain, g2_bias, g_proj_bias = (extra[PAD + expert_count + s] for s in range(3))
    return (
        block_out.reshape(tokens.shape),
        input_grad.reshape(tokens.shape),
        g1_gain,
        g1_bias,
        grad_qkv,
        g_query_bias,
        g_value_bias,
        grad_proj,
        g_proj_bias,
        g2_gain,
        g2_bias,
        grad_router,
        grad_up[None],
        grad_up_bias,
        grad_down[None],
        grad_down_bias,
    )


def solution(mesh):
    images = P(("expert", "dp"), "ctx", None)
    ints = P(("expert", "dp"), "ctx")
    placed = (images, images, ints, images, ints) + (P(),) * 10 + (
        P("expert", None, None),
        P("expert", None),
        P("expert", None, None),
        P("expert", None),
    )
    sizes = tuple(mesh.shape[a] for a in ("expert", "ctx", "dp"))

    def run(*args):
        return local(sizes, *args)

    return jax.shard_map(
        run,
        mesh=mesh,
        in_specs=placed,
        out_specs=(
            images,
            images,
            P("expert"),
            P("expert"),
            P("expert", None),
            P("expert"),
            P("expert"),
            P("expert", None),
            P("expert"),
            P("expert"),
            P("expert"),
            P("expert", None),
            P("expert", None, None),
            P("expert", None),
            P("expert", None, None),
            P("expert", None),
        ),
        check_vma=False,
    )
```

profile of v0, /device:TPU:0, one launch (start us, length us, event | category | flops | bytes accessed | tf_op | source)
XLA Modules:
  0.0 286.5 jit_solution(10171115579855566330)
XLA Ops:
  3.5 2.9 %collective-permute-start = (bf16[208,512]{1,0:T(8,128)(2,1)}, bf16[208,512]{1,0:T(8,128)(2,1)}, u32[]{:S(2)}, u32[]{:S(2)}) collective-permute-start(bf16[208,512]{1,0:T(8,128)(2,1)} %get-tuple-element.122.refs_5_), channel_id=1, source_target_pairs={{0,2},{2,0},{4,6},{6,4},{1,3},{3,1},{5,7},{7,5},{8,10},{10,8},{12,... | collective-permute-start | bytes 638984 | tf_op jit(solution)/shard_map/tokens_ctx_1/ppermute | solution.py:771
  6.5 1.5 collective-permute-start.1
  9.6 4.5 %route.1 = (s32[8,768]{1,0:T(8,128)}, s32[768,8]{1,0:T(8,128)}, bf16[4,384,512]{2,1,0:T(8,128)(2,1)}, bf16[1,384,512]{2,1,0:T(8,128)(2,1)}) custom-call(s32[3]{0:T(128)} %pad_add_fusion.2.place_ref, s32[8,768]{1,0:T(8,128)} %pad.13.ints_ref, bf16[4,192,512]{2,1,0:T(8,128)(2,1)} %bitcast.92), custom_call_target="tpu_custom_call" | custom-call | flops 4600000000 | bytes 131072 | tf_op jit(solution)/shard_map/route/pallas_call | solution.py:121
  14.1 6.0 %all-to-all-start = ((bf16[4,384,512]{2,1,0:T(8,128)(2,1)}), bf16[4,384,512]{2,1,0:T(8,128)(2,1)S(1)}, u32[]{:S(2)}, u32[]{:S(2)}) async-start(bf16[4,384,512]{2,1,0:T(8,128)(2,1)} %get-tuple-element.70), calls=%async_computation | async-start | bytes 3145728 | tf_op jit(solution)/shard_map/upstream/all_to_all | solution.py:776
  20.1 1.6 copy.43
  23.5 12.8 %attend.1 = (bf16[192,512]{1,0:T(8,128)(2,1)}, bf16[192,512]{1,0:T(8,128)(2,1)}, bf16[192,512]{1,0:T(8,128)(2,1)}, bf16[192,512]{1,0:T(8,128)(2,1)}, bf16[3,512,...) custom-call(bf16[208,512]{1,0:T(8,128)(2,1)} %get-tuple-element.123.refs_, ...), custom_call_target="tpu_custom_call" | custom-call | flops 14949999616 | bytes 131072 | tf_op jit(solution)/shard_map/attend/pallas_call | solution.py:196
  36.3 1.6 collective-permute-start.3
  37.8 1.5 collective-permute-start.4
  40.7 3.5 %collective-permute-done.3.refs_1_.refs_9_ = bf16[192,512]{1,0:T(8,128)(2,1)S(1)} collective-permute-done((bf16[192,512]{1,0:T(8,128)(2,1)}, bf16[192,512]{1,0:T(8,128)(2,1)S(1)}, u32[]{:S(2)}, u32[]{:S(2)}) %collective-permute-start.3) | collective-permute-done | bytes 196640 | tf_op jit(solution)/shard_map/attended_ctx_1/ppermute | solution.py:771
  44.2 3.5 %collective-permute-done.4.refs_2_.refs_10_ = bf16[192,512]{1,0:T(8,128)(2,1)S(1)} collective-permute-done((bf16[192,512]{1,0:T(8,128)(2,1)}, bf16[192,512]{1,0:T(8,128)(2,1)S(1)}, u32[]{:S(2)}, u32[]{:S(2)}) %collective-permute-start.4) | collective-permute-done | bytes 196640 | tf_op jit(solution)/shard_map/attended_ctx_2/ppermute | solution.py:771
  48.5 4.7 %middle.1 = (f32[768,512]{1,0:T(8,128)}, bf16[768,512]{1,0:T(8,128)(2,1)}, bf16[384,512]{1,0:T(8,128)(2,1)}, bf16[384,512]{1,0:T(8,128)(2,1)}, bf16[384,512]{1,0:T(8,128)(2,1)}, /*index=5*/bf16[384,512]{1,0:T(8,128)(2,1)}) custom-call(s32[3]{0:T(128)} %pad_add_fusion.2.place_ref, bf16[192,512]{1,0:T(8,128)(2,1)} %get-tuple-element.65.refs_0_.refs_8_, ...), custom_call_target="tpu_custom_call" | custom-call | flops 5750000128 | bytes 131072 | tf_op jit(solution)/shard_map/middle/pallas_call | solution.py:243
  53.2 3.6 %collective-permute-start.6 = (bf16[384,512]{1,0:T(8,128)(2,1)}, bf16[384,512]{1,0:T(8,128)(2,1)S(1)}, u32[]{:S(2)}, u32[]{:S(2)}) collective-permute-start(bf16[384,512]{1,0:T(8,128)(2,1)} %get-tuple-element.69), channel_id=1, source_target_pairs={{0,24},{8,16},{16,8},{24,0},{1,25},{9,17},{17,9},{25,1},{2,26},{10... | collective-permute-start | bytes 1179656 | tf_op jit(solution)/shard_map/rows_expert_3/ppermute | solution.py:771
  57.6 13.2 %expert.4 = (bf16[4,384,512]{2,1,0:T(8,128)(2,1)}, bf16[400,512]{1,0:T(8,128)(2,1)}, bf16[8,528,512]{2,1,0:T(8,128)(2,1)}) custom-call(s32[3]{0:T(128)} %pad_add_fusion.2.place_ref, bf16[384,512]{1,0:T(8,128)(2,1)} %get-tuple-element.73.refs_0_, bf16[1,384,512]{2,1,0:T(8,128)(2,1)} %get-tuple-element.74.refs_1_, bf16[512,128]{1,0:T(8,128)(2,1)} %pad.14.refs_2_.refs_12_, ...), custom_call_target="tpu_custom_call" | custom-call | flops 14949999616 | bytes 131072 | tf_op jit(solution)/shard_map/expert/pallas_call | solution.py:403
  70.8 9.0 %collective-permute-done.8.refs_0_ = bf16[384,512]{1,0:T(8,128)(2,1)S(1)} collective-permute-done((bf16[384,512]{1,0:T(8,128)(2,1)}, bf16[384,512]{1,0:T(8,128)(2,1)S(1)}, u32[]{:S(2)}, u32[]{:S(2)}) %collective-permute-start.8) | collective-permute-done | bytes 393248 | tf_op jit(solution)/shard_map/rows_expert_1/ppermute | solution.py:771
  81.1 14.1 %expert.5 = (bf16[4,384,512]{2,1,0:T(8,128)(2,1)}, bf16[400,512]{1,0:T(8,128)(2,1)}, bf16[8,528,512]{2,1,0:T(8,128)(2,1)}) custom-call(s32[3]{0:T(128)} %pad_add_fusion.2.place_ref, bf16[384,512]{1,0:T(8,128)(2,1)} %copy-done.27, bf16[4,384,512]{2,1,0:T(8,128)(2,1)} %copy-done.2, ...), custom_call_target="tpu_custom_call", output_to_operand_aliasing={{0}: (9, {})} | custom-call | flops 14949999616 | bytes 131072 | tf_op jit(solution)/shard_map/expert/pallas_call | solution.py:403
  95.2 2.4 collective-permute-start.9
  98.4 14.3 %expert.6 = (bf16[4,384,512]{2,1,0:T(8,128)(2,1)}, bf16[400,512]{1,0:T(8,128)(2,1)}, bf16[8,528,512]{2,1,0:T(8,128)(2,1)}) custom-call(s32[3]{0:T(128)} %pad_add_fusion.2.place_ref, bf16[384,512]{1,0:T(8,128)(2,1)} %copy-done.26, bf16[4,384,512]{2,1,0:T(8,128)(2,1)} %copy-done.2, ...), custom_call_target="tpu_custom_call", output_to_operand_aliasing={{0}: (9, {})} | custom-call | flops 14949999616 | bytes 131072 | tf_op jit(solution)/shard_map/expert/pallas_call | solution.py:403
  113.6 16.1 %expert.7 = (bf16[4,384,512]{2,1,0:T(8,128)(2,1)}, bf16[400,512]{1,0:T(8,128)(2,1)}, bf16[4,528,512]{2,1,0:T(8,128)(2,1)}, bf16[4,528,512]{2,1,0:T(8,128)(2,1)}) custom-call(s32[3]{0:T(128)} %pad_add_fusion.2.place_ref, bf16[384,512]{1,0:T(8,128)(2,1)} %copy-done.25, bf16[4,384,512]{2,1,0:T(8,128)(2,1)} %copy-done.2, ...), custom_call_target="tpu_custom_call", output_to_operand_aliasing={{0}: (9, {})} | custom-call | flops 14949999616 | bytes 131072 | tf_op jit(solution)/shard_map/expert/pallas_call | solution.py:403
  129.8 4.5 %collective-permute-done.15 = bf16[4,528,512]{2,1,0:T(8,128)(2,1)S(1)} collective-permute-done((bf16[4,528,512]{2,1,0:T(8,128)(2,1)}, bf16[4,528,512]{2,1,0:T(8,128)(2,1)S(1)}, u32[]{:S(2)}, u32[]{:S(2)}) %collective-permute-start.15) | collective-permute-done | bytes 2162720 | tf_op jit(solution)/shard_map/expert_terms_dp_1/ppermute | solution.py:771
  134.3 1.9 fusion.9
  137.0 1.5 collective-permute-start.17
  139.7 2.3 collective-permute-start.11
  142.1 10.2 %collective-permute-done.18 = bf16[528,512]{1,0:T(8,128)(2,1)S(1)} collective-permute-done((bf16[528,512]{1,0:T(8,128)(2,1)S(1)}, bf16[528,512]{1,0:T(8,128)(2,1)S(1)}, u32[]{:S(2)}, u32[]{:S(2)}) %collective-permute-start.18) | collective-permute-done | bytes 540704 | tf_op jit(solution)/shard_map/expert_terms_ctx_3/ppermute | solution.py:771
  152.3 10.3 %collective-permute-done.17 = bf16[528,512]{1,0:T(8,128)(2,1)S(1)} collective-permute-done((bf16[528,512]{1,0:T(8,128)(2,1)S(1)}, bf16[528,512]{1,0:T(8,128)(2,1)S(1)}, u32[]{:S(2)}, u32[]{:S(2)}) %collective-permute-start.17) | collective-permute-done | bytes 540704 | tf_op jit(solution)/shard_map/expert_terms_ctx_2/ppermute | solution.py:771
  162.6 1.4 fusion.3.refs_0_
  166.0 1.6 collective-permute-start.21
  169.2 11.6 %middle_back.1 = (f32[768,512]{1,0:T(8,128)}, bf16[192,512]{1,0:T(8,128)(2,1)}, bf16[192,512]{1,0:T(8,128)(2,1)}, bf16[192,512]{1,0:T(8,128)(2,1)}, bf16[192,512]{1,0:T(8,128)(2,1)}, /*index=5*/bf16[528,512]{1,0:T(8,128)(2,1)}) custom-call(s32[3]{0:T(128)} %pad_add_fusion.2.place_ref, bf16[400,512]{1,0:T(8,128)(2,1)} %get-tuple-element.85.refs_0_, ...), custom_call_target="tpu_custom_call" | custom-call | flops 12650000384 | bytes 131072 | tf_op jit(solution)/shard_map/middle_back/pallas_call | solution.py:520
  182.2 11.6 %collective-permute-done.12.refs_5_ = bf16[192,512]{1,0:T(8,128)(2,1)S(1)} collective-permute-done((bf16[192,512]{1,0:T(8,128)(2,1)}, bf16[192,512]{1,0:T(8,128)(2,1)S(1)}, u32[]{:S(2)}, u32[]{:S(2)}) %collective-permute-start.12) | collective-permute-done | bytes 196640 | tf_op jit(solution)/shard_map/attended_grad_ctx_1/ppermute | solution.py:771
  193.7 1.6 collective-permute-start.14
  195.3 4.0 %all-to-all-start.1 = ((bf16[4,384,512]{2,1,0:T(8,128)(2,1)}), bf16[4,384,512]{2,1,0:T(8,128)(2,1)S(1)}, u32[]{:S(2)}, u32[]{:S(2)}) async-start(bf16[4,384,512]{2,1,0:T(8,128)(2,1)} %get-tuple-element.82), calls=%async_computation.1 | async-start | bytes 3145728 | tf_op jit(solution)/shard_map/results/all_to_all | solution.py:776
  201.6 20.1 %attend_back.1 = (bf16[192,512]{1,0:T(8,128)(2,1)}, bf16[192,512]{1,0:T(8,128)(2,1)}, bf16[192,512]{1,0:T(8,128)(2,1)}, bf16[192,512]{1,0:T(8,128)(2,1)}, bf16[4...) custom-call(s32[3]{0:T(128)} %pad_add_fusion.2.place_ref, bf16[208,512]{1,0:T(8,128)(2,1)} %get-tuple-element.123.refs_0_.refs_4_, ...), custom_call_target="tpu_custom_call" | custom-call | flops 23000000512 | bytes 131072 | tf_op jit(solution)/shard_map/attend_back/pallas_call | solution.py:647
  221.8 3.0 %collective-permute-done.25 = bf16[4,272,512]{2,1,0:T(8,128)(2,1)S(1)} collective-permute-done((bf16[4,272,512]{2,1,0:T(8,128)(2,1)}, bf16[4,272,512]{2,1,0:T(8,128)(2,1)S(1)}, u32[]{:S(2)}, u32[]{:S(2)}) %collective-permute-start.25) | collective-permute-done | bytes 1114144 | tf_op jit(solution)/shard_map/shared_dp_1/ppermute | solution.py:771
  224.7 2.1 fusion.13
  226.9 1.9 collective-permute-start.28
  228.8 1.5 collective-permute-start.27
  230.4 1.9 collective-permute-start.22
  232.8 4.7 %collective-permute-done.28 = bf16[272,512]{1,0:T(8,128)(2,1)S(1)} collective-permute-done((bf16[272,512]{1,0:T(8,128)(2,1)}, bf16[272,512]{1,0:T(8,128)(2,1)S(1)}, u32[]{:S(2)}, u32[]{:S(2)}) %collective-permute-start.28) | collective-permute-done | bytes 278560 | tf_op jit(solution)/shard_map/shared_ctx_3/ppermute | solution.py:771
  237.5 1.9 collective-permute-start.24
  239.4 3.4 %collective-permute-done.27 = bf16[272,512]{1,0:T(8,128)(2,1)} collective-permute-done((bf16[272,512]{1,0:T(8,128)(2,1)}, bf16[272,512]{1,0:T(8,128)(2,1)}, u32[]{:S(2)}, u32[]{:S(2)}) %collective-permute-start.27) | collective-permute-done | bytes 278560 | tf_op jit(solution)/shard_map/shared_ctx_2/ppermute | solution.py:771
  245.2 2.5 collective-permute-start.31
  247.7 1.8 collective-permute-start.30
  250.6 4.7 %output.1 = bf16[4,192,512]{2,1,0:T(8,128)(2,1)} custom-call(s32[3]{0:T(128)} %pad_add_fusion.2.place_ref, bf16[4,384,512]{2,1,0:T(8,128)(2,1)} %copy-done.1, f32[768,512]{1,0:T(8,128)} %get-tuple-element.83.mid_ref.refs_4_, s32[768,8]{1,0:T(8,128)} %get-tuple-element.84.dest_ref.refs_7_), custom_call_target="tpu_custom_call" | custom-call | flops 5750000128 | bytes 131072 | tf_op jit(solution)/shard_map/output/pallas_call | solution.py:452
  256.6 2.7 input.1
  259.3 1.5 collective-permute-done.29
  264.8 7.6 %expert_grads.1 = (f32[512,2048]{1,0:T(8,128)}, f32[2048,512]{1,0:T(8,128)}, f32[8,16,512]{2,1,0:T(8,128)}) custom-call(s32[3]{0:T(128)} %pad_add_fusion.2.place_ref, bf16[528,512]{1,0:T(8,128)(2,1)} %copy-done.3, bf16[528,512]{1,0:T(8,128)(2,1)} %copy-done.12, bf16[528,512]{1,0:T(8,128)(2,1)} %copy-done.14, ...), custom_call_target="tpu_custom_call" | custom-call | flops 8049999872 | bytes 131072 | tf_op jit(solution)/shard_map/expert_grads/pallas_call | solution.py:714
  275.6 1.5 collective-permute-start.38
  278.4 1.4 slice.110
  281.2 2.4 shared_grads.1
  (165 shorter events, 39.1 us)
Async XLA Ops:
  3.5 19.9 %collective-permute-start = (bf16[208,512]{1,0:T(8,128)(2,1)}, bf16[208,512]{1,0:T(8,128)(2,1)}, u32[]{:S(2)}, u32[]{:S(2)}) collective-permute-start(bf16[208,512]{1,0:T(8,128)(2,1)} %get-tuple-element.122.refs_5_), channel_id=1, source_target_pairs={{0,2},{2,0},{4,6},{6,4},{1,3},{3,1},{5,7},{7,5},{8,10},{10,8},{12,... | collective-permute-start | bytes 638984 | tf_op jit(solution)/shard_map/tokens_ctx_1/ppermute | solution.py:771
  6.5 17.0 %collective-permute-start.1 = (bf16[208,512]{1,0:T(8,128)(2,1)}, bf16[208,512]{1,0:T(8,128)(2,1)}, u32[]{:S(2)}, u32[]{:S(2)}) collective-permute-start(bf16[208,512]{1,0:T(8,128)(2,1)} %get-tuple-element.121.refs_6_), channel_id=1, source_target_pairs={{0,4},{2,6},{4,0},{6,2},{1,5},{3,7},{5,1},{7,3},{8,12},{10,14},{12... | collective-permute-start | bytes 638984 | tf_op jit(solution)/shard_map/tokens_ctx_2/ppermute | solution.py:771
  8.0 15.5 %collective-permute-start.2 = (bf16[208,512]{1,0:T(8,128)(2,1)S(1)}, bf16[208,512]{1,0:T(8,128)(2,1)}, u32[]{:S(2)}, u32[]{:S(2)}) collective-permute-start(bf16[208,512]{1,0:T(8,128)(2,1)S(1)} %get-tuple-element.120.refs_7_), channel_id=1, source_target_pairs={{0,6},{2,4},{4,2},{6,0},{1,7},{3,5},{5,3},{7,1},{8,14},{10,12},{12... | collective-permute-start | bytes 638984 | tf_op jit(solution)/shard_map/tokens_ctx_3/ppermute | solution.py:771
  14.1 65.7 %all-to-all-start = ((bf16[4,384,512]{2,1,0:T(8,128)(2,1)}), bf16[4,384,512]{2,1,0:T(8,128)(2,1)S(1)}, u32[]{:S(2)}, u32[]{:S(2)}) async-start(bf16[4,384,512]{2,1,0:T(8,128)(2,1)} %get-tuple-element.70), calls=%async_computation | async-start | bytes 3145728 | tf_op jit(solution)/shard_map/upstream/all_to_all | solution.py:776
  23.5 16.4 %copy-start.9 = (bf16[512,4]{0,1:T(4,128)(2,1)S(1)}, bf16[512,4]{0,1:T(4,128)(2,1)}, u32[]{:S(2)}) copy-start(bf16[512,4]{0,1:T(4,128)(2,1)} %param.33) | copy-start | bytes 12292
  36.3 7.9 %collective-permute-start.3 = (bf16[192,512]{1,0:T(8,128)(2,1)}, bf16[192,512]{1,0:T(8,128)(2,1)S(1)}, u32[]{:S(2)}, u32[]{:S(2)}) collective-permute-start(bf16[192,512]{1,0:T(8,128)(2,1)} %get-tuple-element.66), channel_id=1, source_target_pairs={{0,2},{2,0},{4,6},{6,4},{1,3},{3,1},{5,7},{7,5},{8,10},{10,8},{12,... | collective-permute-start | bytes 589832 | tf_op jit(solution)/shard_map/attended_ctx_1/ppermute | solution.py:771
  37.8 9.9 %collective-permute-start.4 = (bf16[192,512]{1,0:T(8,128)(2,1)}, bf16[192,512]{1,0:T(8,128)(2,1)S(1)}, u32[]{:S(2)}, u32[]{:S(2)}) collective-permute-start(bf16[192,512]{1,0:T(8,128)(2,1)} %get-tuple-element.67), channel_id=1, source_target_pairs={{0,4},{2,6},{4,0},{6,2},{1,5},{3,7},{5,1},{7,3},{8,12},{10,14},{12... | collective-permute-start | bytes 589832 | tf_op jit(solution)/shard_map/attended_ctx_2/ppermute | solution.py:771
  39.4 8.4 %collective-permute-start.5 = (bf16[192,512]{1,0:T(8,128)(2,1)}, bf16[192,512]{1,0:T(8,128)(2,1)S(1)}, u32[]{:S(2)}, u32[]{:S(2)}) collective-permute-start(bf16[192,512]{1,0:T(8,128)(2,1)} %get-tuple-element.68), channel_id=1, source_target_pairs={{0,6},{2,4},{4,2},{6,0},{1,7},{3,5},{5,3},{7,1},{8,14},{10,12},{12... | collective-permute-start | bytes 589832 | tf_op jit(solution)/shard_map/attended_ctx_3/ppermute | solution.py:771
  53.2 59.5 %collective-permute-start.6 = (bf16[384,512]{1,0:T(8,128)(2,1)}, bf16[384,512]{1,0:T(8,128)(2,1)S(1)}, u32[]{:S(2)}, u32[]{:S(2)}) collective-permute-start(bf16[384,512]{1,0:T(8,128)(2,1)} %get-tuple-element.69), channel_id=1, source_target_pairs={{0,24},{8,16},{16,8},{24,0},{1,25},{9,17},{17,9},{25,1},{2,26},{10... | collective-permute-start | bytes 1179656 | tf_op jit(solution)/shard_map/rows_expert_3/ppermute | solution.py:771
  56.8 40.8 %collective-permute-start.7 = (bf16[384,512]{1,0:T(8,128)(2,1)}, bf16[384,512]{1,0:T(8,128)(2,1)S(1)}, u32[]{:S(2)}, u32[]{:S(2)}) collective-permute-start(bf16[384,512]{1,0:T(8,128)(2,1)} %get-tuple-element.71), channel_id=1, source_target_pairs={{0,16},{8,24},{16,0},{24,8},{1,17},{9,25},{17,1},{25,9},{2,18},{10... | collective-permute-start | bytes 1179656 | tf_op jit(solution)/shard_map/rows_expert_2/ppermute | solution.py:771
  56.8 23.0 %collective-permute-start.8 = (bf16[384,512]{1,0:T(8,128)(2,1)}, bf16[384,512]{1,0:T(8,128)(2,1)S(1)}, u32[]{:S(2)}, u32[]{:S(2)}) collective-permute-start(bf16[384,512]{1,0:T(8,128)(2,1)} %get-tuple-element.72), channel_id=1, source_target_pairs={{0,8},{8,0},{16,24},{24,16},{1,9},{9,1},{17,25},{25,17},{2,10},{10... | collective-permute-start | bytes 1179656 | tf_op jit(solution)/shard_map/rows_expert_1/ppermute | solution.py:771
  95.2 17.5 %collective-permute-start.9 = (bf16[400,512]{1,0:T(8,128)(2,1)}, bf16[400,512]{1,0:T(8,128)(2,1)S(1)}, u32[]{:S(2)}, u32[]{:S(2)}) collective-permute-start(bf16[400,512]{1,0:T(8,128)(2,1)} %get-tuple-element.81), channel_id=1, source_target_pairs={{0,8},{8,0},{16,24},{24,16},{1,9},{9,1},{17,25},{25,17},{2,10},{10... | collective-permute-start | bytes 1228808 | tf_op jit(solution)/shard_map/rows_grad_expert_1/ppermute | solution.py:771
  129.7 4.5 %collective-permute-start.15 = (bf16[4,528,512]{2,1,0:T(8,128)(2,1)}, bf16[4,528,512]{2,1,0:T(8,128)(2,1)S(1)}, u32[]{:S(2)}, u32[]{:S(2)}) collective-permute-start(bf16[4,528,512]{2,1,0:T(8,128)(2,1)} %get-tuple-element.99), channel_id=1, source_target_pairs={{0,1},{1,0},{2,3},{3,2},{4,5},{5,4},{6,7},{7,6},{8,9},{9,8},{10,11... | collective-permute-start | bytes 6488072 | tf_op jit(solution)/shard_map/expert_terms_dp_1/ppermute | solution.py:771
  136.2 16.1 %collective-permute-start.18 = (bf16[528,512]{1,0:T(8,128)(2,1)S(1)}, bf16[528,512]{1,0:T(8,128)(2,1)S(1)}, u32[]{:S(2)}, u32[]{:S(2)}) collective-permute-start(bf16[528,512]{1,0:T(8,128)(2,1)S(1)} %get-tuple-element.115), channel_id=1, source_target_pairs={{0,6},{2,4},{4,2},{6,0},{1,7},{3,5},{5,3},{7,1},{8,14},{10,12},{12... | collective-permute-start | bytes 1622024 | tf_op jit(solution)/shard_map/expert_terms_ctx_3/ppermute | solution.py:771
  137.0 25.6 %collective-permute-start.17 = (bf16[528,512]{1,0:T(8,128)(2,1)S(1)}, bf16[528,512]{1,0:T(8,128)(2,1)S(1)}, u32[]{:S(2)}, u32[]{:S(2)}) collective-permute-start(bf16[528,512]{1,0:T(8,128)(2,1)S(1)} %get-tuple-element.116), channel_id=1, source_target_pairs={{0,4},{2,6},{4,0},{6,2},{1,5},{3,7},{5,1},{7,3},{8,12},{10,14},{12... | collective-permute-start | bytes 1622024 | tf_op jit(solution)/shard_map/expert_terms_ctx_2/ppermute | solution.py:771
  138.5 24.1 %collective-permute-start.16 = (bf16[528,512]{1,0:T(8,128)(2,1)S(1)}, bf16[528,512]{1,0:T(8,128)(2,1)S(1)}, u32[]{:S(2)}, u32[]{:S(2)}) collective-permute-start(bf16[528,512]{1,0:T(8,128)(2,1)S(1)} %get-tuple-element.114), channel_id=1, source_target_pairs={{0,2},{2,0},{4,6},{6,4},{1,3},{3,1},{5,7},{7,5},{8,10},{10,8},{12,... | collective-permute-start | bytes 1622024 | tf_op jit(solution)/shard_map/expert_terms_ctx_1/ppermute | solution.py:771
  139.7 28.6 %collective-permute-start.10 = (bf16[400,512]{1,0:T(8,128)(2,1)S(1)}, bf16[400,512]{1,0:T(8,128)(2,1)S(1)}, u32[]{:S(2)}, u32[]{:S(2)}) collective-permute-start(bf16[400,512]{1,0:T(8,128)(2,1)S(1)} %copy-done.21), channel_id=1, source_target_pairs={{0,16},{8,24},{16,0},{24,8},{1,17},{9,25},{17,1},{25,9},{2,18},{10... | collective-permute-start | bytes 1228808 | tf_op jit(solution)/shard_map/rows_grad_expert_2/ppermute | solution.py:771
  139.7 28.6 %collective-permute-start.11 = (bf16[400,512]{1,0:T(8,128)(2,1)S(1)}, bf16[400,512]{1,0:T(8,128)(2,1)S(1)}, u32[]{:S(2)}, u32[]{:S(2)}) collective-permute-start(bf16[400,512]{1,0:T(8,128)(2,1)S(1)} %copy-done.22), channel_id=1, source_target_pairs={{0,24},{8,16},{16,8},{24,0},{1,25},{9,17},{17,9},{25,1},{2,26},{10... | collective-permute-start | bytes 1228808 | tf_op jit(solution)/shard_map/rows_grad_expert_3/ppermute | solution.py:771
  164.0 91.4 %copy-start.3 = (bf16[528,512]{1,0:T(8,128)(2,1)}, bf16[528,512]{1,0:T(8,128)(2,1)S(1)}, u32[]{:S(2)}) copy-start(bf16[528,512]{1,0:T(8,128)(2,1)S(1)} %fusion.3.refs_0_) | copy-start | bytes 1622020
  164.0 36.6 %collective-permute-start.19 = (bf16[528,512]{1,0:T(8,128)(2,1)S(1)}, bf16[528,512]{1,0:T(8,128)(2,1)S(1)}, u32[]{:S(2)}, u32[]{:S(2)}) collective-permute-start(bf16[528,512]{1,0:T(8,128)(2,1)S(1)} %fusion.3.refs_0_), channel_id=1, source_target_pairs={{0,2},{2,0},{4,6},{6,4},{1,3},{3,1},{5,7},{7,5},{8,10},{10,8},{12,... | collective-permute-start | bytes 1622024 | tf_op jit(solution)/shard_map/expert_sums_ctx_1/ppermute | solution.py:771
  165.3 35.3 %collective-permute-start.20 = (bf16[528,512]{1,0:T(8,128)(2,1)S(1)}, bf16[528,512]{1,0:T(8,128)(2,1)S(1)}, u32[]{:S(2)}, u32[]{:S(2)}) collective-permute-start(bf16[528,512]{1,0:T(8,128)(2,1)S(1)} %fusion.3.refs_0_), channel_id=1, source_target_pairs={{0,4},{2,6},{4,0},{6,2},{1,5},{3,7},{5,1},{7,3},{8,12},{10,14},{12... | collective-permute-start | bytes 1622024 | tf_op jit(solution)/shard_map/expert_sums_ctx_2/ppermute | solution.py:771
  166.0 34.7 %collective-permute-start.21 = (bf16[528,512]{1,0:T(8,128)(2,1)S(1)}, bf16[528,512]{1,0:T(8,128)(2,1)}, u32[]{:S(2)}, u32[]{:S(2)}) collective-permute-start(bf16[528,512]{1,0:T(8,128)(2,1)S(1)} %fusion.3.refs_0_), channel_id=1, source_target_pairs={{0,6},{2,4},{4,2},{6,0},{1,7},{3,5},{5,3},{7,1},{8,14},{10,12},{12... | collective-permute-start | bytes 1622024 | tf_op jit(solution)/shard_map/expert_sums_ctx_3/ppermute | solution.py:771
  180.8 12.9 %collective-permute-start.12 = (bf16[192,512]{1,0:T(8,128)(2,1)}, bf16[192,512]{1,0:T(8,128)(2,1)S(1)}, u32[]{:S(2)}, u32[]{:S(2)}) collective-permute-start(bf16[192,512]{1,0:T(8,128)(2,1)} %get-tuple-element.91), channel_id=1, source_target_pairs={{0,2},{2,0},{4,6},{6,4},{1,3},{3,1},{5,7},{7,5},{8,10},{10,8},{12,... | collective-permute-start | bytes 589832 | tf_op jit(solution)/shard_map/attended_grad_ctx_1/ppermute | solution.py:771
  181.7 17.6 %collective-permute-start.13 = (bf16[192,512]{1,0:T(8,128)(2,1)}, bf16[192,512]{1,0:T(8,128)(2,1)}, u32[]{:S(2)}, u32[]{:S(2)}) collective-permute-start(bf16[192,512]{1,0:T(8,128)(2,1)} %get-tuple-element.92), channel_id=1, source_target_pairs={{0,4},{2,6},{4,0},{6,2},{1,5},{3,7},{5,1},{7,3},{8,12},{10,14},{12... | collective-permute-start | bytes 589832 | tf_op jit(solution)/shard_map/attended_grad_ctx_2/ppermute | solution.py:771
  193.7 6.9 %collective-permute-start.14 = (bf16[192,512]{1,0:T(8,128)(2,1)}, bf16[192,512]{1,0:T(8,128)(2,1)}, u32[]{:S(2)}, u32[]{:S(2)}) collective-permute-start(bf16[192,512]{1,0:T(8,128)(2,1)} %get-tuple-element.93), channel_id=1, source_target_pairs={{0,6},{2,4},{4,2},{6,0},{1,7},{3,5},{5,3},{7,1},{8,14},{10,12},{12... | collective-permute-start | bytes 589832 | tf_op jit(solution)/shard_map/attended_grad_ctx_3/ppermute | solution.py:771
  195.3 54.2 %all-to-all-start.1 = ((bf16[4,384,512]{2,1,0:T(8,128)(2,1)}), bf16[4,384,512]{2,1,0:T(8,128)(2,1)S(1)}, u32[]{:S(2)}, u32[]{:S(2)}) async-start(bf16[4,384,512]{2,1,0:T(8,128)(2,1)} %get-tuple-element.82), calls=%async_computation.1 | async-start | bytes 3145728 | tf_op jit(solution)/shard_map/results/all_to_all | solution.py:776
  221.7 3.0 %collective-permute-start.25 = (bf16[4,272,512]{2,1,0:T(8,128)(2,1)}, bf16[4,272,512]{2,1,0:T(8,128)(2,1)S(1)}, u32[]{:S(2)}, u32[]{:S(2)}) collective-permute-start(bf16[4,272,512]{2,1,0:T(8,128)(2,1)} %get-tuple-element.105), channel_id=1, source_target_pairs={{0,1},{1,0},{2,3},{3,2},{4,5},{5,4},{6,7},{7,6},{8,9},{9,8},{10,11... | collective-permute-start | bytes 3342344 | tf_op jit(solution)/shard_map/shared_dp_1/ppermute | solution.py:771
  226.9 10.7 %collective-permute-start.28 = (bf16[272,512]{1,0:T(8,128)(2,1)}, bf16[272,512]{1,0:T(8,128)(2,1)S(1)}, u32[]{:S(2)}, u32[]{:S(2)}) collective-permute-start(bf16[272,512]{1,0:T(8,128)(2,1)} %get-tuple-element.118), channel_id=1, source_target_pairs={{0,6},{2,4},{4,2},{6,0},{1,7},{3,5},{5,3},{7,1},{8,14},{10,12},{12... | collective-permute-start | bytes 835592 | tf_op jit(solution)/shard_map/shared_ctx_3/ppermute | solution.py:771
  228.8 14.1 %collective-permute-start.27 = (bf16[272,512]{1,0:T(8,128)(2,1)}, bf16[272,512]{1,0:T(8,128)(2,1)}, u32[]{:S(2)}, u32[]{:S(2)}) collective-permute-start(bf16[272,512]{1,0:T(8,128)(2,1)} %get-tuple-element.119), channel_id=1, source_target_pairs={{0,4},{2,6},{4,0},{6,2},{1,5},{3,7},{5,1},{7,3},{8,12},{10,14},{12... | collective-permute-start | bytes 835592 | tf_op jit(solution)/shard_map/shared_ctx_2/ppermute | solution.py:771
  230.2 13.5 %collective-permute-start.26 = (bf16[272,512]{1,0:T(8,128)(2,1)}, bf16[272,512]{1,0:T(8,128)(2,1)}, u32[]{:S(2)}, u32[]{:S(2)}) collective-permute-start(bf16[272,512]{1,0:T(8,128)(2,1)} %get-tuple-element.117), channel_id=1, source_target_pairs={{0,2},{2,0},{4,6},{6,4},{1,3},{3,1},{5,7},{7,5},{8,10},{10,8},{12,... | collective-permute-start | bytes 835592 | tf_op jit(solution)/shard_map/shared_ctx_1/ppermute | solution.py:771
  230.4 25.0 %collective-permute-start.22 = (bf16[192,512]{1,0:T(8,128)(2,1)}, bf16[192,512]{1,0:T(8,128)(2,1)}, u32[]{:S(2)}, u32[]{:S(2)}) collective-permute-start(bf16[192,512]{1,0:T(8,128)(2,1)} %get-tuple-element.101), channel_id=1, source_target_pairs={{0,2},{2,0},{4,6},{6,4},{1,3},{3,1},{5,7},{7,5},{8,10},{10,8},{12,... | collective-permute-start | bytes 589832 | tf_op jit(solution)/shard_map/input_grad_ctx_1/ppermute | solution.py:771
  232.3 23.1 %collective-permute-start.23 = (bf16[192,512]{1,0:T(8,128)(2,1)}, bf16[192,512]{1,0:T(8,128)(2,1)}, u32[]{:S(2)}, u32[]{:S(2)}) collective-permute-start(bf16[192,512]{1,0:T(8,128)(2,1)} %get-tuple-element.102), channel_id=1, source_target_pairs={{0,4},{2,6},{4,0},{6,2},{1,5},{3,7},{5,1},{7,3},{8,12},{10,14},{12... | collective-permute-start | bytes 589832 | tf_op jit(solution)/shard_map/input_grad_ctx_2/ppermute | solution.py:771
  237.5 18.4 %collective-permute-start.24 = (bf16[192,512]{1,0:T(8,128)(2,1)}, bf16[192,512]{1,0:T(8,128)(2,1)}, u32[]{:S(2)}, u32[]{:S(2)}) collective-permute-start(bf16[192,512]{1,0:T(8,128)(2,1)} %get-tuple-element.103), channel_id=1, source_target_pairs={{0,6},{2,4},{4,2},{6,0},{1,7},{3,5},{5,3},{7,1},{8,14},{10,12},{12... | collective-permute-start | bytes 589832 | tf_op jit(solution)/shard_map/input_grad_ctx_3/ppermute | solution.py:771
  245.2 10.8 %collective-permute-start.31 = (bf16[272,128]{1,0:T(8,128)(2,1)S(1)}, bf16[272,128]{1,0:T(8,128)(2,1)S(1)}, u32[]{:S(2)}, u32[]{:S(2)}) collective-permute-start(bf16[272,128]{1,0:T(8,128)(2,1)S(1)} %get-tuple-element.125), channel_id=1, source_target_pairs={{0,24},{8,16},{16,8},{24,0},{1,25},{9,17},{17,9},{25,1},{2,26},{10... | collective-permute-start | bytes 208904 | tf_op jit(solution)/shard_map/shared_expert_3/ppermute | solution.py:771
  247.7 8.7 %collective-permute-start.30 = (bf16[272,128]{1,0:T(8,128)(2,1)S(1)}, bf16[272,128]{1,0:T(8,128)(2,1)S(1)}, u32[]{:S(2)}, u32[]{:S(2)}) collective-permute-start(bf16[272,128]{1,0:T(8,128)(2,1)S(1)} %get-tuple-element.126), channel_id=1, source_target_pairs={{0,16},{8,24},{16,0},{24,8},{1,17},{9,25},{17,1},{25,9},{2,18},{10... | collective-permute-start | bytes 208904 | tf_op jit(solution)/shard_map/shared_expert_2/ppermute | solution.py:771
  255.4 6.3 %collective-permute-start.39 = (bf16[528,512]{1,0:T(8,128)(2,1)S(1)}, bf16[528,512]{1,0:T(8,128)(2,1)S(1)}, u32[]{:S(2)}, u32[]{:S(2)}) collective-permute-start(bf16[528,512]{1,0:T(8,128)(2,1)S(1)} %fusion.3.refs_0_), channel_id=1, source_target_pairs={{0,1},{1,0},{2,3},{3,2},{4,5},{5,4},{6,7},{7,6},{8,9},{9,8},{10,11... | collective-permute-start | bytes 1622024 | tf_op jit(solution)/shard_map/expert_sums_dp_1/ppermute | solution.py:771
  255.4 7.6 %collective-permute-start.40 = (bf16[528,512]{1,0:T(8,128)(2,1)S(1)}, bf16[528,512]{1,0:T(8,128)(2,1)S(1)}, u32[]{:S(2)}, u32[]{:S(2)}) collective-permute-start(bf16[528,512]{1,0:T(8,128)(2,1)S(1)} %copy-done.13), channel_id=1, source_target_pairs={{0,1},{1,0},{2,3},{3,2},{4,5},{5,4},{6,7},{7,6},{8,9},{9,8},{10,11... | collective-permute-start | bytes 1622024 | tf_op jit(solution)/shard_map/expert_sums_dp_1/ppermute | solution.py:771
  255.9 7.1 %collective-permute-start.41 = (bf16[528,512]{1,0:T(8,128)(2,1)S(1)}, bf16[528,512]{1,0:T(8,128)(2,1)S(1)}, u32[]{:S(2)}, u32[]{:S(2)}) collective-permute-start(bf16[528,512]{1,0:T(8,128)(2,1)S(1)} %copy-done.15), channel_id=1, source_target_pairs={{0,1},{1,0},{2,3},{3,2},{4,5},{5,4},{6,7},{7,6},{8,9},{9,8},{10,11... | collective-permute-start | bytes 1622024 | tf_op jit(solution)/shard_map/expert_sums_dp_1/ppermute | solution.py:771
  256.0 7.0 %collective-permute-start.42 = (bf16[528,512]{1,0:T(8,128)(2,1)}, bf16[528,512]{1,0:T(8,128)(2,1)S(1)}, u32[]{:S(2)}, u32[]{:S(2)}) collective-permute-start(bf16[528,512]{1,0:T(8,128)(2,1)} %collective-permute-done.21.refs_19_.refs_3_), channel_id=1, source_target_pairs={{0,1},{1,0},{2,3},{3,2},{4,5},{5,4},{6,7},{7,6},{8,9},{9,8},{10,11... | collective-permute-start | bytes 1622024 | tf_op jit(solution)/shard_map/expert_sums_dp_1/ppermute | solution.py:771
  256.4 4.3 %collective-permute-start.29 = (bf16[272,128]{1,0:T(8,128)(2,1)S(1)}, bf16[272,128]{1,0:T(8,128)(2,1)S(1)}, u32[]{:S(2)}, u32[]{:S(2)}) collective-permute-start(bf16[272,128]{1,0:T(8,128)(2,1)S(1)} %get-tuple-element.124), channel_id=1, source_target_pairs={{0,8},{8,0},{16,24},{24,16},{1,9},{9,1},{17,25},{25,17},{2,10},{10... | collective-permute-start | bytes 208904 | tf_op jit(solution)/shard_map/shared_expert_1/ppermute | solution.py:771
  260.8 14.8 %copy-start.6 = (bf16[272,128]{1,0:T(8,128)(2,1)}, bf16[272,128]{1,0:T(8,128)(2,1)S(1)}, u32[]{:S(2)}) copy-start(bf16[272,128]{1,0:T(8,128)(2,1)S(1)} %add_convert_fusion.8.refs_0_) | copy-start | bytes 208900
  260.8 13.9 %collective-permute-start.32 = (bf16[272,128]{1,0:T(8,128)(2,1)S(1)}, bf16[272,128]{1,0:T(8,128)(2,1)S(1)}, u32[]{:S(2)}, u32[]{:S(2)}) collective-permute-start(bf16[272,128]{1,0:T(8,128)(2,1)S(1)} %add_convert_fusion.8.refs_0_), channel_id=1, source_target_pairs={{0,2},{1,3},{2,0},{3,1},{4,6},{5,7},{6,4},{7,5},{8,10},{9,11},{10,... | collective-permute-start | bytes 208904 | tf_op jit(solution)/shard_map/shared_sums/ppermute | solution.py:781
  261.7 13.9 %collective-permute-start.33 = (bf16[272,128]{1,0:T(8,128)(2,1)S(1)}, bf16[272,128]{1,0:T(8,128)(2,1)S(1)}, u32[]{:S(2)}, u32[]{:S(2)}) collective-permute-start(bf16[272,128]{1,0:T(8,128)(2,1)S(1)} %add_convert_fusion.8.refs_0_), channel_id=1, source_target_pairs={{0,4},{1,5},{2,6},{3,7},{4,0},{5,1},{6,2},{7,3},{8,12},{9,13},{10,... | collective-permute-start | bytes 208904 | tf_op jit(solution)/shard_map/shared_sums/ppermute | solution.py:781
  272.4 7.5 %collective-permute-start.34 = (bf16[272,128]{1,0:T(8,128)(2,1)S(1)}, bf16[272,128]{1,0:T(8,128)(2,1)S(1)}, u32[]{:S(2)}, u32[]{:S(2)}) collective-permute-start(bf16[272,128]{1,0:T(8,128)(2,1)S(1)} %add_convert_fusion.8.refs_0_), channel_id=1, source_target_pairs={{0,6},{1,7},{2,4},{3,5},{4,2},{5,3},{6,0},{7,1},{8,14},{9,15},{10,... | collective-permute-start | bytes 208904 | tf_op jit(solution)/shard_map/shared_sums/ppermute | solution.py:781
  273.7 6.1 %collective-permute-start.35 = (bf16[272,128]{1,0:T(8,128)(2,1)S(1)}, bf16[272,128]{1,0:T(8,128)(2,1)S(1)}, u32[]{:S(2)}, u32[]{:S(2)}) collective-permute-start(bf16[272,128]{1,0:T(8,128)(2,1)S(1)} %add_convert_fusion.8.refs_0_), channel_id=1, source_target_pairs={{0,1},{1,0},{2,3},{3,2},{4,5},{5,4},{6,7},{7,6},{8,9},{9,8},{10,11... | collective-permute-start | bytes 208904 | tf_op jit(solution)/shard_map/shared_sums/ppermute | solution.py:781
  273.7 6.2 %collective-permute-start.36 = (bf16[272,128]{1,0:T(8,128)(2,1)S(1)}, bf16[272,128]{1,0:T(8,128)(2,1)S(1)}, u32[]{:S(2)}, u32[]{:S(2)}) collective-permute-start(bf16[272,128]{1,0:T(8,128)(2,1)S(1)} %add_convert_fusion.8.refs_0_), channel_id=1, source_target_pairs={{0,3},{1,2},{2,1},{3,0},{4,7},{5,6},{6,5},{7,4},{8,11},{9,10},{10,... | collective-permute-start | bytes 208904 | tf_op jit(solution)/shard_map/shared_sums/ppermute | solution.py:781
  274.7 5.2 %collective-permute-start.37 = (bf16[272,128]{1,0:T(8,128)(2,1)S(1)}, bf16[272,128]{1,0:T(8,128)(2,1)S(1)}, u32[]{:S(2)}, u32[]{:S(2)}) collective-permute-start(bf16[272,128]{1,0:T(8,128)(2,1)S(1)} %add_convert_fusion.8.refs_0_), channel_id=1, source_target_pairs={{0,5},{1,4},{2,7},{3,6},{4,1},{5,0},{6,3},{7,2},{8,13},{9,12},{10,... | collective-permute-start | bytes 208904 | tf_op jit(solution)/shard_map/shared_sums/ppermute | solution.py:781
  275.6 4.8 %collective-permute-start.38 = (bf16[272,128]{1,0:T(8,128)(2,1)S(1)}, bf16[272,128]{1,0:T(8,128)(2,1)S(1)}, u32[]{:S(2)}, u32[]{:S(2)}) collective-permute-start(bf16[272,128]{1,0:T(8,128)(2,1)S(1)} %add_convert_fusion.8.refs_0_), channel_id=1, source_target_pairs={{0,7},{1,6},{2,5},{3,4},{4,3},{5,2},{6,1},{7,0},{8,15},{9,14},{10,... | collective-permute-start | bytes 208904 | tf_op jit(solution)/shard_map/shared_sums/ppermute | solution.py:781
  (36 other events, 96.5 us)
where the time goes:
time: 290 us; the launch traced here: 287 us
  Pallas kernels  129 us (44%)
  waiting for transfers between devices  68.7 us (24%)
  starting transfers between devices  57.5 us (20%)
  local copies, waits for them, and re-layouts  20.6 us (7%)
  other arithmetic  9.47 us (3%)
    ppermute x36, waiting for transfers between devices, swap(): return lax.ppermute(x, axis, [(i, i ^ d) for i in range(size)])  68.2 us
    pallas_call x4, Pallas kernels, expert_call(): pl.pallas_call(kernel, grid_spec=pltpu.PrefetchScalarGridSpec(num_scalar_...  57.8 us
    ppermute x36, starting transfers between devices, swap(): return lax.ppermute(x, axis, [(i, i ^ d) for i in range(size)])  40.6 us
    pallas_call x1, Pallas kernels, attend_back_call(): pl.pallas_call(kernel, grid=(images,), in_specs=[SMEM_SPEC] + [full(a) fo...  20.1 us
    pallas_call x1, Pallas kernels, attend_call(): pl.pallas_call(kernel, grid=(images,), in_specs=[full(a) for a in ins] +...  12.8 us
    pallas_call x1, Pallas kernels, middle_back_call(): pl.pallas_call(kernel, in_specs=[SMEM_SPEC] + [VMEM_SPEC] * len(ins) + [A...  11.6 us
    unnamed x82, local copies, waits for them, and re-layouts  11 us
    all_to_all x2, starting transfers between devices, exchange(): return lax.all_to_all(x, axis, split_axis=0, concat_axis=0, tiled=True)  9.95 us
  transfers between devices with their start and end apart: 45, of which 15 were waited for; matrix products, arithmetic and copies ran while one was open for 5% of the time, Pallas kernels for 38%

commit v1 on v0

v1 whole, which is shorter than its diff:
```python
import jax
import jax.numpy as jnp
from jax import lax
from jax.experimental import pallas as pl
from jax.experimental.pallas import tpu as pltpu
from jax.sharding import PartitionSpec as P

HEADS = 8
EPS = 1e-06
NEG = -1e30
F32 = jnp.float32
BF16 = jnp.bfloat16
I32 = jnp.int32
LANES = 128
PAD = 16
EXPERT_CALLS = 4
EXPERT_CHUNK = 512


def dot_nn(a, b):
    return lax.dot_general(a, b, (((1,), (0,)), ((), ())), preferred_element_type=F32)


def dot_nt(a, b):
    return lax.dot_general(a, b, (((1,), (1,)), ((), ())), preferred_element_type=F32)


def iota(shape, axis):
    return lax.broadcasted_iota(I32, shape, axis)


def norm_stats(v):
    centre = v - jnp.mean(v, axis=1, keepdims=True)
    inv = lax.rsqrt(jnp.mean(centre * centre, axis=1, keepdims=True) + EPS)
    return centre * inv, inv


def norm_back(gy, xhat, inv):
    return (
        gy - jnp.mean(gy, axis=1, keepdims=True) - xhat * jnp.mean(gy * xhat, axis=1, keepdims=True)
    ) * inv


def soft_gates(logits, expert_count):
    logits = jnp.where(iota(logits.shape, 1) < expert_count, logits, NEG)
    e = jnp.exp(logits - jnp.max(logits, axis=1, keepdims=True))
    return e / jnp.sum(e, axis=1, keepdims=True)


ERF = (0.254829592, -0.284496736, 1.421413741, -1.453152027, 1.061405429)
ERF_P = 0.3275911 * 0.7071067811865476


def gelu_parts(h):
    t = 1.0 / (1.0 + ERF_P * jnp.abs(h))
    e = jnp.exp(-0.5 * h * h)
    poly = 0.5 * ERF[4]
    for c in ERF[3::-1]:
        poly = poly * t + 0.5 * c
    tail = poly * t * e
    cdf = jnp.where(h >= 0, 1.0 - tail, tail)
    return h * cdf, cdf + h * (e * 0.3989422804014327)


def params(mib):
    return pltpu.CompilerParams(vmem_limit_bytes=mib * 2**20)


def takes(us):
    return pl.CostEstimate(flops=int(us * 1.15e9), bytes_accessed=1 << 17, transcendentals=0)


ANY_SPEC = pl.BlockSpec(memory_space=pl.ANY)
SMEM_SPEC = pl.BlockSpec(memory_space=pltpu.SMEM)
VMEM_SPEC = pl.BlockSpec(memory_space=pltpu.VMEM)


def shape(dims, dtype):
    return jax.ShapeDtypeStruct(dims, dtype)


def pieces_call(place, tokens, mask):
    groups, body, width = tokens.shape
    images, rows = mask.shape[1:]

    def kernel(place_ref, tokens_ref, mask_ref, *outs):
        for d in range(groups):
            group = place_ref[0] ^ d
            outs[d][:body, :] = tokens_ref[group]
            outs[d][body:, :] = jnp.zeros((PAD, width), BF16)
            live = mask_ref[group].astype(F32)
            live = jnp.concatenate([live, jnp.zeros((images, LANES - rows), F32)], axis=1)
            live = jnp.concatenate([live, jnp.zeros((PAD - images, LANES), F32)], axis=0)
            outs[d][body:, :LANES] = live.astype(BF16)

    return pl.pallas_call(
        kernel,
        in_specs=[SMEM_SPEC] + [VMEM_SPEC] * 2,
        out_specs=[VMEM_SPEC] * groups,
        out_shape=[shape((body + PAD, width), BF16)] * groups,
        compiler_params=params(58),
        cost_estimate=takes(1),
        name="pieces",
    )(place, tokens, mask)


def route_call(place, ints, cotangent, expert_count, capacity):
    groups, group_rows, width = cotangent.shape
    tok = groups * group_rows
    e_rows = max(PAD, expert_count)

    def kernel(place_ref, ints_ref, cot_ref, *outs):
        row_ref, col_ref = outs[:2]
        slots = outs[2:]
        ctx, expert = place_ref[0], place_ref[1]
        vals = ints_ref[...]
        ids = (vals[0:1], vals[1:2])
        key = vals[2:3]
        keys = jnp.broadcast_to(key.astype(F32), (8, tok))
        key_col = keys.T[:, :1]
        before = (key_col < keys[:1]).astype(BF16)
        hot = [(iota((e_rows, tok), 0) == i).astype(F32) for i in ids]
        counts = dot_nn(jnp.concatenate(hot, axis=0).astype(BF16), before)
        first_total = jnp.sum(hot[0], axis=1, keepdims=True)
        ranks = (
            jnp.sum(hot[0] * counts[:e_rows], axis=0, keepdims=True),
            jnp.sum(hot[1] * (counts[e_rows:] + first_total), axis=0, keepdims=True),
        )
        dest = [
            jnp.where(r < capacity, i.astype(F32) * capacity + r, -1.0)
            for r, i in zip(ranks, ids)
        ]
        rows = jnp.concatenate(
            [dest[0], dest[1], jnp.full((6, tok), -1.0, F32)], axis=0
        )
        row_ref[...] = rows.astype(I32)
        col_ref[...] = rows.T.astype(I32)
        d0, d1 = dest[0].astype(I32), dest[1].astype(I32)
        up = jnp.concatenate([cot_ref[ctx ^ d] for d in range(groups)], axis=0)
        for e in range(expert_count):
            ids_here = iota((capacity, tok), 0) + e * capacity
            pick = ((ids_here == d0) | (ids_here == d1)).astype(F32).astype(BF16)
            slots[0][e] = dot_nn(pick, up).astype(BF16)
        slots[1][0] = slots[0][expert]

    return pl.pallas_call(
        kernel,
        in_specs=[SMEM_SPEC, VMEM_SPEC, VMEM_SPEC],
        out_specs=[VMEM_SPEC] * 4,
        out_shape=[
            shape((8, tok), I32),
            shape((tok, 8), I32),
            shape((expert_count, capacity, width), BF16),
            shape((1, capacity, width), BF16),
        ],
        compiler_params=params(58),
        cost_estimate=takes(4),
        name="route",
    )(place, ints, cotangent)


def gather_image(pieces, i, rows):
    at = pl.ds(pl.multiple_of(i * rows, rows), rows)
    return jnp.concatenate([p[at, :] for p in pieces], axis=0).astype(F32)


def gather_mask(pieces, i, rows, body):
    cols = []
    for p in pieces:
        block = p[body : body + PAD, :LANES].astype(F32).T
        cols.append(
            jnp.sum(jnp.where(iota(block.shape, 1) == i, block, 0.0), axis=1, keepdims=True)[:rows]
        )
    return jnp.concatenate(cols, axis=0)


def two_heads(block, size):
    zero = jnp.zeros((size, block.shape[1]), block.dtype)
    return jnp.concatenate(
        [
            jnp.concatenate([block[:size], zero], axis=0),
            jnp.concatenate([zero, block[size:]], axis=0),
        ],
        axis=1,
    )


def attend_call(pieces, gain, shift, qkv, query_bias, value_bias, images, rows, after):
    count = len(pieces)
    width = qkv.shape[0]
    seq = count * rows
    size = width // HEADS
    body = images * rows
    scale = size ** (-0.5)

    def kernel(*refs):
        ps = refs[:count]
        gain_ref, shift_ref, qkv_ref, qb_ref, vb_ref = refs[count : count + 5]
        outs = refs[count + 6 : 2 * count + 6]
        qt_ref, k_ref, v_ref, lse_ref, ot, vt = refs[2 * count + 6 :]
        i = pl.program_id(0)
        x = gather_image(ps, i, rows)
        live = gather_mask(ps, i, rows, body) > 0
        xhat, _ = norm_stats(x)
        n = (xhat * gain_ref[...] + shift_ref[...]).astype(BF16)
        qt_ref[0] = ((dot_nn(n, qkv_ref[:, :width]) + qb_ref[...]) * scale).astype(BF16).T
        k_ref[0] = dot_nn(n, qkv_ref[:, width : 2 * width]).astype(BF16)
        v = (dot_nn(n, qkv_ref[:, 2 * width :]) + vb_ref[...]).astype(BF16)
        v_ref[0] = v
        vt[...] = v.T
        for h in range(0, HEADS, 2):
            pair = slice(h * size, (h + 2) * size)
            s = dot_nn(k_ref[0, :, pair], two_heads(qt_ref[0, pair, :], size))
            s = jnp.where(live, s, NEG)
            top = jnp.max(s, axis=0, keepdims=True)
            e = jnp.exp(s - top)
            total = jnp.sum(e, axis=0, keepdims=True)
            lse_ref[0, h // 2 : h // 2 + 1, :] = top + jnp.log(total)
            p = (e * (1.0 / total)).astype(BF16)
            for k in range(2):
                at = slice((h + k) * size, (h + k + 1) * size)
                ot[at, :] = dot_nn(vt[at, :], p[:, k * seq : (k + 1) * seq])
        o = ot[...].T.astype(BF16)
        at = pl.ds(pl.multiple_of(i * rows, rows), rows)
        for d in range(count):
            outs[d][at, :] = o[d * rows : (d + 1) * rows]

    full = lambda a: pl.BlockSpec(a.shape, lambda i: (0,) * a.ndim)
    ins = list(pieces) + [gain, shift, qkv, query_bias, value_bias]
    per_image = lambda dims: pl.BlockSpec((1,) + dims, lambda i: (i, 0, 0))
    saved = [(width, seq), (seq, width), (seq, width), (HEADS // 2, 2 * seq)]
    return pl.pallas_call(
        kernel,
        grid=(images,),
        in_specs=[full(a) for a in ins] + [ANY_SPEC],
        out_specs=[pl.BlockSpec((body, width), lambda i: (0, 0))] * count
        + [per_image(dims) for dims in saved],
        out_shape=[shape((body, width), BF16)] * count
        + [shape((images,) + dims, BF16) for dims in saved[:3]]
        + [shape((images,) + saved[3], F32)],
        scratch_shapes=[pltpu.VMEM((width, seq), F32), pltpu.VMEM((width, seq), BF16)],
        compiler_params=params(58),
        cost_estimate=takes(12),
        name="attend",
    )(*ins, after)


def middle_call(place, attended, pieces, proj, proj_bias, gain, shift, dest_rows, expert_count, capacity):
    count = len(attended)
    body, width = attended[0].shape
    tok = count * body

    def kernel(place_ref, *refs):
        att, ps = refs[:count], refs[count : 2 * count]
        proj_ref, pb_ref, gain_ref, shift_ref, dest_ref = refs[2 * count : 2 * count + 5]
        mid_ref, n_ref = refs[2 * count + 5 : 2 * count + 7]
        slots = refs[2 * count + 7 :]
        expert = place_ref[1]
        for d in range(count):
            at = slice(d * body, (d + 1) * body)
            mid = (
                ps[d][:body, :].astype(F32) + dot_nn(att[d][...], proj_ref[...]) + pb_ref[...]
            )
            mid_ref[at, :] = mid
            xhat, _ = norm_stats(mid)
            n_ref[at, :] = (xhat * gain_ref[...] + shift_ref[...]).astype(BF16)
        n = n_ref[...]
        d0, d1 = dest_ref[0:1, :], dest_ref[1:2, :]
        for d in range(expert_count):
            ids_here = iota((capacity, tok), 0) + (expert ^ d) * capacity
            pick = ((ids_here == d0) | (ids_here == d1)).astype(F32).astype(BF16)
            slots[d][...] = dot_nn(pick, n).astype(BF16)

    ins = list(attended) + list(pieces) + [proj, proj_bias, gain, shift, dest_rows]
    return pl.pallas_call(
        kernel,
        in_specs=[SMEM_SPEC] + [VMEM_SPEC] * len(ins),
        out_specs=[VMEM_SPEC] * (2 + expert_count),
        out_shape=[shape((tok, width), F32), shape((tok, width), BF16)]
        + [shape((capacity, width), BF16)] * expert_count,
        compiler_params=params(58),
        cost_estimate=takes(5),
        name="middle",
    )(place, *ins)


def expert_call(
    place, xs, upstream, first, router, up, up_bias, down, down_bias, held, expert_count, after
):
    blocks = len(xs)
    capacity, width = xs[0].shape
    hidden_width = up.shape[1]
    total = blocks * capacity
    chunk = EXPERT_CHUNK
    steps = hidden_width // chunk
    sub = min(total, 384)
    ins = list(xs) + [upstream, router, up, up_bias, down, down_bias]
    n_own = len(ins)
    ins += [] if held is None else list(held)
    n_in = len(ins) + len(after)

    def kernel(place_ref, *refs):
        x_refs, u_ref = refs[:blocks], refs[blocks]
        rw, up_ref, ub_ref, dn_ref, db_ref = refs[blocks + 1 : blocks + 6]
        o = refs[n_in:]
        out_ref, g_all, act, gh_all = o[:4]
        gx_refs = o[4 : 4 + blocks]
        x_all, gate, out_acc, gx_acc = o[4 + blocks :]
        j = pl.program_id(0)
        slots = [lax.rem(place_ref[1] ^ (first + b), blocks) for b in range(blocks)]

        @pl.when(j == 0)
        def _():
            expert = place_ref[1]
            for b in range(blocks):
                at = slice(b * capacity, (b + 1) * capacity)
                x = x_refs[b][...]
                gates = soft_gates(dot_nn(x, rw[...]), expert_count)
                mine = jnp.sum(
                    jnp.where(iota(gates.shape, 1) == expert, gates, 0.0), axis=1, keepdims=True
                )
                x_all[at, :] = x
                g_all[at, :] = (u_ref[slots[b]].astype(F32) * mine).astype(BF16)
                gate[at, :] = jnp.broadcast_to(mine, (capacity, LANES))
            out_acc[...] = jnp.zeros_like(out_acc)
            gx_acc[...] = jnp.zeros_like(gx_acc)

        w_up, w_dn = up_ref[...], dn_ref[...]
        for r in range(total // sub):
            at = slice(r * sub, (r + 1) * sub)
            h = dot_nn(x_all[at, :], w_up) + ub_ref[...]
            a, slope = gelu_parts(h)
            a = a.astype(BF16)
            act[at, :] = a
            out_acc[at, :] += dot_nn(a, w_dn)
            gh = (dot_nt(g_all[at, :], w_dn) * slope).astype(BF16)
            gh_all[at, :] = gh
            gx_acc[at, :] += dot_nt(gh, w_up)

        @pl.when(j == steps - 1)
        def _():
            for b in range(blocks):
                at = slice(b * capacity, (b + 1) * capacity)
                out = (out_acc[at, :] + db_ref[...]).astype(BF16).astype(F32)
                out_ref[slots[b]] = (out * gate[at, :1]).astype(BF16)
                gg = jnp.sum(out * u_ref[slots[b]].astype(F32), axis=1, keepdims=True)
                line = jnp.broadcast_to(gg, (capacity, LANES)).T[:PAD]
                high = line.astype(BF16).astype(F32)
                mean = (line - high).astype(BF16).astype(F32)
                k = iota(line.shape, 0)
                parts = jnp.where(
                    k == 0, high, jnp.where(k == 1, mean, jnp.where(k == 2, line - high - mean, 0.0))
                )
                gx_refs[b][:capacity, :] = gx_acc[at, :].astype(BF16)
                gx_refs[b][capacity:, :] = jnp.concatenate(
                    [parts, jnp.zeros((PAD, width - capacity), F32)], axis=1
                ).astype(BF16)

    full = lambda a: pl.BlockSpec(a.shape, lambda j, p: (0,) * a.ndim)
    const = lambda dims: pl.BlockSpec(dims, lambda j, p: (0,) * len(dims))
    blocks_of = pl.BlockSpec((blocks, capacity, width), lambda j, p: ((p[1] ^ first) // blocks, 0, 0))
    hidden_of = pl.BlockSpec((total, chunk), lambda j, p: (first // blocks, j))
    specs = (
        [full(a) for a in xs]
        + [full(upstream) if upstream.shape[0] == blocks else blocks_of]
        + [
            full(router),
            pl.BlockSpec((width, chunk), lambda j, p: (0, j)),
            pl.BlockSpec((1, chunk), lambda j, p: (0, j)),
            pl.BlockSpec((chunk, width), lambda j, p: (j, 0)),
            full(down_bias),
        ]
        + [ANY_SPEC] * (len(ins) - n_own)
    )
    return pl.pallas_call(
        kernel,
        grid_spec=pltpu.PrefetchScalarGridSpec(
            num_scalar_prefetch=1,
            grid=(steps,),
            in_specs=specs + [ANY_SPEC] * len(after),
            out_specs=[
                blocks_of,
                pl.BlockSpec((total, width), lambda j, p: (first // blocks, 0)),
                hidden_of,
                hidden_of,
            ]
            + [const((capacity + PAD, width))] * blocks,
            scratch_shapes=[
                pltpu.VMEM((total, width), BF16),
                pltpu.VMEM((total, LANES), F32),
                pltpu.VMEM((total, width), F32),
                pltpu.VMEM((total, width), F32),
            ],
        ),
        out_shape=[
            shape((expert_count, capacity, width), BF16),
            shape((expert_count * capacity, width), BF16),
            shape((expert_count * capacity, hidden_width), BF16),
            shape((expert_count * capacity, hidden_width), BF16),
        ]
        + [shape((capacity + PAD, width), BF16)] * blocks,
        input_output_aliases={} if held is None else {1 + n_own + k: k for k in range(4)},
        compiler_params=params(58),
        cost_estimate=takes(9),
        name="expert",
    )(place, *ins, *after)


def weights_call(place, xs, grads, act, grad_hidden, n_ctx, n_dp):
    capacity, width = xs[0].shape
    hidden_width = act.shape[1]
    total = len(xs) * capacity
    chunk = width
    steps = hidden_width // chunk
    per_step = n_ctx * n_dp // steps
    part = chunk // per_step
    piece_rows = 2 * part + PAD
    nx = len(xs)

    def kernel(place_ref, *refs):
        x_refs, (g_ref, act_ref, gh_ref), refs = refs[:nx], refs[nx : nx + 3], refs[nx + 3 :]
        grad_refs, (x_t, g_t, down_bias_sum) = refs[:n_dp], refs[n_dp:]
        j = pl.program_id(0)

        @pl.when(j == 0)
        def _():
            x_t[:width, :] = jnp.concatenate([r[...] for r in x_refs], axis=0).T
            x_t[width:, :] = jnp.ones((PAD, total), BF16)
            g_t[...] = g_ref[...].T
            down_bias_sum[...] = jnp.sum(g_ref[...].astype(F32), axis=0, keepdims=True)

        g_up = dot_nn(x_t[...], gh_ref[...])
        g_dn = dot_nn(g_t[...], act_ref[...]).T
        row = iota((PAD, width), 0)
        extra = jnp.where(row == 0, g_up[width:], 0.0)
        extra = jnp.where((row == 1) & (j == 0), down_bias_sum[...], extra)
        for k in range(per_step):
            vals = (
                g_up[k * part : (k + 1) * part].astype(BF16),
                g_dn[k * part : (k + 1) * part].astype(BF16),
                extra.astype(BF16) if k == 0 else jnp.zeros((PAD, width), BF16),
            )
            piece = j * per_step + k
            slot = lax.rem(piece, n_ctx) ^ place_ref[0]

            def put(ref):
                ref[slot, :part, :] = vals[0]
                ref[slot, part : 2 * part, :] = vals[1]
                ref[slot, 2 * part :, :] = vals[2]

            @pl.when(piece // n_ctx == place_ref[2])
            def _():
                put(grad_refs[0])

            @pl.when(piece // n_ctx != place_ref[2])
            def _():
                put(grad_refs[1])

    full = lambda a: pl.BlockSpec(a.shape, lambda j: (0,) * a.ndim)
    hidden_of = lambda a: pl.BlockSpec((a.shape[0], chunk), lambda j: (0, j))
    return pl.pallas_call(
        kernel,
        grid=(steps,),
        in_specs=[SMEM_SPEC]
        + [full(a) for a in xs]
        + [full(grads), hidden_of(act), hidden_of(grad_hidden)],
        out_specs=[pl.BlockSpec((n_ctx, piece_rows, width), lambda j: (0, 0, 0))] * n_dp,
        out_shape=[shape((n_ctx, piece_rows, width), BF16)] * n_dp,
        scratch_shapes=[
            pltpu.VMEM((width + PAD, total), BF16),
            pltpu.VMEM((width, total), BF16),
            pltpu.VMEM((1, width), F32),
        ],
        compiler_params=params(58),
        cost_estimate=takes(13),
        name="weights",
    )(place, *xs, grads, act, grad_hidden)


def slot_match(dest_ref, at, first, capacity):
    d = dest_ref[at, :]
    lanes = iota((d.shape[0], capacity), 1) + first
    return ((lanes == d[:, 0:1]) | (lanes == d[:, 1:2])).astype(F32).astype(BF16)


def output_call(place, results, mid, dest_cols, groups):
    blocks, capacity, width = results.shape
    tok = mid.shape[0]
    body = tok // groups

    def kernel(place_ref, o_ref, mid_ref, dest_ref, out_ref):
        rows = o_ref[...].reshape(blocks * capacity, width)
        for g in range(groups):
            at = slice(g * body, (g + 1) * body)
            acc = mid_ref[at, :] + dot_nn(slot_match(dest_ref, at, 0, blocks * capacity), rows)
            out_ref[place_ref[0] ^ g] = acc.astype(BF16)

    return pl.pallas_call(
        kernel,
        in_specs=[SMEM_SPEC] + [VMEM_SPEC] * 3,
        out_specs=VMEM_SPEC,
        out_shape=shape((groups, body, width), BF16),
        compiler_params=params(58),
        cost_estimate=takes(30),
        name="output",
    )(place, results, mid, dest_cols)


def middle_back_call(
    place, gxs, mid, normed, cotangent, dest_cols, attended, router, gain, proj, expert_count, after
):
    blocks = len(gxs)
    groups, body, width = cotangent.shape
    capacity = gxs[0].shape[0] - PAD
    tok = groups * body
    misc = -(-(expert_count + 3) // PAD) * PAD

    def kernel(place_ref, *refs):
        gx_refs = refs[:blocks]
        mid_ref, n_ref, cot_ref, dest_ref = refs[blocks : blocks + 4]
        att = refs[blocks + 4 : blocks + 4 + groups]
        router_ref, gain_ref, proj_ref = refs[blocks + 4 + groups : blocks + 7 + groups]
        refs = refs[blocks + 7 + groups + len(after) :]
        gmid_ref, ga_refs = refs[0], refs[1 : 1 + groups]
        shared_ref, branch_t, logit_t, att_all, slot_rows = refs[1 + groups :]
        ctx, expert = place_ref[0], place_ref[1]
        for d in range(blocks):
            at = pl.ds(pl.multiple_of((expert ^ d) * capacity, PAD), capacity)
            slot_rows[at, :width] = gx_refs[d][:capacity, :]
            cols = gx_refs[d][capacity:, :].astype(F32).T
            lane = iota((capacity, LANES), 1) == (expert ^ d)
            for k in range(3):
                slot_rows[at, width + k * LANES : width + (k + 1) * LANES] = jnp.where(
                    lane, cols[:capacity, k : k + 1], 0.0
                ).astype(BF16)
        g_gain = jnp.zeros((1, width), F32)
        g_shift = jnp.zeros((1, width), F32)
        g_proj_bias = jnp.zeros((1, width), F32)
        for g in range(groups):
            at = slice(g * body, (g + 1) * body)
            both = dot_nn(slot_match(dest_ref, at, 0, blocks * capacity), slot_rows[...])
            gn = both[:, :width]
            gg = both[:, width : width + LANES] + (
                both[:, width + LANES : width + 2 * LANES] + both[:, width + 2 * LANES :]
            )
            gates = soft_gates(dot_nn(n_ref[at, :], router_ref[...]), expert_count)
            logit = gates * (gg - jnp.sum(gates * gg, axis=1, keepdims=True))
            logit_t[:, at] = logit.T.astype(BF16)
            gn = gn + dot_nt(logit.astype(BF16), router_ref[...])
            xhat, inv = norm_stats(mid_ref[at, :])
            g_gain = g_gain + jnp.sum(gn * xhat, axis=0, keepdims=True)
            g_shift = g_shift + jnp.sum(gn, axis=0, keepdims=True)
            gmid = cot_ref[ctx ^ g].astype(F32) + norm_back(gn * gain_ref[...], xhat, inv)
            gmid_ref[at, :] = gmid
            branch = gmid.astype(BF16)
            g_proj_bias = g_proj_bias + jnp.sum(branch.astype(F32), axis=0, keepdims=True)
            branch_t[:, at] = branch.T
            att_all[at, :] = att[g][...]
            ga_refs[g][...] = dot_nt(branch, proj_ref[...]).astype(BF16)
        shared_ref[:width, :] = dot_nn(branch_t[...], att_all[...]).astype(BF16)
        rows = dot_nn(logit_t[...], n_ref[...])[:misc]
        k = iota((misc, width), 0)
        for s, vec in enumerate((g_gain, g_shift, g_proj_bias)):
            rows = jnp.where(k == expert_count + s, vec, rows)
        shared_ref[width:, :] = rows.astype(BF16)

    ins = (
        list(gxs) + [mid, normed, cotangent, dest_cols] + list(attended) + [router, gain, proj]
    )
    return pl.pallas_call(
        kernel,
        in_specs=[SMEM_SPEC] + [VMEM_SPEC] * len(ins) + [ANY_SPEC] * len(after),
        out_specs=[VMEM_SPEC] * (2 + groups),
        out_shape=[shape((tok, width), F32)]
        + [shape((body, width), BF16)] * groups
        + [shape((width + misc, width), BF16)],
        scratch_shapes=[
            pltpu.VMEM((width, tok), BF16),
            pltpu.VMEM((LANES, tok), BF16),
            pltpu.VMEM((tok, width), BF16),
            pltpu.VMEM((blocks * capacity, width + 3 * LANES), BF16),
        ],
        compiler_params=params(58),
        cost_estimate=takes(30),
        name="middle_back",
    )(place, *ins, *after)


def attend_back_call(
    place, pieces, grads, saved, shared, gain, shift, qkv, images, rows, n_dp, after
):
    count = len(pieces)
    width = qkv.shape[0]
    seq = count * rows
    size = width // HEADS
    body = images * rows
    scale = size ** (-0.5)
    part = (4 * width) // (n_dp * count)
    extra_rows = shared.shape[0] - width

    def kernel(place_ref, *refs):
        ps, gs = refs[:count], refs[count : 2 * count]
        qt_ref, k_ref, v_ref, lse_ref, shared_ref, gain_ref, shift_ref, qkv_ref = refs[
            2 * count : 2 * count + 8
        ]
        refs = refs[2 * count + 8 + len(after) :]
        gin_ref, sums = refs[0], refs[1 : 1 + n_dp]
        gt, w_acc, gain_acc, shift_acc, qb_acc, vb_acc = refs[1 + n_dp :]
        i = pl.program_id(0)
        x = gather_image(ps, i, rows)
        live = gather_mask(ps, i, rows, body) > 0
        xhat, inv = norm_stats(x)
        n = (xhat * gain_ref[...] + shift_ref[...]).astype(BF16)
        out_t = gather_image(gs, i, rows).astype(BF16).T
        k, v, qt = k_ref[0], v_ref[0], qt_ref[0]
        kt = k.T
        for h in range(0, HEADS, 2):
            pair = slice(h * size, (h + 2) * size)
            s = dot_nn(k[:, pair], two_heads(qt[pair], size))
            p = jnp.exp(jnp.where(live, s, NEG) - lse_ref[0, h // 2 : h // 2 + 1, :])
            dp = dot_nn(v[:, pair], two_heads(out_t[pair], size))
            pdp = p * dp
            ds = (pdp - p * jnp.sum(pdp, axis=0, keepdims=True)).astype(BF16)
            p = p.astype(BF16)
            for m in range(2):
                at = slice((h + m) * size, (h + m + 1) * size)
                one = slice(m * seq, (m + 1) * seq)
                gt[at, :] = (dot_nn(kt[at], ds[:, one]) * scale).astype(BF16)
                gt[width + at.start : width + at.stop, :] = dot_nt(qt[at], ds[:, one]).astype(BF16)
                gt[2 * width + at.start : 2 * width + at.stop, :] = dot_nt(
                    out_t[at], p[:, one]
                ).astype(BF16)
        gall = gt[...]
        gw = dot_nn(gall, n)
        gn = dot_nn(qkv_ref[...], gall).T
        qb = gall[:width].astype(F32)
        vb = gall[2 * width :].astype(F32)
        g_gain = jnp.sum(gn * xhat, axis=0, keepdims=True)
        g_shift = jnp.sum(gn, axis=0, keepdims=True)

        @pl.when(i == 0)
        def _():
            w_acc[...] = jnp.zeros_like(w_acc)
            gain_acc[...] = jnp.zeros_like(gain_acc)
            shift_acc[...] = jnp.zeros_like(shift_acc)
            qb_acc[...] = jnp.zeros_like(qb_acc)
            vb_acc[...] = jnp.zeros_like(vb_acc)

        w_acc[...] += gw
        gain_acc[...] += g_gain
        shift_acc[...] += g_shift
        qb_acc[...] += qb
        vb_acc[...] += vb
        gin = norm_back(gn * gain_ref[...], xhat, inv).astype(BF16)
        at = pl.ds(pl.multiple_of(i * rows, rows), rows)
        for d in range(count):
            gin_ref[place_ref[0] ^ d, at, :] = gin[d * rows : (d + 1) * rows]

        @pl.when(i == images - 1)
        def _():
            rows_of = [
                jnp.broadcast_to(jnp.sum(a[...], axis=1, keepdims=True), (width, LANES)).T[:1]
                for a in (qb_acc, vb_acc)
            ]
            k16 = iota((PAD, width), 0)
            vecs = jnp.zeros((PAD, width), F32)
            for s, vec in enumerate((gain_acc[...], shift_acc[...], *rows_of)):
                vecs = jnp.where(k16 == s, vec, vecs)
            for p in range(n_dp * count):
                first = p * part
                if first < 3 * width:
                    block = w_acc[first : first + part, :].astype(BF16)
                else:
                    block = shared_ref[first - 3 * width : first - 3 * width + part, :]
                if p == 0:
                    extra = vecs.astype(BF16)
                elif p * PAD <= extra_rows:
                    extra = shared_ref[width + (p - 1) * PAD : width + p * PAD, :]
                else:
                    extra = jnp.zeros((PAD, width), BF16)
                slot = p % count ^ place_ref[0]

                def put(ref):
                    ref[slot, :part, :] = block
                    ref[slot, part:, :] = extra

                @pl.when(place_ref[2] == p // count)
                def _():
                    put(sums[0])

                @pl.when(place_ref[2] != p // count)
                def _():
                    put(sums[1])

    full = lambda a: pl.BlockSpec(a.shape, lambda i: (0,) * a.ndim)
    const = lambda dims: pl.BlockSpec(dims, lambda i: (0,) * len(dims))
    per_image = lambda a: pl.BlockSpec((1,) + a.shape[1:], lambda i: (i, 0, 0))
    rest = [shared, gain, shift, qkv]
    return pl.pallas_call(
        kernel,
        grid=(images,),
        in_specs=[SMEM_SPEC] + [full(a) for a in pieces]
        + [full(a) for a in grads]
        + [per_image(a) for a in saved]
        + [full(a) for a in rest]
        + [ANY_SPEC] * len(after),
        out_specs=[const((count, body, width))] + [const((count, part + PAD, width))] * n_dp,
        out_shape=[shape((count, body, width), BF16)]
        + [shape((count, part + PAD, width), BF16)] * n_dp,
        scratch_shapes=[
            pltpu.VMEM((3 * width, seq), BF16),
            pltpu.VMEM((3 * width, width), F32),
            pltpu.VMEM((1, width), F32),
            pltpu.VMEM((1, width), F32),
            pltpu.VMEM((width, seq), F32),
            pltpu.VMEM((width, seq), F32),
        ],
        compiler_params=params(58),
        cost_estimate=takes(20),
        name="attend_back",
    )(place, *pieces, *grads, *saved, *rest, *after)


def input_call(place, gmid, gins, after):
    groups, body, width = gins.shape

    def kernel(place_ref, gmid_ref, gin_ref, *refs):
        for g in range(groups):
            group = place_ref[0] ^ g
            refs[-1][group] = (
                gmid_ref[g * body : (g + 1) * body, :] + gin_ref[group].astype(F32)
            ).astype(BF16)

    return pl.pallas_call(
        kernel,
        in_specs=[SMEM_SPEC] + [VMEM_SPEC] * 2 + [ANY_SPEC] * len(after),
        out_specs=VMEM_SPEC,
        out_shape=shape((groups, body, width), BF16),
        compiler_params=params(58),
        cost_estimate=takes(3),
        name="input",
    )(place, gmid, gins, *after)


def expert_grads_call(place, pieces, flip, hidden_width, half):
    n_ctx, piece_rows, width = pieces.shape
    chunk = width
    per_step = 2 * n_ctx * chunk // hidden_width
    part = chunk // per_step
    half = [] if half is None else list(half)

    def piece_of(q, p):
        return (p[2] ^ flip) * n_ctx + (p[0] ^ q)

    def kernel(place_ref, ref, *refs):
        up_ref, down_ref, up_bias_ref, down_bias_ref = refs[len(half) :]
        q = pl.program_id(0)
        piece = piece_of(q, place_ref)
        if half:

            @pl.when(q == 0)
            def _():
                up_bias_ref[...] = refs[2][...]
                down_bias_ref[...] = refs[3][...]

        up_ref[...] = ref[0, :part, :].astype(F32)
        down_ref[...] = ref[0, part : 2 * part, :].astype(F32)
        extra = ref[0, 2 * part :, :].astype(F32)

        @pl.when(lax.rem(piece, per_step) == 0)
        def _():
            at = pl.multiple_of(piece // per_step * chunk, chunk)
            up_bias_ref[:, pl.ds(at, chunk)] = extra[0:1]

        @pl.when(piece == 0)
        def _():
            down_bias_ref[...] = extra[1:2]

    biases = [
        pl.BlockSpec((1, hidden_width), lambda q, p: (0, 0)),
        pl.BlockSpec((1, width), lambda q, p: (0, 0)),
    ]
    return pl.pallas_call(
        kernel,
        grid_spec=pltpu.PrefetchScalarGridSpec(
            num_scalar_prefetch=1,
            grid=(n_ctx,),
            in_specs=[pl.BlockSpec((1, piece_rows, width), lambda q, p: (q, 0, 0))]
            + ([ANY_SPEC] * 2 + biases if half else []),
            out_specs=[
                pl.BlockSpec(
                    (part, chunk),
                    lambda q, p: (lax.rem(piece_of(q, p), per_step), piece_of(q, p) // per_step),
                ),
                pl.BlockSpec((part, width), lambda q, p: (piece_of(q, p), 0)),
            ]
            + biases,
        ),
        out_shape=[
            shape((width, hidden_width), F32),
            shape((hidden_width, width), F32),
            shape((1, hidden_width), F32),
            shape((1, width), F32),
        ],
        input_output_aliases={2: 0, 3: 1} if half else {},
        compiler_params=params(58),
        cost_estimate=takes(3),
        name="expert_grads",
    )(place, pieces, *half)


def shared_grads_call(place, pieces, width, expert_count):
    n_ctx, rows, share = pieces[0].shape
    count = len(pieces) * n_ctx
    part = rows - PAD

    def kernel(place_ref, *refs):
        ins, refs = refs[: len(pieces)], refs[len(pieces) :]
        qkv_ref, proj_ref, router_ref = refs[:3]
        vec_refs, (hold, extra) = refs[3:10], refs[10:]
        for q in range(count):
            piece = (place_ref[2] ^ (q // n_ctx)) * n_ctx + (place_ref[0] ^ (q % n_ctx))
            hold[piece] = ins[q // n_ctx][q % n_ctx].astype(F32)
        for p in range(count):
            block = hold[p, :part, :].T
            if p * part < 3 * width:
                qkv_ref[:, p * part : (p + 1) * part] = block
            else:
                proj_ref[:, p * part - 3 * width : (p + 1) * part - 3 * width] = block
            extra[p * PAD : (p + 1) * PAD, :] = hold[p, part:, :]
        cols = extra[...].T
        router_ref[...] = cols[:, PAD : PAD + expert_count]
        for s in range(4):
            vec_refs[s][...] = extra[s : s + 1, :]
        for s in range(3):
            vec_refs[4 + s][...] = extra[PAD + expert_count + s : PAD + expert_count + s + 1, :]

    return pl.pallas_call(
        kernel,
        in_specs=[SMEM_SPEC] + [VMEM_SPEC] * len(pieces),
        out_specs=[VMEM_SPEC] * 10,
        out_shape=[shape((share, 3 * width), F32), shape((share, width), F32), shape((share, expert_count), F32)]
        + [shape((1, share), F32)] * 7,
        scratch_shapes=[pltpu.VMEM((count, rows, share), F32), pltpu.VMEM((count * PAD, share), F32)],
        compiler_params=params(58),
        cost_estimate=takes(3),
        name="shared_grads",
    )(place, *pieces)


def swap(x, axis, d, size, what="sums"):
    with jax.named_scope(f"{what}_{axis}_{d}"):
        return lax.ppermute(x, axis, [(i, i ^ d) for i in range(size)])


def exchange(x, axis, what):
    with jax.named_scope(what):
        return lax.all_to_all(x, axis, split_axis=0, concat_axis=0, tiled=True)


def pick(x, i):
    return lax.dynamic_index_in_dim(x, i, 0, keepdims=False)


class Order:
    def __init__(self):
        self.seen = []

    def after(self, x, *others):
        x, others = lax.optimization_barrier((x, others))
        self.seen += others
        return x


def add_all(parts):
    acc = parts[0].astype(F32)
    for p in parts[1:]:
        acc = acc + p.astype(F32)
    return acc.astype(BF16)


def reduce_core(stay, go, n_dp, what):
    came = swap(go, "dp", 1, n_dp, what)
    return [add_all([stay[g], came[g]]) for g in range(stay.shape[0])]


def reduce_ctx(parts, n_ctx, what):
    return [parts[0]] + [swap(parts[d], "ctx", d, n_ctx, what) for d in range(1, n_ctx)]


def local(
    mesh_sizes,
    tokens,
    cotangent,
    key_mask,
    route_ids,
    priority,
    norm1_gain,
    norm1_bias,
    qkv_weight,
    query_bias,
    value_bias,
    proj_weight,
    proj_bias,
    norm2_gain,
    norm2_bias,
    router_weight,
    expert_up,
    expert_up_bias,
    expert_down,
    expert_down_bias,
):
    n_expert, n_ctx, n_dp = mesh_sizes
    order = Order()
    images_all, rows, width = tokens.shape
    tok = images_all * rows
    images = images_all // n_ctx
    body = images * rows
    expert_count = router_weight.shape[1]
    capacity = max(2, 2 * tok // expert_count)
    ctx, expert, core = (lax.axis_index(a) for a in ("ctx", "expert", "dp"))
    place = jnp.stack([ctx, expert, core]).astype(I32)

    mine = pieces_call(
        place, tokens.reshape(n_ctx, body, width), key_mask.reshape(n_ctx, images, rows)
    )
    pieces = [mine[0]] + [swap(mine[d], "ctx", d, n_ctx, "tokens") for d in range(1, n_ctx)]

    token_of = jnp.arange(tok, dtype=I32).reshape(n_ctx, body)
    ints4 = jnp.stack(
        [
            route_ids[..., 0].reshape(n_ctx, body),
            route_ids[..., 1].reshape(n_ctx, body),
            priority.reshape(n_ctx, body) * tok + token_of,
        ],
        axis=1,
    )
    ints = jnp.concatenate([pick(ints4, ctx ^ d) for d in range(n_ctx)], axis=1)
    ints = jnp.pad(ints, ((0, 5), (0, 0)))
    cot4 = cotangent.reshape(n_ctx, body, width)
    dest_rows, dest_cols, u_send, u_own = route_call(place, ints, cot4, expert_count, capacity)
    u_came = exchange(u_send, "expert", "upstream")

    row = lambda v: v.reshape(1, -1)
    att = attend_call(
        pieces, row(norm1_gain), row(norm1_bias), qkv_weight, row(query_bias), row(value_bias), images, rows,
        dest_rows,
    )
    att_out, saved = att[:n_ctx], att[n_ctx:]
    attended = [att_out[0]] + [swap(att_out[d], "ctx", d, n_ctx, "attended") for d in range(1, n_ctx)]

    mid, normed2, *x_send = middle_call(
        place, attended, mine, proj_weight, row(proj_bias), row(norm2_gain), row(norm2_bias), dest_rows,
        expert_count, capacity,
    )

    router = jnp.pad(router_weight, ((0, 0), (0, LANES - expert_count)))
    held, gxs = None, []
    xs = [x_send[0]] + [swap(x_send[d], "expert", d, n_expert, "rows") for d in range(1, n_expert)]
    group = max(1, n_expert // EXPERT_CALLS)
    for first in range(0, n_expert, group):
        res = expert_call(
            place, xs[first : first + group], u_own if first + group == 1 else u_came, first, router, expert_up[0],
            expert_up_bias, expert_down[0], expert_down_bias, held, expert_count,
            gxs[1:2] if first + group == n_expert else [],
        )
        gxs += [
            g if first + b == 0 else swap(g, "expert", first + b, n_expert, "rows_grad")
            for b, g in enumerate(res[4:])
        ]
        held = res[:4]
    results, *held = held
    stay, go = weights_call(place, xs, *held, n_ctx, n_dp)
    came = swap(order.after(go, gxs[2]), "dp", 1, n_dp, "expert_terms")
    gxs[0] = order.after(gxs[0], stay)
    grad_mid, *rest = middle_back_call(
        place, gxs, mid, normed2, cot4, dest_cols, attended, router, row(norm2_gain), proj_weight, expert_count,
        [],
    )
    ga_send, shared = rest[:n_ctx], rest[n_ctx]
    gas = [ga_send[0]] + [swap(ga_send[d], "ctx", d, n_ctx, "attended_grad") for d in range(1, n_ctx)]
    results = order.after(results, ga_send[0])
    came = order.after(came, ga_send[0])
    terms = [add_all([stay[g], came[g]]) for g in range(n_ctx)]
    gas[0] = order.after(gas[0], *terms)
    terms = reduce_ctx(order.after(terms, *gas), n_ctx, "expert_terms")
    block_out = output_call(place, exchange(results, "expert", "results"), mid, dest_cols, n_ctx)

    gin_send, flat_stay, flat_go = attend_back_call(
        place, pieces, gas, saved, shared, row(norm1_gain), row(norm1_bias), qkv_weight, images, rows, n_dp, [],
    )
    terms, flat_go = lax.optimization_barrier((terms, flat_go))
    sums = add_all(terms)
    own = [sums] + [swap(sums, "ctx", d, n_ctx, "expert_sums") for d in range(1, n_ctx - 1)]
    flat = reduce_ctx(reduce_core(flat_stay, flat_go, n_dp, "shared"), n_ctx, "shared")

    share = width // n_expert
    flat = order.after(flat, *own[1:])
    own.append(swap(order.after(sums, flat[1]), "ctx", n_ctx - 1, n_ctx, "expert_sums"))
    part = add_all(flat)
    gin_send = order.after(gin_send, part)
    cut = [lax.dynamic_slice_in_dim(part, (expert ^ d) * share, share, 1) for d in range(n_expert)]
    part = add_all([cut[0]] + [swap(cut[d], "expert", d, n_expert, "shared") for d in range(1, n_expert)])
    gins = exchange(gin_send, "ctx", "input_grad")
    part = order.after(part, block_out)
    part = jnp.stack(reduce_ctx([part] * n_ctx, n_ctx, "shared_sums"))
    every = [part, swap(part, "dp", 1, n_dp, "shared_sums")]
    own = order.after(jnp.stack(own), part)
    hidden_width = expert_up.shape[2]
    other = swap(own, "dp", 1, n_dp, "expert_sums")
    half = expert_grads_call(place, own, 0, hidden_width, None)
    grad_up, grad_down, grad_up_bias, grad_down_bias = expert_grads_call(place, other, 1, hidden_width, half)
    input_grad = input_call(place, grad_mid, gins, order.seen)
    grad_qkv, grad_proj, grad_router, *vectors = shared_grads_call(place, every, width, expert_count)
    g1_gain, g1_bias, g_query_bias, g_value_bias, g2_gain, g2_bias, g_proj_bias = (
        v.reshape(share) for v in vectors
    )
    return (
        block_out.reshape(tokens.shape),
        input_grad.reshape(tokens.shape),
        g1_gain,
        g1_bias,
        grad_qkv,
        g_query_bias,
        g_value_bias,
        grad_proj,
        g_proj_bias,
        g2_gain,
        g2_bias,
        grad_router,
        grad_up[None],
        grad_up_bias,
        grad_down[None],
        grad_down_bias,
    )


def solution(mesh):
    images = P(("expert", "dp"), "ctx", None)
    ints = P(("expert", "dp"), "ctx")
    placed = (images, images, ints, images, ints) + (P(),) * 10 + (
        P("expert", None, None),
        P("expert", None),
        P("expert", None, None),
        P("expert", None),
    )
    sizes = tuple(mesh.shape[a] for a in ("expert", "ctx", "dp"))

    def run(*args):
        return local(sizes, *args)

    return jax.shard_map(
        run,
        mesh=mesh,
        in_specs=placed,
        out_specs=(
            images,
            images,
            P("expert"),
            P("expert"),
            P("expert", None),
            P("expert"),
            P("expert"),
            P("expert", None),
            P("expert"),
            P("expert"),
            P("expert"),
            P("expert", None),
            P("expert", None, None),
            P("expert", None),
            P("expert", None, None),
            P("expert", None),
        ),
        check_vma=False,
    )
```

time: 290 us -> 257 us (0.89)
  waiting for transfers between devices: 68.7 us -> 52.4 us
  local copies, waits for them, and re-layouts: 20.6 us -> 12.3 us
  Pallas kernels: 129 us -> 125 us
  other arithmetic: 9.47 us -> 6.15 us
    ppermute x36 -> x34, waiting for transfers between devices: 68.2 us -> 51 us  [swap(): return lax.ppermute(x, axis, [(i, i ^ d) for i in range(size)])]
    pallas_call x2 -> x4, Pallas kernels: 5.11 us -> 21.2 us  [the longest x1 14 us: weights_call(): pl.pallas_call(kernel, grid=(steps,), in_specs=[SMEM_SPEC] + [full(a) for...]
    pallas_call x4, Pallas kernels: 57.8 us -> 43.2 us  [expert_call(): pl.pallas_call(kernel, grid_spec=pltpu.PrefetchScalarGridSpec(num_scalar_...]
    ppermute x7 -> x0, starting transfers between devices: 6.92 us -> none  [named_permute(): return lax.ppermute(x, axes, pairs)]
    all_to_all x2 -> x3, starting transfers between devices: 9.95 us -> 15.4 us  [exchange(): return lax.all_to_all(x, axis, split_axis=0, concat_axis=0, tiled=True)]
    pallas_call x1, Pallas kernels: 20.1 us -> 16.6 us  [attend_back_call(): pl.pallas_call(kernel, grid=(images,), in_specs=[SMEM_SPEC] + [full(a) fo...]
    pallas_call x1, Pallas kernels: 12.8 us -> 9.78 us  [attend_call(): pl.pallas_call(kernel, grid=(images,), in_specs=[full(a) for a in ins] +...]
    convert_element_type x5, other arithmetic: 6.86 us -> 3.9 us  [add_all(): return acc.astype(BF16)]
  transfers between devices with their start and end apart: 45 -> 37, of which waited for: 15 -> 16; matrix products, arithmetic and copies ran while one was open for 5% -> 3% of each run, Pallas kernels for 38% -> 46%
where the time goes in v1:
time: 257 us; the launch traced here: 256 us
  Pallas kernels  125 us (49%)
  starting transfers between devices  58.1 us (23%)
  waiting for transfers between devices  52.4 us (20%)
  local copies, waits for them, and re-layouts  12.3 us (5%)
  other arithmetic  6.15 us (2%)
    ppermute x34, waiting for transfers between devices, swap(): return lax.ppermute(x, axis, [(i, i ^ d) for i in range(size)])  51 us
    pallas_call x4, Pallas kernels, expert_call(): pl.pallas_call(kernel, grid_spec=pltpu.PrefetchScalarGridSpec(num_scalar_...  43.2 us
    ppermute x34, starting transfers between devices, swap(): return lax.ppermute(x, axis, [(i, i ^ d) for i in range(size)])  42.7 us
    pallas_call x1, Pallas kernels, attend_back_call(): pl.pallas_call(kernel, grid=(images,), in_specs=[SMEM_SPEC] + [full(a) fo...  16.6 us
    all_to_all x3, starting transfers between devices, exchange(): return lax.all_to_all(x, axis, split_axis=0, concat_axis=0, tiled=True)  15.4 us
    pallas_call x1, Pallas kernels, weights_call(): pl.pallas_call(kernel, grid=(steps,), in_specs=[SMEM_SPEC] + [full(a) for...  14 us
    pallas_call x1, Pallas kernels, middle_back_call(): pl.pallas_call(kernel, in_specs=[SMEM_SPEC] + [VMEM_SPEC] * len(ins) + [A...  11.3 us
    pallas_call x2, Pallas kernels, expert_grads_call(): pl.pallas_call(kernel, grid_spec=pltpu.PrefetchScalarGridSpec(num_scalar_...  9.86 us
  transfers between devices with their start and end apart: 37, of which 16 were waited for; matrix products, arithmetic and copies ran while one was open for 3% of the time, Pallas kernels for 46%

profile of v1, /device:TPU:0, one launch (start us, length us, event | category | flops | bytes accessed | tf_op | source)
XLA Modules:
  0.0 255.5 jit_solution(12072098217154607610)
XLA Ops:
  2.6 2.1 pieces.1
  4.7 2.9 %collective-permute-start = (bf16[208,512]{1,0:T(8,128)(2,1)}, bf16[208,512]{1,0:T(8,128)(2,1)S(1)}, u32[]{:S(2)}, u32[]{:S(2)}) collective-permute-start(bf16[208,512]{1,0:T(8,128)(2,1)} %get-tuple-element.128.refs_5_), channel_id=1, source_target_pairs={{0,2},{2,0},{4,6},{6,4},{1,3},{3,1},{5,7},{7,5},{8,10},{10,8},{12,... | collective-permute-start | bytes 638984 | tf_op jit(solution)/shard_map/tokens_ctx_1/ppermute | solution.py:853
  7.7 1.5 collective-permute-start.1
  10.2 4.5 %route.1 = (s32[8,768]{1,0:T(8,128)}, s32[768,8]{1,0:T(8,128)}, bf16[4,384,512]{2,1,0:T(8,128)(2,1)}, bf16[1,384,512]{2,1,0:T(8,128)(2,1)}) custom-call(s32[3]{0:T(128)} %pad_add_fusion.2.place_ref, s32[8,768]{1,0:T(8,128)} %pad.8.ints_ref, bf16[4,192,512]{2,1,0:T(8,128)(2,1)} %bitcast.74), custom_call_target="tpu_custom_call" | custom-call | flops 4600000000 | bytes 131072 | tf_op jit(solution)/shard_map/route/pallas_call | solution.py:146
  14.7 5.3 %all-to-all-start = ((bf16[4,384,512]{2,1,0:T(8,128)(2,1)}), bf16[4,384,512]{2,1,0:T(8,128)(2,1)S(1)}, u32[]{:S(2)}, u32[]{:S(2)}) async-start(bf16[4,384,512]{2,1,0:T(8,128)(2,1)} %get-tuple-element.137), calls=%async_computation | async-start | bytes 3145728 | tf_op jit(solution)/shard_map/upstream/all_to_all | solution.py:858
  20.9 9.8 %attend.1 = (bf16[192,512]{1,0:T(8,128)(2,1)}, bf16[192,512]{1,0:T(8,128)(2,1)}, bf16[192,512]{1,0:T(8,128)(2,1)}, bf16[192,512]{1,0:T(8,128)(2,1)}, bf16[3,512,...) custom-call(bf16[208,512]{1,0:T(8,128)(2,1)} %get-tuple-element.127.refs_, ...), custom_call_target="tpu_custom_call" | custom-call | flops 13799999488 | bytes 131072 | tf_op jit(solution)/shard_map/attend/pallas_call | solution.py:232
  30.7 1.5 collective-permute-start.3
  32.2 1.5 collective-permute-start.4
  35.1 3.5 %collective-permute-done.3.refs_1_.refs_9_ = bf16[192,512]{1,0:T(8,128)(2,1)S(1)} collective-permute-done((bf16[192,512]{1,0:T(8,128)(2,1)}, bf16[192,512]{1,0:T(8,128)(2,1)S(1)}, u32[]{:S(2)}, u32[]{:S(2)}) %collective-permute-start.3) | collective-permute-done | bytes 196640 | tf_op jit(solution)/shard_map/attended_ctx_1/ppermute | solution.py:853
  38.6 3.5 %collective-permute-done.4.refs_2_.refs_10_ = bf16[192,512]{1,0:T(8,128)(2,1)S(1)} collective-permute-done((bf16[192,512]{1,0:T(8,128)(2,1)}, bf16[192,512]{1,0:T(8,128)(2,1)S(1)}, u32[]{:S(2)}, u32[]{:S(2)}) %collective-permute-start.4) | collective-permute-done | bytes 196640 | tf_op jit(solution)/shard_map/attended_ctx_2/ppermute | solution.py:853
  42.9 4.7 %middle.1 = (f32[768,512]{1,0:T(8,128)}, bf16[768,512]{1,0:T(8,128)(2,1)}, bf16[384,512]{1,0:T(8,128)(2,1)}, bf16[384,512]{1,0:T(8,128)(2,1)}, bf16[384,512]{1,0:T(8,128)(2,1)}, /*index=5*/bf16[384,512]{1,0:T(8,128)(2,1)}) custom-call(s32[3]{0:T(128)} %pad_add_fusion.2.place_ref, bf16[192,512]{1,0:T(8,128)(2,1)} %get-tuple-element.132.refs_0_.refs_8_, ...), custom_call_target="tpu_custom_call" | custom-call | flops 5750000128 | bytes 131072 | tf_op jit(solution)/shard_map/middle/pallas_call | solution.py:275
  47.6 1.8 collective-permute-start.8
  49.4 2.3 collective-permute-start.7
  52.0 10.8 %expert.4 = (bf16[4,384,512]{2,1,0:T(8,128)(2,1)}, bf16[1536,512]{1,0:T(8,128)(2,1)}, bf16[1536,2048]{1,0:T(8,128)(2,1)}, bf16[1536,2048]{1,0:T(8,128)(2,1)}, bf16[400,512]{1,0:T(8,128)(2,1)}) custom-call(s32[3]{0:T(128)} %pad_add_fusion.2.place_ref, bf16[384,512]{1,0:T(8,128)(2,1)} %get-tuple-element.140.refs_0_, ...), custom_call_target="tpu_custom_call" | custom-call | flops 10350000128 | bytes 131072 | tf_op jit(solution)/shard_map/expert/pallas_call | solution.py:375
  62.7 6.3 %collective-permute-done.8.refs_0_.refs_1_ = bf16[384,512]{1,0:T(8,128)(2,1)S(1)} collective-permute-done((bf16[384,512]{1,0:T(8,128)(2,1)}, bf16[384,512]{1,0:T(8,128)(2,1)S(1)}, u32[]{:S(2)}, u32[]{:S(2)}) %collective-permute-start.8) | collective-permute-done | bytes 393248 | tf_op jit(solution)/shard_map/rows_expert_1/ppermute | solution.py:853
  70.3 10.7 %expert.5 = (bf16[4,384,512]{2,1,0:T(8,128)(2,1)}, bf16[1536,512]{1,0:T(8,128)(2,1)}, bf16[1536,2048]{1,0:T(8,128)(2,1)}, bf16[1536,2048]{1,0:T(8,128)(2,1)}, bf16[400,512]{1,0:T(8,128)(2,1)}) custom-call(s32[3]{0:T(128)} %pad_add_fusion.2.place_ref, ...), custom_call_target="tpu_custom_call", output_to_operand_aliasing={{0}: (8, {}), {1}: (9, {}), {2}: (10, {}), {3}: (11, {})} | custom-call | flops 10350000128 | bytes 131072 | tf_op jit(solution)/shard_map/expert/pallas_call | solution.py:375
  81.1 1.5 collective-permute-done.7.refs_0_.refs_2_
  83.3 10.7 %expert.6 = (bf16[4,384,512]{2,1,0:T(8,128)(2,1)}, bf16[1536,512]{1,0:T(8,128)(2,1)}, bf16[1536,2048]{1,0:T(8,128)(2,1)}, bf16[1536,2048]{1,0:T(8,128)(2,1)}, bf16[400,512]{1,0:T(8,128)(2,1)}) custom-call(s32[3]{0:T(128)} %pad_add_fusion.2.place_ref, ...), custom_call_target="tpu_custom_call", output_to_operand_aliasing={{0}: (8, {}), {1}: (9, {}), {2}: (10, {}), {3}: (11, {})} | custom-call | flops 10350000128 | bytes 131072 | tf_op jit(solution)/shard_map/expert/pallas_call | solution.py:375
  94.1 6.9 %collective-permute-start.10 = (bf16[400,512]{1,0:T(8,128)(2,1)}, bf16[400,512]{1,0:T(8,128)(2,1)S(1)}, u32[]{:S(2)}, u32[]{:S(2)}) collective-permute-start(bf16[400,512]{1,0:T(8,128)(2,1)} %get-tuple-element.162), channel_id=1, source_target_pairs={{0,16},{8,24},{16,0},{24,8},{1,17},{9,25},{17,1},{25,9},{2,18},{10... | collective-permute-start | bytes 1228808 | tf_op jit(solution)/shard_map/rows_grad_expert_2/ppermute | solution.py:853
  101.8 11.0 %expert.7 = (bf16[4,384,512]{2,1,0:T(8,128)(2,1)}, bf16[1536,512]{1,0:T(8,128)(2,1)}, bf16[1536,2048]{1,0:T(8,128)(2,1)}, bf16[1536,2048]{1,0:T(8,128)(2,1)}, bf16[400,512]{1,0:T(8,128)(2,1)}) custom-call(s32[3]{0:T(128)} %pad_add_fusion.2.place_ref, ...), custom_call_target="tpu_custom_call", output_to_operand_aliasing={{0}: (8, {}), {1}: (9, {}), {2}: (10, {}), {3}: (11, {})} | custom-call | flops 10350000128 | bytes 131072 | tf_op jit(solution)/shard_map/expert/pallas_call | solution.py:375
  112.8 14.0 %weights.1 = (bf16[4,528,512]{2,1,0:T(8,128)(2,1)}, bf16[4,528,512]{2,1,0:T(8,128)(2,1)}) custom-call(s32[3]{0:T(128)} %pad_add_fusion.2.place_ref, bf16[384,512]{1,0:T(8,128)(2,1)} %get-tuple-element.140.refs_0_, bf16[384,512]{1,0:T(8,128)(2,1)} %copy-done.21, bf16[384,512]{1,0:T(8,128)(2,1)} %copy-done.22, ...), custom_call_target="tpu_custom_call" | custom-call | flops 14949999616 | bytes 131072 | tf_op jit(solution)/shard_map/weights/pallas_call | solution.py:461
  127.8 11.3 %middle_back.1 = (f32[768,512]{1,0:T(8,128)}, bf16[192,512]{1,0:T(8,128)(2,1)}, bf16[192,512]{1,0:T(8,128)(2,1)}, bf16[192,512]{1,0:T(8,128)(2,1)}, bf16[192,512]{1,0:T(8,128)(2,1)}, /*index=5*/bf16[528,512]{1,0:T(8,128)(2,1)}) custom-call(s32[3]{0:T(128)} %pad_add_fusion.2.place_ref, bf16[400,512]{1,0:T(8,128)(2,1)} %get-tuple-element.161.refs_0_, ...), custom_call_target="tpu_custom_call" | custom-call | flops 34500001792 | bytes 131072 | tf_op jit(solution)/shard_map/middle_back/pallas_call | solution.py:570
  139.0 1.5 collective-permute-start.13
  140.5 2.5 collective-permute-start.14
  143.1 6.6 %all-to-all-start.1 = ((bf16[4,384,512]{2,1,0:T(8,128)(2,1)}), bf16[4,384,512]{2,1,0:T(8,128)(2,1)}, u32[]{:S(2)}, u32[]{:S(2)}) async-start(bf16[4,384,512]{2,1,0:T(8,128)(2,1)} %get-tuple-element.168), calls=%async_computation.1 | async-start | bytes 3145728 | tf_op jit(solution)/shard_map/results/all_to_all | solution.py:858
  149.7 2.1 fusion.3
  152.8 1.5 collective-permute-start.16
  156.3 16.6 %attend_back.1 = (bf16[4,192,512]{2,1,0:T(8,128)(2,1)}, bf16[4,272,512]{2,1,0:T(8,128)(2,1)}, bf16[4,272,512]{2,1,0:T(8,128)(2,1)}) custom-call(s32[3]{0:T(128)} %pad_add_fusion.2.place_ref, bf16[208,512]{1,0:T(8,128)(2,1)} %get-tuple-element.127.refs_0_.refs_4_, bf16[208,512]{1,0:T(8,128)(2,1)} %copy-done.24, bf16[208,512]{1,0:T(8,128)(2,1)} %copy-done.25, ...), custom_call_target="tpu_custom_call" | custom-call | flops 23000000512 | bytes 131072 | tf_op jit(solution)/shard_map/attend_back/pallas_call | solution.py:699
  173.0 6.5 %collective-permute-done.17 = bf16[528,512]{1,0:T(8,128)(2,1)S(1)} collective-permute-done((bf16[528,512]{1,0:T(8,128)(2,1)S(1)}, bf16[528,512]{1,0:T(8,128)(2,1)S(1)}, u32[]{:S(2)}, u32[]{:S(2)}) %collective-permute-start.17) | collective-permute-done | bytes 540704 | tf_op jit(solution)/shard_map/expert_terms_ctx_2/ppermute | solution.py:853
  180.4 1.4 collective-permute-start.24
  183.4 1.4 collective-permute-start.21
  184.8 1.5 collective-permute-start.22
  186.3 8.6 %collective-permute-done.23.refs_12_ = bf16[528,512]{1,0:T(8,128)(2,1)S(1)} collective-permute-done((bf16[528,512]{1,0:T(8,128)(2,1)S(1)}, bf16[528,512]{1,0:T(8,128)(2,1)S(1)}, u32[]{:S(2)}, u32[]{:S(2)}) %collective-permute-start.23) | collective-permute-done | bytes 540704 | tf_op jit(solution)/shard_map/expert_sums_ctx_1/ppermute | solution.py:853
  195.5 5.4 %collective-permute-done.20.refs_14_ = bf16[272,512]{1,0:T(8,128)(2,1)S(1)} collective-permute-done((bf16[272,512]{1,0:T(8,128)(2,1)S(1)}, bf16[272,512]{1,0:T(8,128)(2,1)S(1)}, u32[]{:S(2)}, u32[]{:S(2)}) %collective-permute-start.20) | collective-permute-done | bytes 278560 | tf_op jit(solution)/shard_map/shared_ctx_1/ppermute | solution.py:853
  200.8 5.8 %collective-permute-done.21 = bf16[272,512]{1,0:T(8,128)(2,1)S(1)} collective-permute-done((bf16[272,512]{1,0:T(8,128)(2,1)S(1)}, bf16[272,512]{1,0:T(8,128)(2,1)S(1)}, u32[]{:S(2)}, u32[]{:S(2)}) %collective-permute-start.21) | collective-permute-done | bytes 278560 | tf_op jit(solution)/shard_map/shared_ctx_2/ppermute | solution.py:853
  207.9 3.4 %collective-permute-start.26 = (bf16[272,128]{1,0:T(8,128)(2,1)S(1)}, bf16[272,128]{1,0:T(8,128)(2,1)S(1)}, u32[]{:S(2)}, u32[]{:S(2)}) collective-permute-start(bf16[272,128]{1,0:T(8,128)(2,1)S(1)} %get-tuple-element.282), channel_id=1, source_target_pairs={{0,16},{8,24},{16,0},{24,8},{1,17},{9,25},{17,1},{25,9},{2,18},{10... | collective-permute-start | bytes 208904 | tf_op jit(solution)/shard_map/shared_expert_2/ppermute | solution.py:853
  212.3 1.4 collective-permute-start.28
  213.7 4.3 %output.1.refs_16_ = bf16[4,192,512]{2,1,0:T(8,128)(2,1)} custom-call(s32[3]{0:T(128)} %pad_add_fusion.2.place_ref, bf16[4,384,512]{2,1,0:T(8,128)(2,1)} %all-to-all-done.1.o_ref, f32[768,512]{1,0:T(8,128)} %get-tuple-element.164.refs_4_.mid_ref, s32[768,8]{1,0:T(8,128)} %get-tuple-element.166.refs_7_.dest_ref), custom_call_target="tpu_custom_call" | custom-call | flops 34500001792 | bytes 131072 | tf_op jit(solution)/shard_map/output/pallas_call | solution.py:498
  218.1 1.5 collective-permute-start.29
  221.7 6.8 %collective-permute-done.29 = bf16[272,128]{1,0:T(8,128)(2,1)S(1)} collective-permute-done((bf16[272,128]{1,0:T(8,128)(2,1)S(1)}, bf16[272,128]{1,0:T(8,128)(2,1)S(1)}, u32[]{:S(2)}, u32[]{:S(2)}) %collective-permute-start.29) | collective-permute-done | bytes 69664 | tf_op jit(solution)/shard_map/shared_sums_ctx_1/ppermute | solution.py:853
  230.0 1.5 pad_maximum_fusion.ref
  232.1 3.5 %all-to-all-start.2 = ((bf16[4,192,512]{2,1,0:T(8,128)(2,1)}), bf16[4,192,512]{2,1,0:T(8,128)(2,1)S(1)}, u32[]{:S(2)}, u32[]{:S(2)}) async-start(bf16[4,192,512]{2,1,0:T(8,128)(2,1)} %get-tuple-element.198), calls=%async_computation.2 | async-start | bytes 1572864 | tf_op jit(solution)/shard_map/input_grad/all_to_all | solution.py:858
  236.6 2.4 shared_grads.1
  239.0 1.5 copy.55
  240.5 4.9 %expert_grads.2 = (f32[512,2048]{1,0:T(8,128)}, f32[2048,512]{1,0:T(8,128)}, f32[1,2048]{1,0:T(1,128)}, f32[1,512]{1,0:T(1,128)}) custom-call(s32[3]{0:T(128)} %pad_add_fusion.2.place_ref, bf16[4,528,512]{2,1,0:T(8,128)(2,1)} %copy-done.2), custom_call_target="tpu_custom_call" | custom-call | flops 3449999872 | bytes 131072 | tf_op jit(solution)/shard_map/expert_grads/pallas_call | solution.py:783
  245.4 1.5 all-to-all-done.2.gin_ref
  247.8 2.6 %input.1 = bf16[4,192,512]{2,1,0:T(8,128)(2,1)} custom-call(s32[3]{0:T(128)} %pad_add_fusion.2.place_ref, f32[768,512]{1,0:T(8,128)} %get-tuple-element.169.gmid_ref, bf16[4,192,512]{2,1,0:T(8,128)(2,1)} %copy-done.6, bf16[400,512]{1,0:T(8,128)(2,1)} %copy-done.18, bf16[4,528,512]{2,1,0:T(8,128)(2,1)} %get-tuple-element.200.refs_1_, ...), custom_call_target="tpu_custom_call" | custom-call | flops 3449999872 | bytes 131072 | tf_op jit(solution)/shard_map/input/pallas_call | solution.py:734
  250.4 4.9 %expert_grads.3 = (f32[512,2048]{1,0:T(8,128)}, f32[2048,512]{1,0:T(8,128)}, f32[1,2048]{1,0:T(1,128)}, f32[1,512]{1,0:T(1,128)}) custom-call(s32[3]{0:T(128)} %pad_add_fusion.2.place_ref, bf16[4,528,512]{2,1,0:T(8,128)(2,1)} %collective-permute-done.33.ref, f32[512,2048]{1,0:T(8,128)} %get-tuple-element.230.refs_0_, ...), custom_call_target="tpu_custom_call", output_to_operand_aliasing={{0}: (2, {}), {1}: (3, {})} | custom-call | flops 3449999872 | bytes 131072 | tf_op jit(solution)/shard_map/expert_grads/pallas_call | solution.py:783
  (129 shorter events, 24.3 us)
Async XLA Ops:
  4.7 15.4 %collective-permute-start = (bf16[208,512]{1,0:T(8,128)(2,1)}, bf16[208,512]{1,0:T(8,128)(2,1)S(1)}, u32[]{:S(2)}, u32[]{:S(2)}) collective-permute-start(bf16[208,512]{1,0:T(8,128)(2,1)} %get-tuple-element.128.refs_5_), channel_id=1, source_target_pairs={{0,2},{2,0},{4,6},{6,4},{1,3},{3,1},{5,7},{7,5},{8,10},{10,8},{12,... | collective-permute-start | bytes 638984 | tf_op jit(solution)/shard_map/tokens_ctx_1/ppermute | solution.py:853
  7.7 12.4 %collective-permute-start.1 = (bf16[208,512]{1,0:T(8,128)(2,1)}, bf16[208,512]{1,0:T(8,128)(2,1)S(1)}, u32[]{:S(2)}, u32[]{:S(2)}) collective-permute-start(bf16[208,512]{1,0:T(8,128)(2,1)} %get-tuple-element.129.refs_6_), channel_id=1, source_target_pairs={{0,4},{2,6},{4,0},{6,2},{1,5},{3,7},{5,1},{7,3},{8,12},{10,14},{12... | collective-permute-start | bytes 638984 | tf_op jit(solution)/shard_map/tokens_ctx_2/ppermute | solution.py:853
  9.2 10.9 %collective-permute-start.2 = (bf16[208,512]{1,0:T(8,128)(2,1)}, bf16[208,512]{1,0:T(8,128)(2,1)S(1)}, u32[]{:S(2)}, u32[]{:S(2)}) collective-permute-start(bf16[208,512]{1,0:T(8,128)(2,1)} %get-tuple-element.130.refs_7_), channel_id=1, source_target_pairs={{0,6},{2,4},{4,2},{6,0},{1,7},{3,5},{5,3},{7,1},{8,14},{10,12},{12... | collective-permute-start | bytes 638984 | tf_op jit(solution)/shard_map/tokens_ctx_3/ppermute | solution.py:853
  14.7 54.3 %all-to-all-start = ((bf16[4,384,512]{2,1,0:T(8,128)(2,1)}), bf16[4,384,512]{2,1,0:T(8,128)(2,1)S(1)}, u32[]{:S(2)}, u32[]{:S(2)}) async-start(bf16[4,384,512]{2,1,0:T(8,128)(2,1)} %get-tuple-element.137), calls=%async_computation | async-start | bytes 3145728 | tf_op jit(solution)/shard_map/upstream/all_to_all | solution.py:858
  20.9 13.3 %copy-start.17 = (bf16[512,4]{0,1:T(4,128)(2,1)S(1)}, bf16[512,4]{0,1:T(4,128)(2,1)}, u32[]{:S(2)}) copy-start(bf16[512,4]{0,1:T(4,128)(2,1)} %param.33) | copy-start | bytes 12292
  30.7 7.9 %collective-permute-start.3 = (bf16[192,512]{1,0:T(8,128)(2,1)}, bf16[192,512]{1,0:T(8,128)(2,1)S(1)}, u32[]{:S(2)}, u32[]{:S(2)}) collective-permute-start(bf16[192,512]{1,0:T(8,128)(2,1)} %get-tuple-element.133), channel_id=1, source_target_pairs={{0,2},{2,0},{4,6},{6,4},{1,3},{3,1},{5,7},{7,5},{8,10},{10,8},{12,... | collective-permute-start | bytes 589832 | tf_op jit(solution)/shard_map/attended_ctx_1/ppermute | solution.py:853
  32.2 9.9 %collective-permute-start.4 = (bf16[192,512]{1,0:T(8,128)(2,1)}, bf16[192,512]{1,0:T(8,128)(2,1)S(1)}, u32[]{:S(2)}, u32[]{:S(2)}) collective-permute-start(bf16[192,512]{1,0:T(8,128)(2,1)} %get-tuple-element.134), channel_id=1, source_target_pairs={{0,4},{2,6},{4,0},{6,2},{1,5},{3,7},{5,1},{7,3},{8,12},{10,14},{12... | collective-permute-start | bytes 589832 | tf_op jit(solution)/shard_map/attended_ctx_2/ppermute | solution.py:853
  33.8 8.4 %collective-permute-start.5 = (bf16[192,512]{1,0:T(8,128)(2,1)}, bf16[192,512]{1,0:T(8,128)(2,1)S(1)}, u32[]{:S(2)}, u32[]{:S(2)}) collective-permute-start(bf16[192,512]{1,0:T(8,128)(2,1)} %get-tuple-element.135), channel_id=1, source_target_pairs={{0,6},{2,4},{4,2},{6,0},{1,7},{3,5},{5,3},{7,1},{8,14},{10,12},{12... | collective-permute-start | bytes 589832 | tf_op jit(solution)/shard_map/attended_ctx_3/ppermute | solution.py:853
  47.6 21.4 %collective-permute-start.8 = (bf16[384,512]{1,0:T(8,128)(2,1)}, bf16[384,512]{1,0:T(8,128)(2,1)S(1)}, u32[]{:S(2)}, u32[]{:S(2)}) collective-permute-start(bf16[384,512]{1,0:T(8,128)(2,1)} %get-tuple-element.139), channel_id=1, source_target_pairs={{0,8},{8,0},{16,24},{24,16},{1,9},{9,1},{17,25},{25,17},{2,10},{10... | collective-permute-start | bytes 1179656 | tf_op jit(solution)/shard_map/rows_expert_1/ppermute | solution.py:853
  49.4 33.2 %collective-permute-start.7 = (bf16[384,512]{1,0:T(8,128)(2,1)}, bf16[384,512]{1,0:T(8,128)(2,1)S(1)}, u32[]{:S(2)}, u32[]{:S(2)}) collective-permute-start(bf16[384,512]{1,0:T(8,128)(2,1)} %get-tuple-element.138), channel_id=1, source_target_pairs={{0,16},{8,24},{16,0},{24,8},{1,17},{9,25},{17,1},{25,9},{2,18},{10... | collective-permute-start | bytes 1179656 | tf_op jit(solution)/shard_map/rows_expert_2/ppermute | solution.py:853
  51.7 49.2 %collective-permute-start.6 = (bf16[384,512]{1,0:T(8,128)(2,1)}, bf16[384,512]{1,0:T(8,128)(2,1)}, u32[]{:S(2)}, u32[]{:S(2)}) collective-permute-start(bf16[384,512]{1,0:T(8,128)(2,1)} %get-tuple-element.136), channel_id=1, source_target_pairs={{0,24},{8,16},{16,8},{24,0},{1,25},{9,17},{17,9},{25,1},{2,26},{10... | collective-permute-start | bytes 1179656 | tf_op jit(solution)/shard_map/rows_expert_3/ppermute | solution.py:853
  81.0 20.0 %collective-permute-start.9 = (bf16[400,512]{1,0:T(8,128)(2,1)}, bf16[400,512]{1,0:T(8,128)(2,1)S(1)}, u32[]{:S(2)}, u32[]{:S(2)}) collective-permute-start(bf16[400,512]{1,0:T(8,128)(2,1)} %get-tuple-element.154), channel_id=1, source_target_pairs={{0,8},{8,0},{16,24},{24,16},{1,9},{9,1},{17,25},{25,17},{2,10},{10... | collective-permute-start | bytes 1228808 | tf_op jit(solution)/shard_map/rows_grad_expert_1/ppermute | solution.py:853
  94.1 32.8 %collective-permute-start.10 = (bf16[400,512]{1,0:T(8,128)(2,1)}, bf16[400,512]{1,0:T(8,128)(2,1)S(1)}, u32[]{:S(2)}, u32[]{:S(2)}) collective-permute-start(bf16[400,512]{1,0:T(8,128)(2,1)} %get-tuple-element.162), channel_id=1, source_target_pairs={{0,16},{8,24},{16,0},{24,8},{1,17},{9,25},{17,1},{25,9},{2,18},{10... | collective-permute-start | bytes 1228808 | tf_op jit(solution)/shard_map/rows_grad_expert_2/ppermute | solution.py:853
  112.7 14.2 %collective-permute-start.11 = (bf16[400,512]{1,0:T(8,128)(2,1)}, bf16[400,512]{1,0:T(8,128)(2,1)S(1)}, u32[]{:S(2)}, u32[]{:S(2)}) collective-permute-start(bf16[400,512]{1,0:T(8,128)(2,1)} %get-tuple-element.163), channel_id=1, source_target_pairs={{0,24},{8,16},{16,8},{24,0},{1,25},{9,17},{17,9},{25,1},{2,26},{10... | collective-permute-start | bytes 1228808 | tf_op jit(solution)/shard_map/rows_grad_expert_3/ppermute | solution.py:853
  126.9 22.8 %collective-permute-start.12 = (bf16[4,528,512]{2,1,0:T(8,128)(2,1)}, bf16[4,528,512]{2,1,0:T(8,128)(2,1)}, u32[]{:S(2)}, u32[]{:S(2)}) collective-permute-start(bf16[4,528,512]{2,1,0:T(8,128)(2,1)} %get-tuple-element.171), channel_id=1, source_target_pairs={{0,1},{1,0},{2,3},{3,2},{4,5},{5,4},{6,7},{7,6},{8,9},{9,8},{10,11... | collective-permute-start | bytes 6488072 | tf_op jit(solution)/shard_map/expert_terms_dp_1/ppermute | solution.py:853
  139.0 12.8 %collective-permute-start.13 = (bf16[192,512]{1,0:T(8,128)(2,1)}, bf16[192,512]{1,0:T(8,128)(2,1)S(1)}, u32[]{:S(2)}, u32[]{:S(2)}) collective-permute-start(bf16[192,512]{1,0:T(8,128)(2,1)} %get-tuple-element.174), channel_id=1, source_target_pairs={{0,2},{2,0},{4,6},{6,4},{1,3},{3,1},{5,7},{7,5},{8,10},{10,8},{12,... | collective-permute-start | bytes 589832 | tf_op jit(solution)/shard_map/attended_grad_ctx_1/ppermute | solution.py:853
  140.5 11.6 %collective-permute-start.14 = (bf16[192,512]{1,0:T(8,128)(2,1)}, bf16[192,512]{1,0:T(8,128)(2,1)}, u32[]{:S(2)}, u32[]{:S(2)}) collective-permute-start(bf16[192,512]{1,0:T(8,128)(2,1)} %get-tuple-element.175), channel_id=1, source_target_pairs={{0,4},{2,6},{4,0},{6,2},{1,5},{3,7},{5,1},{7,3},{8,12},{10,14},{12... | collective-permute-start | bytes 589832 | tf_op jit(solution)/shard_map/attended_grad_ctx_2/ppermute | solution.py:853
  143.1 9.8 %collective-permute-start.15 = (bf16[192,512]{1,0:T(8,128)(2,1)}, bf16[192,512]{1,0:T(8,128)(2,1)}, u32[]{:S(2)}, u32[]{:S(2)}) collective-permute-start(bf16[192,512]{1,0:T(8,128)(2,1)} %get-tuple-element.176), channel_id=1, source_target_pairs={{0,6},{2,4},{4,2},{6,0},{1,7},{3,5},{5,3},{7,1},{8,14},{10,12},{12... | collective-permute-start | bytes 589832 | tf_op jit(solution)/shard_map/attended_grad_ctx_3/ppermute | solution.py:853
  143.1 70.7 %all-to-all-start.1 = ((bf16[4,384,512]{2,1,0:T(8,128)(2,1)}), bf16[4,384,512]{2,1,0:T(8,128)(2,1)}, u32[]{:S(2)}, u32[]{:S(2)}) async-start(bf16[4,384,512]{2,1,0:T(8,128)(2,1)} %get-tuple-element.168), calls=%async_computation.1 | async-start | bytes 3145728 | tf_op jit(solution)/shard_map/results/all_to_all | solution.py:858
  151.8 21.1 %copy-start.7 = (bf16[528,512]{1,0:T(8,128)(2,1)}, bf16[528,512]{1,0:T(8,128)(2,1)S(1)}, u32[]{:S(2)}) copy-start(bf16[528,512]{1,0:T(8,128)(2,1)S(1)} %get-tuple-element.206.refs_7_) | copy-start | bytes 1622020
  151.8 21.1 %copy-start.8 = (bf16[528,512]{1,0:T(8,128)(2,1)}, bf16[528,512]{1,0:T(8,128)(2,1)S(1)}, u32[]{:S(2)}) copy-start(bf16[528,512]{1,0:T(8,128)(2,1)S(1)} %get-tuple-element.205.refs_6_) | copy-start | bytes 1622020
  151.8 21.1 %copy-start.9 = (bf16[528,512]{1,0:T(8,128)(2,1)}, bf16[528,512]{1,0:T(8,128)(2,1)S(1)}, u32[]{:S(2)}) copy-start(bf16[528,512]{1,0:T(8,128)(2,1)S(1)} %get-tuple-element.204.refs_5_) | copy-start | bytes 1622020
  151.8 27.6 %copy-start.1 = (bf16[528,512]{1,0:T(8,128)(2,1)}, bf16[528,512]{1,0:T(8,128)(2,1)S(1)}, u32[]{:S(2)}) copy-start(bf16[528,512]{1,0:T(8,128)(2,1)S(1)} %get-tuple-element.203.refs_4_) | copy-start | bytes 1622020
  152.8 20.1 %collective-permute-start.16 = (bf16[528,512]{1,0:T(8,128)(2,1)S(1)}, bf16[528,512]{1,0:T(8,128)(2,1)S(1)}, u32[]{:S(2)}, u32[]{:S(2)}) collective-permute-start(bf16[528,512]{1,0:T(8,128)(2,1)S(1)} %get-tuple-element.204.refs_5_), channel_id=1, source_target_pairs={{0,2},{2,0},{4,6},{6,4},{1,3},{3,1},{5,7},{7,5},{8,10},{10,8},{12,... | collective-permute-start | bytes 1622024 | tf_op jit(solution)/shard_map/expert_terms_ctx_1/ppermute | solution.py:853
  154.3 25.1 %collective-permute-start.17 = (bf16[528,512]{1,0:T(8,128)(2,1)S(1)}, bf16[528,512]{1,0:T(8,128)(2,1)S(1)}, u32[]{:S(2)}, u32[]{:S(2)}) collective-permute-start(bf16[528,512]{1,0:T(8,128)(2,1)S(1)} %get-tuple-element.205.refs_6_), channel_id=1, source_target_pairs={{0,4},{2,6},{4,0},{6,2},{1,5},{3,7},{5,1},{7,3},{8,12},{10,14},{12... | collective-permute-start | bytes 1622024 | tf_op jit(solution)/shard_map/expert_terms_ctx_2/ppermute | solution.py:853
  155.1 24.3 %collective-permute-start.18 = (bf16[528,512]{1,0:T(8,128)(2,1)S(1)}, bf16[528,512]{1,0:T(8,128)(2,1)S(1)}, u32[]{:S(2)}, u32[]{:S(2)}) collective-permute-start(bf16[528,512]{1,0:T(8,128)(2,1)S(1)} %get-tuple-element.206.refs_7_), channel_id=1, source_target_pairs={{0,6},{2,4},{4,2},{6,0},{1,7},{3,5},{5,3},{7,1},{8,14},{10,12},{12... | collective-permute-start | bytes 1622024 | tf_op jit(solution)/shard_map/expert_terms_ctx_3/ppermute | solution.py:853
  172.9 9.5 %copy-start.4 = (bf16[4,272,512]{2,1,0:T(8,128)(2,1)S(1)}, bf16[4,272,512]{2,1,0:T(8,128)(2,1)}, u32[]{:S(2)}) copy-start(bf16[4,272,512]{2,1,0:T(8,128)(2,1)} %get-tuple-element.183) | copy-start | bytes 3342340
  179.4 3.0 %collective-permute-start.19 = (bf16[4,272,512]{2,1,0:T(8,128)(2,1)}, bf16[4,272,512]{2,1,0:T(8,128)(2,1)S(1)}, u32[]{:S(2)}, u32[]{:S(2)}) collective-permute-start(bf16[4,272,512]{2,1,0:T(8,128)(2,1)} %get-tuple-element.189), channel_id=1, source_target_pairs={{0,1},{1,0},{2,3},{3,2},{4,5},{5,4},{6,7},{7,6},{8,9},{9,8},{10,11... | collective-permute-start | bytes 3342344 | tf_op jit(solution)/shard_map/shared_dp_1/ppermute | solution.py:853
  179.7 15.1 %collective-permute-start.23 = (bf16[528,512]{1,0:T(8,128)(2,1)S(1)}, bf16[528,512]{1,0:T(8,128)(2,1)S(1)}, u32[]{:S(2)}, u32[]{:S(2)}) collective-permute-start(bf16[528,512]{1,0:T(8,128)(2,1)S(1)} %add_convert_fusion), channel_id=1, source_target_pairs={{0,2},{2,0},{4,6},{6,4},{1,3},{3,1},{5,7},{7,5},{8,10},{10,8},{12,... | collective-permute-start | bytes 1622024 | tf_op jit(solution)/shard_map/expert_sums_ctx_1/ppermute | solution.py:853
  180.4 15.1 %collective-permute-start.24 = (bf16[528,512]{1,0:T(8,128)(2,1)S(1)}, bf16[528,512]{1,0:T(8,128)(2,1)S(1)}, u32[]{:S(2)}, u32[]{:S(2)}) collective-permute-start(bf16[528,512]{1,0:T(8,128)(2,1)S(1)} %add_convert_fusion), channel_id=1, source_target_pairs={{0,4},{2,6},{4,0},{6,2},{1,5},{3,7},{5,1},{7,3},{8,12},{10,14},{12... | collective-permute-start | bytes 1622024 | tf_op jit(solution)/shard_map/expert_sums_ctx_2/ppermute | solution.py:853
  182.7 18.1 %collective-permute-start.20 = (bf16[272,512]{1,0:T(8,128)(2,1)S(1)}, bf16[272,512]{1,0:T(8,128)(2,1)S(1)}, u32[]{:S(2)}, u32[]{:S(2)}) collective-permute-start(bf16[272,512]{1,0:T(8,128)(2,1)S(1)} %get-tuple-element.278), channel_id=1, source_target_pairs={{0,2},{2,0},{4,6},{6,4},{1,3},{3,1},{5,7},{7,5},{8,10},{10,8},{12,... | collective-permute-start | bytes 835592 | tf_op jit(solution)/shard_map/shared_ctx_1/ppermute | solution.py:853
  183.4 23.3 %collective-permute-start.21 = (bf16[272,512]{1,0:T(8,128)(2,1)S(1)}, bf16[272,512]{1,0:T(8,128)(2,1)S(1)}, u32[]{:S(2)}, u32[]{:S(2)}) collective-permute-start(bf16[272,512]{1,0:T(8,128)(2,1)S(1)} %get-tuple-element.277), channel_id=1, source_target_pairs={{0,4},{2,6},{4,0},{6,2},{1,5},{3,7},{5,1},{7,3},{8,12},{10,14},{12... | collective-permute-start | bytes 835592 | tf_op jit(solution)/shard_map/shared_ctx_2/ppermute | solution.py:853
  184.8 21.9 %collective-permute-start.22 = (bf16[272,512]{1,0:T(8,128)(2,1)S(1)}, bf16[272,512]{1,0:T(8,128)(2,1)}, u32[]{:S(2)}, u32[]{:S(2)}) collective-permute-start(bf16[272,512]{1,0:T(8,128)(2,1)S(1)} %get-tuple-element.276), channel_id=1, source_target_pairs={{0,6},{2,4},{4,2},{6,0},{1,7},{3,5},{5,3},{7,1},{8,14},{10,12},{12... | collective-permute-start | bytes 835592 | tf_op jit(solution)/shard_map/shared_ctx_3/ppermute | solution.py:853
  194.9 35.2 %copy-start.10 = (bf16[528,512]{1,0:T(8,128)(2,1)}, bf16[528,512]{1,0:T(8,128)(2,1)S(1)}, u32[]{:S(2)}) copy-start(bf16[528,512]{1,0:T(8,128)(2,1)S(1)} %collective-permute-done.23.refs_12_) | copy-start | bytes 1622020
  195.5 22.6 %copy-start.11 = (bf16[528,512]{1,0:T(8,128)(2,1)}, bf16[528,512]{1,0:T(8,128)(2,1)S(1)}, u32[]{:S(2)}) copy-start(bf16[528,512]{1,0:T(8,128)(2,1)S(1)} %collective-permute-done.24.refs_13_) | copy-start | bytes 1622020
  200.8 17.2 %copy-start.13 = (bf16[272,512]{1,0:T(8,128)(2,1)}, bf16[272,512]{1,0:T(8,128)(2,1)S(1)}, u32[]{:S(2)}) copy-start(bf16[272,512]{1,0:T(8,128)(2,1)S(1)} %collective-permute-done.20.refs_14_) | copy-start | bytes 835588
  207.8 10.3 %copy-start.5 = (bf16[272,512]{1,0:T(8,128)(2,1)}, bf16[272,512]{1,0:T(8,128)(2,1)S(1)}, u32[]{:S(2)}) copy-start(bf16[272,512]{1,0:T(8,128)(2,1)S(1)} %add_convert_fusion.5.refs_15_) | copy-start | bytes 835588
  207.9 10.2 %collective-permute-start.25 = (bf16[272,128]{1,0:T(8,128)(2,1)S(1)}, bf16[272,128]{1,0:T(8,128)(2,1)S(1)}, u32[]{:S(2)}, u32[]{:S(2)}) collective-permute-start(bf16[272,128]{1,0:T(8,128)(2,1)S(1)} %get-tuple-element.280), channel_id=1, source_target_pairs={{0,8},{8,0},{16,24},{24,16},{1,9},{9,1},{17,25},{25,17},{2,10},{10... | collective-permute-start | bytes 208904 | tf_op jit(solution)/shard_map/shared_expert_1/ppermute | solution.py:853
  207.9 10.1 %collective-permute-start.26 = (bf16[272,128]{1,0:T(8,128)(2,1)S(1)}, bf16[272,128]{1,0:T(8,128)(2,1)S(1)}, u32[]{:S(2)}, u32[]{:S(2)}) collective-permute-start(bf16[272,128]{1,0:T(8,128)(2,1)S(1)} %get-tuple-element.282), channel_id=1, source_target_pairs={{0,16},{8,24},{16,0},{24,8},{1,17},{9,25},{17,1},{25,9},{2,18},{10... | collective-permute-start | bytes 208904 | tf_op jit(solution)/shard_map/shared_expert_2/ppermute | solution.py:853
  211.3 6.7 %collective-permute-start.27 = (bf16[272,128]{1,0:T(8,128)(2,1)S(1)}, bf16[272,128]{1,0:T(8,128)(2,1)S(1)}, u32[]{:S(2)}, u32[]{:S(2)}) collective-permute-start(bf16[272,128]{1,0:T(8,128)(2,1)S(1)} %get-tuple-element.281), channel_id=1, source_target_pairs={{0,24},{8,16},{16,8},{24,0},{1,25},{9,17},{17,9},{25,1},{2,26},{10... | collective-permute-start | bytes 208904 | tf_op jit(solution)/shard_map/shared_expert_3/ppermute | solution.py:853
  212.3 16.9 %collective-permute-start.28 = (bf16[528,512]{1,0:T(8,128)(2,1)S(1)}, bf16[528,512]{1,0:T(8,128)(2,1)S(1)}, u32[]{:S(2)}, u32[]{:S(2)}) collective-permute-start(bf16[528,512]{1,0:T(8,128)(2,1)S(1)} %add_convert_fusion), channel_id=1, source_target_pairs={{0,6},{2,4},{4,2},{6,0},{1,7},{3,5},{5,3},{7,1},{8,14},{10,12},{12... | collective-permute-start | bytes 1622024 | tf_op jit(solution)/shard_map/expert_sums_ctx_3/ppermute | solution.py:853
  218.1 10.3 %collective-permute-start.29 = (bf16[272,128]{1,0:T(8,128)(2,1)S(1)}, bf16[272,128]{1,0:T(8,128)(2,1)S(1)}, u32[]{:S(2)}, u32[]{:S(2)}) collective-permute-start(bf16[272,128]{1,0:T(8,128)(2,1)S(1)} %add_convert_fusion.10), channel_id=1, source_target_pairs={{0,2},{2,0},{4,6},{6,4},{1,3},{3,1},{5,7},{7,5},{8,10},{10,8},{12,... | collective-permute-start | bytes 208904 | tf_op jit(solution)/shard_map/shared_sums_ctx_1/ppermute | solution.py:853
  219.7 8.8 %collective-permute-start.30 = (bf16[272,128]{1,0:T(8,128)(2,1)S(1)}, bf16[272,128]{1,0:T(8,128)(2,1)S(1)}, u32[]{:S(2)}, u32[]{:S(2)}) collective-permute-start(bf16[272,128]{1,0:T(8,128)(2,1)S(1)} %add_convert_fusion.10), channel_id=1, source_target_pairs={{0,4},{2,6},{4,0},{6,2},{1,5},{3,7},{5,1},{7,3},{8,12},{10,14},{12... | collective-permute-start | bytes 208904 | tf_op jit(solution)/shard_map/shared_sums_ctx_2/ppermute | solution.py:853
  220.2 8.9 %collective-permute-start.31 = (bf16[272,128]{1,0:T(8,128)(2,1)S(1)}, bf16[272,128]{1,0:T(8,128)(2,1)S(1)}, u32[]{:S(2)}, u32[]{:S(2)}) collective-permute-start(bf16[272,128]{1,0:T(8,128)(2,1)S(1)} %add_convert_fusion.10), channel_id=1, source_target_pairs={{0,6},{2,4},{4,2},{6,0},{1,7},{3,5},{5,3},{7,1},{8,14},{10,12},{12... | collective-permute-start | bytes 208904 | tf_op jit(solution)/shard_map/shared_sums_ctx_3/ppermute | solution.py:853
  231.5 7.5 %copy-start.2 = (bf16[4,528,512]{2,1,0:T(8,128)(2,1)}, bf16[4,528,512]{2,1,0:T(8,128)(2,1)S(1)}, u32[]{:S(2)}) copy-start(bf16[4,528,512]{2,1,0:T(8,128)(2,1)S(1)} %pad_maximum_fusion.ref) | copy-start | bytes 6488068
  231.5 18.9 %collective-permute-start.33 = (bf16[4,528,512]{2,1,0:T(8,128)(2,1)S(1)}, bf16[4,528,512]{2,1,0:T(8,128)(2,1)}, u32[]{:S(2)}, u32[]{:S(2)}) collective-permute-start(bf16[4,528,512]{2,1,0:T(8,128)(2,1)S(1)} %pad_maximum_fusion.ref), channel_id=1, source_target_pairs={{0,1},{1,0},{2,3},{3,2},{4,5},{5,4},{6,7},{7,6},{8,9},{9,8},{10,11... | collective-permute-start | bytes 6488072 | tf_op jit(solution)/shard_map/expert_sums_dp_1/ppermute | solution.py:853
  231.6 4.3 %collective-permute-start.32 = (bf16[4,272,128]{2,1,0:T(8,128)(2,1)S(1)}, bf16[4,272,128]{2,1,0:T(8,128)(2,1)S(1)}, u32[]{:S(2)}, u32[]{:S(2)}) collective-permute-start(bf16[4,272,128]{2,1,0:T(8,128)(2,1)S(1)} %pad_maximum_fusion.1.refs_17_.refs_0_), channel_id=1, source_target_pairs={{0,1},{1,0},{2,3},{3,2},{4,5},{5,4},{6,7},{7,6},{8,9},{9,8},{10,11... | collective-permute-start | bytes 835592 | tf_op jit(solution)/shard_map/shared_sums_dp_1/ppermute | solution.py:853
  232.1 14.8 %all-to-all-start.2 = ((bf16[4,192,512]{2,1,0:T(8,128)(2,1)}), bf16[4,192,512]{2,1,0:T(8,128)(2,1)S(1)}, u32[]{:S(2)}, u32[]{:S(2)}) async-start(bf16[4,192,512]{2,1,0:T(8,128)(2,1)} %get-tuple-element.198), calls=%async_computation.2 | async-start | bytes 1572864 | tf_op jit(solution)/shard_map/input_grad/all_to_all | solution.py:858
  (20 other events, 45.9 us)

commit v2 on v1

--- a/solution.py
+++ b/solution.py
@@ -81,14 +81,17 @@
 
 def pieces_call(place, tokens, mask):
     groups, body, width = tokens.shape
-    images, rows = mask.shape[1:]
+    rows = mask.shape[1]
+    images = mask.shape[0] // groups
 
     def kernel(place_ref, tokens_ref, mask_ref, *outs):
         for d in range(groups):
             group = place_ref[0] ^ d
             outs[d][:body, :] = tokens_ref[group]
             outs[d][body:, :] = jnp.zeros((PAD, width), BF16)
-            live = mask_ref[group].astype(F32)
+            live = jnp.zeros((images, rows), F32)
+            for g in range(groups):
+                live = jnp.where(group == g, mask_ref[g * images : (g + 1) * images, :].astype(F32), live)
             live = jnp.concatenate([live, jnp.zeros((images, LANES - rows), F32)], axis=1)
             live = jnp.concatenate([live, jnp.zeros((PAD - images, LANES), F32)], axis=0)
             outs[d][body:, :LANES] = live.astype(BF16)
@@ -393,14 +396,14 @@
             ],
         ),
         out_shape=[
-            shape((expert_count, capacity, width), BF16),
-            shape((expert_count * capacity, width), BF16),
-            shape((expert_count * capacity, hidden_width), BF16),
-            shape((expert_count * capacity, hidden_width), BF16),
+            pltpu.HBM((expert_count, capacity, width), BF16),
+            pltpu.HBM((expert_count * capacity, width), BF16),
+            pltpu.HBM((expert_count * capacity, hidden_width), BF16),
+            pltpu.HBM((expert_count * capacity, hidden_width), BF16),
         ]
-        + [shape((capacity + PAD, width), BF16)] * blocks,
+        + [pltpu.HBM((capacity + PAD, width), BF16)] * blocks,
         input_output_aliases={} if held is None else {1 + n_own + k: k for k in range(4)},
-        compiler_params=params(58),
+        compiler_params=params(16),
         cost_estimate=takes(9),
         name="expert",
     )(place, *ins, *after)
@@ -742,17 +745,20 @@
     )(place, gmid, gins, *after)
 
 
-def expert_grads_call(place, pieces, flip, hidden_width, half):
-    n_ctx, piece_rows, width = pieces.shape
+def expert_grads_call(place, pieces, first, step, n_ctx, hidden_width, half):
+    piece_rows, width = pieces[0].shape[1:]
+    arrays = len(pieces)
+    count = sum(a.shape[0] for a in pieces)
     chunk = width
     per_step = 2 * n_ctx * chunk // hidden_width
     part = chunk // per_step
     half = [] if half is None else list(half)
 
     def piece_of(q, p):
-        return (p[2] ^ flip) * n_ctx + (p[0] ^ q)
-
-    def kernel(place_ref, ref, *refs):
+        return (p[2] ^ (first[0] + q * step[0])) * n_ctx + (p[0] ^ (first[1] + q * step[1]))
+
+    def kernel(place_ref, *refs):
+        ins, refs = refs[:arrays], refs[arrays:]
         up_ref, down_ref, up_bias_ref, down_bias_ref = refs[len(half) :]
         q = pl.program_id(0)
         piece = piece_of(q, place_ref)
@@ -763,9 +769,16 @@
                 up_bias_ref[...] = refs[2][...]
                 down_bias_ref[...] = refs[3][...]
 
-        up_ref[...] = ref[0, :part, :].astype(F32)
-        down_ref[...] = ref[0, part : 2 * part, :].astype(F32)
-        extra = ref[0, 2 * part :, :].astype(F32)
+        extra = jnp.zeros((PAD, width), F32)
+        for i, ref in enumerate(ins):
+            here = (q == i) if arrays > 1 else (q >= 0)
+
+            @pl.when(here)
+            def _():
+                up_ref[...] = ref[0, :part, :].astype(F32)
+                down_ref[...] = ref[0, part : 2 * part, :].astype(F32)
+
+            extra = jnp.where(here, ref[0, 2 * part :, :].astype(F32), extra)
 
         @pl.when(lax.rem(piece, per_step) == 0)
         def _():
@@ -784,8 +797,13 @@
         kernel,
         grid_spec=pltpu.PrefetchScalarGridSpec(
             num_scalar_prefetch=1,
-            grid=(n_ctx,),
-            in_specs=[pl.BlockSpec((1, piece_rows, width), lambda q, p: (q, 0, 0))]
+            grid=(count,),
+            in_specs=[
+                pl.BlockSpec(
+                    (1, piece_rows, width), lambda q, p: (q if arrays == 1 else 0, 0, 0)
+                )
+            ]
+            * arrays
             + ([ANY_SPEC] * 2 + biases if half else []),
             out_specs=[
                 pl.BlockSpec(
@@ -802,11 +820,11 @@
             shape((1, hidden_width), F32),
             shape((1, width), F32),
         ],
-        input_output_aliases={2: 0, 3: 1} if half else {},
+        input_output_aliases={1 + arrays: 0, 2 + arrays: 1} if half else {},
         compiler_params=params(58),
         cost_estimate=takes(3),
         name="expert_grads",
-    )(place, pieces, *half)
+    )(place, *pieces, *half)
 
 
 def shared_grads_call(place, pieces, width, expert_count):
@@ -828,8 +846,7 @@
             else:
                 proj_ref[:, p * part - 3 * width : (p + 1) * part - 3 * width] = block
             extra[p * PAD : (p + 1) * PAD, :] = hold[p, part:, :]
-        cols = extra[...].T
-        router_ref[...] = cols[:, PAD : PAD + expert_count]
+        router_ref[...] = extra[PAD : PAD + expert_count, :]
         for s in range(4):
             vec_refs[s][...] = extra[s : s + 1, :]
         for s in range(3):
@@ -839,7 +856,7 @@
         kernel,
         in_specs=[SMEM_SPEC] + [VMEM_SPEC] * len(pieces),
         out_specs=[VMEM_SPEC] * 10,
-        out_shape=[shape((share, 3 * width), F32), shape((share, width), F32), shape((share, expert_count), F32)]
+        out_shape=[shape((share, 3 * width), F32), shape((share, width), F32), shape((expert_count, share), F32)]
         + [shape((1, share), F32)] * 7,
         scratch_shapes=[pltpu.VMEM((count, rows, share), F32), pltpu.VMEM((count * PAD, share), F32)],
         compiler_params=params(58),
@@ -877,11 +894,6 @@
     for p in parts[1:]:
         acc = acc + p.astype(F32)
     return acc.astype(BF16)
-
-
-def reduce_core(stay, go, n_dp, what):
-    came = swap(go, "dp", 1, n_dp, what)
-    return [add_all([stay[g], came[g]]) for g in range(stay.shape[0])]
 
 
 def reduce_ctx(parts, n_ctx, what):
@@ -921,9 +933,7 @@
     ctx, expert, core = (lax.axis_index(a) for a in ("ctx", "expert", "dp"))
     place = jnp.stack([ctx, expert, core]).astype(I32)
 
-    mine = pieces_call(
-        place, tokens.reshape(n_ctx, body, width), key_mask.reshape(n_ctx, images, rows)
-    )
+    mine = pieces_call(place, tokens.reshape(n_ctx, body, width), key_mask)
     pieces = [mine[0]] + [swap(mine[d], "ctx", d, n_ctx, "tokens") for d in range(1, n_ctx)]
 
     token_of = jnp.arange(tok, dtype=I32).reshape(n_ctx, body)
@@ -956,8 +966,9 @@
 
     router = jnp.pad(router_weight, ((0, 0), (0, LANES - expert_count)))
     held, gxs = None, []
-    xs = [x_send[0]] + [swap(x_send[d], "expert", d, n_expert, "rows") for d in range(1, n_expert)]
     group = max(1, n_expert // EXPERT_CALLS)
+    late = n_expert - group if n_expert > group else n_expert
+    xs = [x_send[0]] + [swap(x_send[d], "expert", d, n_expert, "rows") for d in range(1, late)]
     for first in range(0, n_expert, group):
         res = expert_call(
             place, xs[first : first + group], u_own if first + group == 1 else u_came, first, router, expert_up[0],
@@ -969,6 +980,11 @@
             for b, g in enumerate(res[4:])
         ]
         held = res[:4]
+        if first == 0:
+            xs += [
+                swap(order.after(x_send[d], gxs[0]), "expert", d, n_expert, "rows")
+                for d in range(late, n_expert)
+            ]
     results, *held = held
     stay, go = weights_call(place, xs, *held, n_ctx, n_dp)
     came = swap(order.after(go, gxs[2]), "dp", 1, n_dp, "expert_terms")
@@ -984,7 +1000,7 @@
     terms = [add_all([stay[g], came[g]]) for g in range(n_ctx)]
     gas[0] = order.after(gas[0], *terms)
     terms = reduce_ctx(order.after(terms, *gas), n_ctx, "expert_terms")
-    block_out = output_call(place, exchange(results, "expert", "results"), mid, dest_cols, n_ctx)
+    results = exchange(results, "expert", "results")
 
     gin_send, flat_stay, flat_go = attend_back_call(
         place, pieces, gas, saved, shared, row(norm1_gain), row(norm1_bias), qkv_weight, images, rows, n_dp, [],
@@ -992,24 +1008,30 @@
     terms, flat_go = lax.optimization_barrier((terms, flat_go))
     sums = add_all(terms)
     own = [sums] + [swap(sums, "ctx", d, n_ctx, "expert_sums") for d in range(1, n_ctx - 1)]
-    flat = reduce_ctx(reduce_core(flat_stay, flat_go, n_dp, "shared"), n_ctx, "shared")
 
     share = width // n_expert
-    flat = order.after(flat, *own[1:])
-    own.append(swap(order.after(sums, flat[1]), "ctx", n_ctx - 1, n_ctx, "expert_sums"))
-    part = add_all(flat)
-    gin_send = order.after(gin_send, part)
-    cut = [lax.dynamic_slice_in_dim(part, (expert ^ d) * share, share, 1) for d in range(n_expert)]
-    part = add_all([cut[0]] + [swap(cut[d], "expert", d, n_expert, "shared") for d in range(1, n_expert)])
-    gins = exchange(gin_send, "ctx", "input_grad")
-    part = order.after(part, block_out)
-    part = jnp.stack(reduce_ctx([part] * n_ctx, n_ctx, "shared_sums"))
+    flat = add_all([flat_stay, swap(flat_go, "dp", 1, n_dp, "shared")])
+    cut = [lax.dynamic_slice_in_dim(flat, (expert ^ d) * share, share, 2) for d in range(n_expert)]
+    cut = [cut[0]] + [swap(cut[d], "expert", d, n_expert, "shared") for d in range(1, n_expert)]
+
+    hidden_width = expert_up.shape[2]
+    gins = exchange(order.after(gin_send, results, cut[1]), "ctx", "input_grad")
+    last = swap(order.after(sums, gins), "ctx", n_ctx - 1, n_ctx, "expert_sums")
+    block_out = output_call(place, order.after(results, cut[1]), mid, dest_cols, n_ctx)
+    early = jnp.stack(order.after(own, cut[1]))
+    grads = expert_grads_call(place, [early], (0, 0), (0, 1), n_ctx, hidden_width, None)
+    early = swap(early, "dp", 1, n_dp, "expert_sums")
+    grads = expert_grads_call(place, [early], (1, 0), (0, 1), n_ctx, hidden_width, grads)
+    cut = order.after(cut, grads[3], block_out, gins)
+
+    part = add_all(cut)
+    part = add_all(reduce_ctx([part[g] for g in range(n_ctx)], n_ctx, "shared"))
+    part = jnp.stack(order.after(reduce_ctx([part] * n_ctx, n_ctx, "shared_sums"), last))
     every = [part, swap(part, "dp", 1, n_dp, "shared_sums")]
-    own = order.after(jnp.stack(own), part)
-    hidden_width = expert_up.shape[2]
-    other = swap(own, "dp", 1, n_dp, "expert_sums")
-    half = expert_grads_call(place, own, 0, hidden_width, None)
-    grad_up, grad_down, grad_up_bias, grad_down_bias = expert_grads_call(place, other, 1, hidden_width, half)
+    grad_up, grad_down, grad_up_bias, grad_down_bias = expert_grads_call(
+        place, [last[None], swap(last, "dp", 1, n_dp, "expert_sums")[None]], (0, n_ctx - 1), (1, 0), n_ctx,
+        hidden_width, grads,
+    )
     input_grad = input_call(place, grad_mid, gins, order.seen)
     grad_qkv, grad_proj, grad_router, *vectors = shared_grads_call(place, every, width, expert_count)
     g1_gain, g1_bias, g_query_bias, g_value_bias, g2_gain, g2_bias, g_proj_bias = (
@@ -1027,7 +1049,7 @@
         g_proj_bias,
         g2_gain,
         g2_bias,
-        grad_router,
+        grad_router.T,
         grad_up[None],
         grad_up_bias,
         grad_down[None],

time: 257 us -> 247 us (0.961)
  waiting for transfers between devices: 52.4 us -> 43.2 us
  Pallas kernels: 125 us -> 122 us
    ppermute x34 -> x35, waiting for transfers between devices: 51 us -> 40.4 us  [swap(): return lax.ppermute(x, axis, [(i, i ^ d) for i in range(size)])]
    pallas_call x4, Pallas kernels: 43.2 us -> 37.7 us  [expert_call(): pl.pallas_call(kernel, grid_spec=pltpu.PrefetchScalarGridSpec(num_scalar_...]
    pallas_call x2 -> x3, Pallas kernels: 9.86 us -> 12.4 us  [expert_grads_call(): pl.pallas_call(kernel, grid_spec=pltpu.PrefetchScalarGridSpec(num_scalar_...]
    unnamed x66 -> x91, local copies, waits for them, and re-layouts: 9.33 us -> 11.1 us
    ppermute x34 -> x35, starting transfers between devices: 42.7 us -> 41.5 us  [swap(): return lax.ppermute(x, axis, [(i, i ^ d) for i in range(size)])]
  transfers between devices with their start and end apart: 37 -> 38, of which waited for: 16 -> 14; matrix products, arithmetic and copies ran while one was open for 3% -> 4% of each run, Pallas kernels for 46% -> 48%
where the time goes in v2:
time: 247 us; the launch traced here: 246 us
  Pallas kernels  122 us (49%)
  starting transfers between devices  58.2 us (24%)
  waiting for transfers between devices  43.2 us (17%)
  local copies, waits for them, and re-layouts  13 us (5%)
  other arithmetic  7.3 us (3%)
    ppermute x35, starting transfers between devices, swap(): return lax.ppermute(x, axis, [(i, i ^ d) for i in range(size)])  41.5 us
    ppermute x35, waiting for transfers between devices, swap(): return lax.ppermute(x, axis, [(i, i ^ d) for i in range(size)])  40.4 us
    pallas_call x4, Pallas kernels, expert_call(): pl.pallas_call(kernel, grid_spec=pltpu.PrefetchScalarGridSpec(num_scalar_...  37.7 us
    all_to_all x3, starting transfers between devices, exchange(): return lax.all_to_all(x, axis, split_axis=0, concat_axis=0, tiled=True)  16.7 us
    pallas_call x1, Pallas kernels, attend_back_call(): pl.pallas_call(kernel, grid=(images,), in_specs=[SMEM_SPEC] + [full(a) fo...  16.6 us
    pallas_call x1, Pallas kernels, weights_call(): pl.pallas_call(kernel, grid=(steps,), in_specs=[SMEM_SPEC] + [full(a) for...  14 us
    pallas_call x3, Pallas kernels, expert_grads_call(): pl.pallas_call(kernel, grid_spec=pltpu.PrefetchScalarGridSpec(num_scalar_...  12.4 us
    pallas_call x1, Pallas kernels, middle_back_call(): pl.pallas_call(kernel, in_specs=[SMEM_SPEC] + [VMEM_SPEC] * len(ins) + [A...  11.3 us
  transfers between devices with their start and end apart: 38, of which 14 were waited for; matrix products, arithmetic and copies ran while one was open for 4% of the time, Pallas kernels for 48%

profile of v2, /device:TPU:0, one launch (start us, length us, event | category | flops | bytes accessed | tf_op | source)
XLA Modules:
  0.0 245.6 jit_solution(3144850398183665661)
XLA Ops:
  1.3 2.1 pieces.1
  3.4 2.9 %collective-permute-start = (bf16[208,512]{1,0:T(8,128)(2,1)}, bf16[208,512]{1,0:T(8,128)(2,1)S(1)}, u32[]{:S(2)}, u32[]{:S(2)}) collective-permute-start(bf16[208,512]{1,0:T(8,128)(2,1)} %get-tuple-element.143.refs_5_), channel_id=1, source_target_pairs={{0,2},{2,0},{4,6},{6,4},{1,3},{3,1},{5,7},{7,5},{8,10},{10,8},{12,... | collective-permute-start | bytes 638984 | tf_op jit(solution)/shard_map/tokens_ctx_1/ppermute | solution.py:870
  6.4 1.5 collective-permute-start.1
  8.9 4.5 %route.1 = (s32[8,768]{1,0:T(8,128)}, s32[768,8]{1,0:T(8,128)}, bf16[4,384,512]{2,1,0:T(8,128)(2,1)}, bf16[1,384,512]{2,1,0:T(8,128)(2,1)}) custom-call(s32[3]{0:T(128)} %pad_add_fusion.2.place_ref, s32[8,768]{1,0:T(8,128)} %pad.8.ints_ref, bf16[4,192,512]{2,1,0:T(8,128)(2,1)} %bitcast.79), custom_call_target="tpu_custom_call" | custom-call | flops 4600000000 | bytes 131072 | tf_op jit(solution)/shard_map/route/pallas_call | solution.py:149
  13.4 5.3 %all-to-all-start = ((bf16[4,384,512]{2,1,0:T(8,128)(2,1)}), bf16[4,384,512]{2,1,0:T(8,128)(2,1)S(1)}, u32[]{:S(2)}, u32[]{:S(2)}) async-start(bf16[4,384,512]{2,1,0:T(8,128)(2,1)} %get-tuple-element.156), calls=%async_computation | async-start | bytes 3145728 | tf_op jit(solution)/shard_map/upstream/all_to_all | solution.py:875
  19.6 9.8 %attend.1 = (bf16[192,512]{1,0:T(8,128)(2,1)}, bf16[192,512]{1,0:T(8,128)(2,1)}, bf16[192,512]{1,0:T(8,128)(2,1)}, bf16[192,512]{1,0:T(8,128)(2,1)}, bf16[3,512,...) custom-call(bf16[208,512]{1,0:T(8,128)(2,1)} %get-tuple-element.142.refs_, ...), custom_call_target="tpu_custom_call" | custom-call | flops 13799999488 | bytes 131072 | tf_op jit(solution)/shard_map/attend/pallas_call | solution.py:235
  29.4 1.6 collective-permute-start.3
  31.0 1.5 collective-permute-start.4
  33.2 4.1 %collective-permute-done.3.refs_1_.refs_9_ = bf16[192,512]{1,0:T(8,128)(2,1)S(1)} collective-permute-done((bf16[192,512]{1,0:T(8,128)(2,1)}, bf16[192,512]{1,0:T(8,128)(2,1)S(1)}, u32[]{:S(2)}, u32[]{:S(2)}) %collective-permute-start.3) | collective-permute-done | bytes 196640 | tf_op jit(solution)/shard_map/attended_ctx_1/ppermute | solution.py:870
  37.3 3.6 %collective-permute-done.4.refs_2_.refs_10_ = bf16[192,512]{1,0:T(8,128)(2,1)S(1)} collective-permute-done((bf16[192,512]{1,0:T(8,128)(2,1)}, bf16[192,512]{1,0:T(8,128)(2,1)S(1)}, u32[]{:S(2)}, u32[]{:S(2)}) %collective-permute-start.4) | collective-permute-done | bytes 196640 | tf_op jit(solution)/shard_map/attended_ctx_2/ppermute | solution.py:870
  41.7 4.8 %middle.1 = (f32[768,512]{1,0:T(8,128)}, bf16[768,512]{1,0:T(8,128)(2,1)}, bf16[384,512]{1,0:T(8,128)(2,1)}, bf16[384,512]{1,0:T(8,128)(2,1)}, bf16[384,512]{1,0:T(8,128)(2,1)}, /*index=5*/bf16[384,512]{1,0:T(8,128)(2,1)}) custom-call(s32[3]{0:T(128)} %pad_add_fusion.2.place_ref, bf16[192,512]{1,0:T(8,128)(2,1)} %get-tuple-element.147.refs_0_.refs_8_, ...), custom_call_target="tpu_custom_call" | custom-call | flops 5750000128 | bytes 131072 | tf_op jit(solution)/shard_map/middle/pallas_call | solution.py:278
  46.5 1.8 collective-permute-start.8
  48.3 2.4 collective-permute-start.7
  50.7 1.6 copy-done.4
  53.3 9.3 %expert.4 = (bf16[4,384,512]{2,1,0:T(8,128)(2,1)}, bf16[1536,512]{1,0:T(8,128)(2,1)}, bf16[1536,2048]{1,0:T(8,128)(2,1)}, bf16[1536,2048]{1,0:T(8,128)(2,1)}, bf16[400,512]{1,0:T(8,128)(2,1)}) custom-call(s32[3]{0:T(128)S(1)} %copy-done.1, bf16[384,512]{1,0:T(8,128)(2,1)S(1)} %copy-done.13, bf16[1,384,512]{2,1,0:T(8,128)(2,1)S(1)} %copy-done.12, ...), custom_call_target="tpu_custom_call" | custom-call | flops 10350000128 | bytes 131072 | tf_op jit(solution)/shard_map/expert/pallas_call | solution.py:378
  62.9 4.0 %collective-permute-done.8.refs_0_.refs_1_ = bf16[384,512]{1,0:T(8,128)(2,1)S(1)} collective-permute-done((bf16[384,512]{1,0:T(8,128)(2,1)}, bf16[384,512]{1,0:T(8,128)(2,1)S(1)}, u32[]{:S(2)}, u32[]{:S(2)}) %collective-permute-start.8) | collective-permute-done | bytes 393248 | tf_op jit(solution)/shard_map/rows_expert_1/ppermute | solution.py:870
  66.9 1.7 copy-done.3
  68.6 1.6 copy-done.5
  70.2 9.3 %expert.5 = (bf16[4,384,512]{2,1,0:T(8,128)(2,1)}, bf16[1536,512]{1,0:T(8,128)(2,1)}, bf16[1536,2048]{1,0:T(8,128)(2,1)}, bf16[1536,2048]{1,0:T(8,128)(2,1)}, bf16[400,512]{1,0:T(8,128)(2,1)}) custom-call(s32[3]{0:T(128)S(1)} %copy-done.1, ...), custom_call_target="tpu_custom_call", output_to_operand_aliasing={{0}: (8, {}), {1}: (9, {}), {2}: (10, {}), {3}: (11, {})} | custom-call | flops 10350000128 | bytes 131072 | tf_op jit(solution)/shard_map/expert/pallas_call | solution.py:378
  79.6 1.7 collective-permute-done.7.refs_0_.refs_2_
  81.3 9.4 %expert.6 = (bf16[4,384,512]{2,1,0:T(8,128)(2,1)}, bf16[1536,512]{1,0:T(8,128)(2,1)}, bf16[1536,2048]{1,0:T(8,128)(2,1)}, bf16[1536,2048]{1,0:T(8,128)(2,1)}, bf16[400,512]{1,0:T(8,128)(2,1)}) custom-call(s32[3]{0:T(128)S(1)} %copy-done.1, ...), custom_call_target="tpu_custom_call", output_to_operand_aliasing={{0}: (8, {}), {1}: (9, {}), {2}: (10, {}), {3}: (11, {})} | custom-call | flops 10350000128 | bytes 131072 | tf_op jit(solution)/shard_map/expert/pallas_call | solution.py:378
  90.6 7.5 %collective-permute-start.10 = (bf16[400,512]{1,0:T(8,128)(2,1)}, bf16[400,512]{1,0:T(8,128)(2,1)S(1)}, u32[]{:S(2)}, u32[]{:S(2)}) collective-permute-start(bf16[400,512]{1,0:T(8,128)(2,1)} %get-tuple-element.178), channel_id=1, source_target_pairs={{0,16},{8,24},{16,0},{24,8},{1,17},{9,25},{17,1},{25,9},{2,18},{10... | collective-permute-start | bytes 1228808 | tf_op jit(solution)/shard_map/rows_grad_expert_2/ppermute | solution.py:870
  98.2 9.7 %expert.7 = (bf16[4,384,512]{2,1,0:T(8,128)(2,1)}, bf16[1536,512]{1,0:T(8,128)(2,1)}, bf16[1536,2048]{1,0:T(8,128)(2,1)}, bf16[1536,2048]{1,0:T(8,128)(2,1)}, bf16[400,512]{1,0:T(8,128)(2,1)}) custom-call(s32[3]{0:T(128)S(1)} %copy-done.1, ...), custom_call_target="tpu_custom_call", output_to_operand_aliasing={{0}: (8, {}), {1}: (9, {}), {2}: (10, {}), {3}: (11, {})} | custom-call | flops 10350000128 | bytes 131072 | tf_op jit(solution)/shard_map/expert/pallas_call | solution.py:378
  107.9 14.0 %weights.1 = (bf16[4,528,512]{2,1,0:T(8,128)(2,1)}, bf16[4,528,512]{2,1,0:T(8,128)(2,1)}) custom-call(s32[3]{0:T(128)} %pad_add_fusion.2.place_ref, bf16[384,512]{1,0:T(8,128)(2,1)} %get-tuple-element.152.refs_0_, bf16[384,512]{1,0:T(8,128)(2,1)} %copy-done.7, bf16[384,512]{1,0:T(8,128)(2,1)} %copy-done.8, bf16[384,512]{1,0:T(8,128)(2,1)} %copy-done.9, ...), custom_call_target="tpu_custom_call" | custom-call | flops 14949999616 | bytes 131072 | tf_op jit(solution)/shard_map/weights/pallas_call | solution.py:464
  122.9 11.3 %middle_back.1 = (f32[768,512]{1,0:T(8,128)}, bf16[192,512]{1,0:T(8,128)(2,1)}, bf16[192,512]{1,0:T(8,128)(2,1)}, bf16[192,512]{1,0:T(8,128)(2,1)}, bf16[192,512]{1,0:T(8,128)(2,1)}, /*index=5*/bf16[528,512]{1,0:T(8,128)(2,1)}) custom-call(s32[3]{0:T(128)} %pad_add_fusion.2.place_ref, bf16[400,512]{1,0:T(8,128)(2,1)} %get-tuple-element.208.refs_0_, ...), custom_call_target="tpu_custom_call" | custom-call | flops 34500001792 | bytes 131072 | tf_op jit(solution)/shard_map/middle_back/pallas_call | solution.py:573
  135.7 2.6 %collective-permute-start.14 = (bf16[192,512]{1,0:T(8,128)(2,1)}, bf16[192,512]{1,0:T(8,128)(2,1)S(1)}, u32[]{:S(2)}, u32[]{:S(2)}) collective-permute-start(bf16[192,512]{1,0:T(8,128)(2,1)} %get-tuple-element.190), channel_id=1, source_target_pairs={{0,4},{2,6},{4,0},{6,2},{1,5},{3,7},{5,1},{7,3},{8,12},{10,14},{12... | collective-permute-start | bytes 589832 | tf_op jit(solution)/shard_map/attended_grad_ctx_2/ppermute | solution.py:870
  138.2 7.9 %all-to-all-start.1 = ((bf16[4,384,512]{2,1,0:T(8,128)(2,1)}), bf16[4,384,512]{2,1,0:T(8,128)(2,1)}, u32[]{:S(2)}, u32[]{:S(2)}) async-start(bf16[4,384,512]{2,1,0:T(8,128)(2,1)} %get-tuple-element.184), calls=%async_computation.1 | async-start | bytes 3145728 | tf_op jit(solution)/shard_map/results/all_to_all | solution.py:875
  146.1 2.1 fusion.3
  150.2 1.8 collective-permute-start.18
  151.9 16.6 %attend_back.1 = (bf16[4,192,512]{2,1,0:T(8,128)(2,1)}, bf16[4,272,512]{2,1,0:T(8,128)(2,1)}, bf16[4,272,512]{2,1,0:T(8,128)(2,1)}) custom-call(s32[3]{0:T(128)} %pad_add_fusion.2.place_ref, bf16[208,512]{1,0:T(8,128)(2,1)} %get-tuple-element.142.refs_0_.refs_4_, bf16[208,512]{1,0:T(8,128)(2,1)} %copy-done.38, bf16[208,512]{1,0:T(8,128)(2,1)} %copy-done.39, ...), custom_call_target="tpu_custom_call" | custom-call | flops 23000000512 | bytes 131072 | tf_op jit(solution)/shard_map/attend_back/pallas_call | solution.py:702
  168.6 5.9 %collective-permute-done.17 = bf16[528,512]{1,0:T(8,128)(2,1)S(1)} collective-permute-done((bf16[528,512]{1,0:T(8,128)(2,1)S(1)}, bf16[528,512]{1,0:T(8,128)(2,1)S(1)}, u32[]{:S(2)}, u32[]{:S(2)}) %collective-permute-start.17) | collective-permute-done | bytes 540704 | tf_op jit(solution)/shard_map/expert_terms_ctx_2/ppermute | solution.py:870
  175.3 3.0 %collective-permute-done.19 = bf16[4,272,512]{2,1,0:T(8,128)(2,1)S(1)} collective-permute-done((bf16[4,272,512]{2,1,0:T(8,128)(2,1)}, bf16[4,272,512]{2,1,0:T(8,128)(2,1)S(1)}, u32[]{:S(2)}, u32[]{:S(2)}) %collective-permute-start.19) | collective-permute-done | bytes 1114144 | tf_op jit(solution)/shard_map/shared_dp_1/ppermute | solution.py:870
  178.3 1.6 add_convert_fusion
  181.9 1.5 collective-permute-start.22
  183.4 6.1 %collective-permute-done.20.refs_14_.refs_16_.refs_17_ = bf16[4,272,128]{2,1,0:T(8,128)(2,1)S(1)} collective-permute-done((bf16[4,272,128]{2,1,0:T(8,128)(2,1)S(1)}, bf16[4,272,128]{2,1,0:T(8,128)(2,1)S(1)}, u32[]{:S(2)}, u32[]{:S(2)}) %collective-permute-start.20) | collective-permute-done | bytes 278560 | tf_op jit(solution)/shard_map/shared_expert_1/ppermute | solution.py:870
  189.5 3.5 %all-to-all-start.2 = ((bf16[4,192,512]{2,1,0:T(8,128)(2,1)}), bf16[4,192,512]{2,1,0:T(8,128)(2,1)S(1)}, u32[]{:S(2)}, u32[]{:S(2)}) async-start(bf16[4,192,512]{2,1,0:T(8,128)(2,1)} %get-tuple-element.207), calls=%async_computation.2 | async-start | bytes 1572864 | tf_op jit(solution)/shard_map/input_grad/all_to_all | solution.py:875
  193.0 1.6 collective-permute-start.23
  196.2 3.9 %collective-permute-done.22 = bf16[528,512]{1,0:T(8,128)(2,1)} collective-permute-done((bf16[528,512]{1,0:T(8,128)(2,1)S(1)}, bf16[528,512]{1,0:T(8,128)(2,1)}, u32[]{:S(2)}, u32[]{:S(2)}) %collective-permute-start.22) | collective-permute-done | bytes 540704 | tf_op jit(solution)/shard_map/expert_sums_ctx_2/ppermute | solution.py:870
  201.6 2.8 %all-to-all-done.2.gin_ref.refs_15_.refs_20_ = bf16[4,192,512]{2,1,0:T(8,128)(2,1)S(1)} async-done(((bf16[4,192,512]{2,1,0:T(8,128)(2,1)}), bf16[4,192,512]{2,1,0:T(8,128)(2,1)S(1)}, u32[]{:S(2)}, u32[]{:S(2)}) %all-to-all-start.2) | async-done | bytes 786464 | tf_op jit(solution)/shard_map/input_grad/all_to_all | solution.py:875
  205.8 4.3 %output.1.refs_19_ = bf16[4,192,512]{2,1,0:T(8,128)(2,1)} custom-call(s32[3]{0:T(128)} %pad_add_fusion.2.place_ref, bf16[4,384,512]{2,1,0:T(8,128)(2,1)} %all-to-all-done.1.o_ref.refs_13_, f32[768,512]{1,0:T(8,128)} %get-tuple-element.180.refs_4_.mid_ref, s32[768,8]{1,0:T(8,128)} %get-tuple-element.182.refs_7_.dest_ref), custom_call_target="tpu_custom_call" | custom-call | flops 34500001792 | bytes 131072 | tf_op jit(solution)/shard_map/output/pallas_call | solution.py:501
  210.1 4.4 %expert_grads.3 = (f32[512,2048]{1,0:T(8,128)}, f32[2048,512]{1,0:T(8,128)}, f32[1,2048]{1,0:T(1,128)}, f32[1,512]{1,0:T(1,128)}) custom-call(s32[3]{0:T(128)} %pad_add_fusion.2.place_ref, bf16[3,528,512]{2,1,0:T(8,128)(2,1)} %copy-done.21), custom_call_target="tpu_custom_call" | custom-call | flops 3449999872 | bytes 131072 | tf_op jit(solution)/shard_map/expert_grads/pallas_call | solution.py:796
  214.5 4.5 %collective-permute-done.32.refs_21_ = bf16[528,512]{1,0:T(8,128)(2,1)S(1)} collective-permute-done((bf16[528,512]{1,0:T(8,128)(2,1)S(1)}, bf16[528,512]{1,0:T(8,128)(2,1)S(1)}, u32[]{:S(2)}, u32[]{:S(2)}) %collective-permute-start.32) | collective-permute-done | bytes 540704 | tf_op jit(solution)/shard_map/expert_sums_ctx_3/ppermute | solution.py:870
  219.0 4.6 %expert_grads.4 = (f32[512,2048]{1,0:T(8,128)}, f32[2048,512]{1,0:T(8,128)}, f32[1,2048]{1,0:T(1,128)}, f32[1,512]{1,0:T(1,128)}) custom-call(s32[3]{0:T(128)} %pad_add_fusion.2.place_ref, bf16[3,528,512]{2,1,0:T(8,128)(2,1)} %collective-permute-done.25.refs_0_, ...), custom_call_target="tpu_custom_call", output_to_operand_aliasing={{0}: (2, {}), {1}: (3, {})} | custom-call | flops 3449999872 | bytes 131072 | tf_op jit(solution)/shard_map/expert_grads/pallas_call | solution.py:796
  226.5 1.8 collective-permute-start.28
  229.9 1.9 collective-permute-done.28
  236.2 3.4 %expert_grads.5 = (f32[512,2048]{1,0:T(8,128)}, f32[2048,512]{1,0:T(8,128)}, f32[1,2048]{1,0:T(1,128)}, f32[1,512]{1,0:T(1,128)}) custom-call(s32[3]{0:T(128)} %pad_add_fusion.2.place_ref, bf16[1,528,512]{2,1,0:T(8,128)(2,1)} %bitcast.73, bf16[1,528,512]{2,1,0:T(8,128)(2,1)} %bitcast.81, ...), custom_call_target="tpu_custom_call", output_to_operand_aliasing={{0}: (3, {}), {1}: (4, {})} | custom-call | flops 3449999872 | bytes 131072 | tf_op jit(solution)/shard_map/expert_grads/pallas_call | solution.py:796
  239.7 2.7 %input.1 = bf16[4,192,512]{2,1,0:T(8,128)(2,1)} custom-call(s32[3]{0:T(128)} %pad_add_fusion.2.place_ref, f32[768,512]{1,0:T(8,128)} %get-tuple-element.205.gmid_ref, bf16[4,192,512]{2,1,0:T(8,128)(2,1)} %copy-done.14, bf16[400,512]{1,0:T(8,128)(2,1)} %get-tuple-element.208.refs_0_, bf16[400,512]{1,0:T(8,128)(2,1)} %copy-done.26, ...), custom_call_target="tpu_custom_call" | custom-call | flops 3449999872 | bytes 131072 | tf_op jit(solution)/shard_map/input/pallas_call | solution.py:737
  243.0 2.4 shared_grads.1
  (157 shorter events, 26.6 us)
Async XLA Ops:
  3.4 15.3 %collective-permute-start = (bf16[208,512]{1,0:T(8,128)(2,1)}, bf16[208,512]{1,0:T(8,128)(2,1)S(1)}, u32[]{:S(2)}, u32[]{:S(2)}) collective-permute-start(bf16[208,512]{1,0:T(8,128)(2,1)} %get-tuple-element.143.refs_5_), channel_id=1, source_target_pairs={{0,2},{2,0},{4,6},{6,4},{1,3},{3,1},{5,7},{7,5},{8,10},{10,8},{12,... | collective-permute-start | bytes 638984 | tf_op jit(solution)/shard_map/tokens_ctx_1/ppermute | solution.py:870
  6.4 12.4 %collective-permute-start.1 = (bf16[208,512]{1,0:T(8,128)(2,1)}, bf16[208,512]{1,0:T(8,128)(2,1)S(1)}, u32[]{:S(2)}, u32[]{:S(2)}) collective-permute-start(bf16[208,512]{1,0:T(8,128)(2,1)} %get-tuple-element.144.refs_6_), channel_id=1, source_target_pairs={{0,4},{2,6},{4,0},{6,2},{1,5},{3,7},{5,1},{7,3},{8,12},{10,14},{12... | collective-permute-start | bytes 638984 | tf_op jit(solution)/shard_map/tokens_ctx_2/ppermute | solution.py:870
  7.9 10.9 %collective-permute-start.2 = (bf16[208,512]{1,0:T(8,128)(2,1)}, bf16[208,512]{1,0:T(8,128)(2,1)S(1)}, u32[]{:S(2)}, u32[]{:S(2)}) collective-permute-start(bf16[208,512]{1,0:T(8,128)(2,1)} %get-tuple-element.145.refs_7_), channel_id=1, source_target_pairs={{0,6},{2,4},{4,2},{6,0},{1,7},{3,5},{5,3},{7,1},{8,14},{10,12},{12... | collective-permute-start | bytes 638984 | tf_op jit(solution)/shard_map/tokens_ctx_3/ppermute | solution.py:870
  13.4 53.4 %all-to-all-start = ((bf16[4,384,512]{2,1,0:T(8,128)(2,1)}), bf16[4,384,512]{2,1,0:T(8,128)(2,1)S(1)}, u32[]{:S(2)}, u32[]{:S(2)}) async-start(bf16[4,384,512]{2,1,0:T(8,128)(2,1)} %get-tuple-element.156), calls=%async_computation | async-start | bytes 3145728 | tf_op jit(solution)/shard_map/upstream/all_to_all | solution.py:875
  19.6 13.3 %copy-start.33 = (bf16[512,4]{0,1:T(4,128)(2,1)S(1)}, bf16[512,4]{0,1:T(4,128)(2,1)}, u32[]{:S(2)}) copy-start(bf16[512,4]{0,1:T(4,128)(2,1)} %param.33) | copy-start | bytes 12292
  29.4 7.9 %collective-permute-start.3 = (bf16[192,512]{1,0:T(8,128)(2,1)}, bf16[192,512]{1,0:T(8,128)(2,1)S(1)}, u32[]{:S(2)}, u32[]{:S(2)}) collective-permute-start(bf16[192,512]{1,0:T(8,128)(2,1)} %get-tuple-element.148), channel_id=1, source_target_pairs={{0,2},{2,0},{4,6},{6,4},{1,3},{3,1},{5,7},{7,5},{8,10},{10,8},{12,... | collective-permute-start | bytes 589832 | tf_op jit(solution)/shard_map/attended_ctx_1/ppermute | solution.py:870
  31.0 9.9 %collective-permute-start.4 = (bf16[192,512]{1,0:T(8,128)(2,1)}, bf16[192,512]{1,0:T(8,128)(2,1)S(1)}, u32[]{:S(2)}, u32[]{:S(2)}) collective-permute-start(bf16[192,512]{1,0:T(8,128)(2,1)} %get-tuple-element.149), channel_id=1, source_target_pairs={{0,4},{2,6},{4,0},{6,2},{1,5},{3,7},{5,1},{7,3},{8,12},{10,14},{12... | collective-permute-start | bytes 589832 | tf_op jit(solution)/shard_map/attended_ctx_2/ppermute | solution.py:870
  32.5 8.4 %collective-permute-start.5 = (bf16[192,512]{1,0:T(8,128)(2,1)}, bf16[192,512]{1,0:T(8,128)(2,1)S(1)}, u32[]{:S(2)}, u32[]{:S(2)}) collective-permute-start(bf16[192,512]{1,0:T(8,128)(2,1)} %get-tuple-element.150), channel_id=1, source_target_pairs={{0,6},{2,4},{4,2},{6,0},{1,7},{3,5},{5,3},{7,1},{8,14},{10,12},{12... | collective-permute-start | bytes 589832 | tf_op jit(solution)/shard_map/attended_ctx_3/ppermute | solution.py:870
  33.2 65.0 %copy-start = (bf16[512,128]{1,0:T(8,128)(2,1)}, bf16[512,128]{1,0:T(8,128)(2,1)S(1)}, u32[]{:S(2)}) copy-start(bf16[512,128]{1,0:T(8,128)(2,1)S(1)} %pad.9.refs_2_.refs_12_) | copy-start | bytes 393220
  46.5 20.4 %collective-permute-start.8 = (bf16[384,512]{1,0:T(8,128)(2,1)}, bf16[384,512]{1,0:T(8,128)(2,1)S(1)}, u32[]{:S(2)}, u32[]{:S(2)}) collective-permute-start(bf16[384,512]{1,0:T(8,128)(2,1)} %get-tuple-element.158), channel_id=1, source_target_pairs={{0,8},{8,0},{16,24},{24,16},{1,9},{9,1},{17,25},{25,17},{2,10},{10... | collective-permute-start | bytes 1179656 | tf_op jit(solution)/shard_map/rows_expert_1/ppermute | solution.py:870
  48.3 33.0 %collective-permute-start.7 = (bf16[384,512]{1,0:T(8,128)(2,1)}, bf16[384,512]{1,0:T(8,128)(2,1)S(1)}, u32[]{:S(2)}, u32[]{:S(2)}) collective-permute-start(bf16[384,512]{1,0:T(8,128)(2,1)} %get-tuple-element.157), channel_id=1, source_target_pairs={{0,16},{8,24},{16,0},{24,8},{1,17},{9,25},{17,1},{25,9},{2,18},{10... | collective-permute-start | bytes 1179656 | tf_op jit(solution)/shard_map/rows_expert_2/ppermute | solution.py:870
  62.6 35.5 %collective-permute-start.6 = (bf16[384,512]{1,0:T(8,128)(2,1)S(1)}, bf16[384,512]{1,0:T(8,128)(2,1)S(1)}, u32[]{:S(2)}, u32[]{:S(2)}) collective-permute-start(bf16[384,512]{1,0:T(8,128)(2,1)S(1)} %copy-done.36), channel_id=1, source_target_pairs={{0,24},{8,16},{16,8},{24,0},{1,25},{9,17},{17,9},{25,1},{2,26},{10... | collective-permute-start | bytes 1179656 | tf_op jit(solution)/shard_map/rows_expert_3/ppermute | solution.py:870
  66.8 12.6 %copy-start.7 = (bf16[384,512]{1,0:T(8,128)(2,1)}, bf16[384,512]{1,0:T(8,128)(2,1)S(1)}, u32[]{:S(2)}) copy-start(bf16[384,512]{1,0:T(8,128)(2,1)S(1)} %collective-permute-done.8.refs_0_.refs_1_) | copy-start | bytes 1179652
  79.5 18.7 %collective-permute-start.9 = (bf16[400,512]{1,0:T(8,128)(2,1)}, bf16[400,512]{1,0:T(8,128)(2,1)S(1)}, u32[]{:S(2)}, u32[]{:S(2)}) collective-permute-start(bf16[400,512]{1,0:T(8,128)(2,1)} %get-tuple-element.171), channel_id=1, source_target_pairs={{0,8},{8,0},{16,24},{24,16},{1,9},{9,1},{17,25},{25,17},{2,10},{10... | collective-permute-start | bytes 1228808 | tf_op jit(solution)/shard_map/rows_grad_expert_1/ppermute | solution.py:870
  90.6 31.3 %collective-permute-start.10 = (bf16[400,512]{1,0:T(8,128)(2,1)}, bf16[400,512]{1,0:T(8,128)(2,1)S(1)}, u32[]{:S(2)}, u32[]{:S(2)}) collective-permute-start(bf16[400,512]{1,0:T(8,128)(2,1)} %get-tuple-element.178), channel_id=1, source_target_pairs={{0,16},{8,24},{16,0},{24,8},{1,17},{9,25},{17,1},{25,9},{2,18},{10... | collective-permute-start | bytes 1228808 | tf_op jit(solution)/shard_map/rows_grad_expert_2/ppermute | solution.py:870
  98.2 9.7 %copy-start.9 = (bf16[384,512]{1,0:T(8,128)(2,1)}, bf16[384,512]{1,0:T(8,128)(2,1)S(1)}, u32[]{:S(2)}) copy-start(bf16[384,512]{1,0:T(8,128)(2,1)S(1)} %collective-permute-done.6.refs_0_.refs_3_) | copy-start | bytes 1179652
  98.2 9.7 %copy-start.6 = (bf16[400,512]{1,0:T(8,128)(2,1)}, bf16[400,512]{1,0:T(8,128)(2,1)S(1)}, u32[]{:S(2)}) copy-start(bf16[400,512]{1,0:T(8,128)(2,1)S(1)} %collective-permute-done.9.refs_11_.refs_1_) | copy-start | bytes 1228804
  107.9 14.2 %collective-permute-start.11 = (bf16[400,512]{1,0:T(8,128)(2,1)}, bf16[400,512]{1,0:T(8,128)(2,1)S(1)}, u32[]{:S(2)}, u32[]{:S(2)}) collective-permute-start(bf16[400,512]{1,0:T(8,128)(2,1)} %get-tuple-element.179), channel_id=1, source_target_pairs={{0,24},{8,16},{16,8},{24,0},{1,25},{9,17},{17,9},{25,1},{2,26},{10... | collective-permute-start | bytes 1228808 | tf_op jit(solution)/shard_map/rows_grad_expert_3/ppermute | solution.py:870
  122.0 24.1 %collective-permute-start.12 = (bf16[4,528,512]{2,1,0:T(8,128)(2,1)}, bf16[4,528,512]{2,1,0:T(8,128)(2,1)}, u32[]{:S(2)}, u32[]{:S(2)}) collective-permute-start(bf16[4,528,512]{2,1,0:T(8,128)(2,1)} %get-tuple-element.186), channel_id=1, source_target_pairs={{0,1},{1,0},{2,3},{3,2},{4,5},{5,4},{6,7},{7,6},{8,9},{9,8},{10,11... | collective-permute-start | bytes 6488072 | tf_op jit(solution)/shard_map/expert_terms_dp_1/ppermute | solution.py:870
  134.2 14.1 %collective-permute-start.13 = (bf16[192,512]{1,0:T(8,128)(2,1)}, bf16[192,512]{1,0:T(8,128)(2,1)S(1)}, u32[]{:S(2)}, u32[]{:S(2)}) collective-permute-start(bf16[192,512]{1,0:T(8,128)(2,1)} %get-tuple-element.189), channel_id=1, source_target_pairs={{0,2},{2,0},{4,6},{6,4},{1,3},{3,1},{5,7},{7,5},{8,10},{10,8},{12,... | collective-permute-start | bytes 589832 | tf_op jit(solution)/shard_map/attended_grad_ctx_1/ppermute | solution.py:870
  135.7 12.7 %collective-permute-start.14 = (bf16[192,512]{1,0:T(8,128)(2,1)}, bf16[192,512]{1,0:T(8,128)(2,1)S(1)}, u32[]{:S(2)}, u32[]{:S(2)}) collective-permute-start(bf16[192,512]{1,0:T(8,128)(2,1)} %get-tuple-element.190), channel_id=1, source_target_pairs={{0,4},{2,6},{4,0},{6,2},{1,5},{3,7},{5,1},{7,3},{8,12},{10,14},{12... | collective-permute-start | bytes 589832 | tf_op jit(solution)/shard_map/attended_grad_ctx_2/ppermute | solution.py:870
  138.2 10.1 %collective-permute-start.15 = (bf16[192,512]{1,0:T(8,128)(2,1)}, bf16[192,512]{1,0:T(8,128)(2,1)S(1)}, u32[]{:S(2)}, u32[]{:S(2)}) collective-permute-start(bf16[192,512]{1,0:T(8,128)(2,1)} %get-tuple-element.191), channel_id=1, source_target_pairs={{0,6},{2,4},{4,2},{6,0},{1,7},{3,5},{5,3},{7,1},{8,14},{10,12},{12... | collective-permute-start | bytes 589832 | tf_op jit(solution)/shard_map/attended_grad_ctx_3/ppermute | solution.py:870
  138.2 45.2 %all-to-all-start.1 = ((bf16[4,384,512]{2,1,0:T(8,128)(2,1)}), bf16[4,384,512]{2,1,0:T(8,128)(2,1)}, u32[]{:S(2)}, u32[]{:S(2)}) async-start(bf16[4,384,512]{2,1,0:T(8,128)(2,1)} %get-tuple-element.184), calls=%async_computation.1 | async-start | bytes 3145728 | tf_op jit(solution)/shard_map/results/all_to_all | solution.py:875
  148.3 20.3 %copy-start.18 = (bf16[528,512]{1,0:T(8,128)(2,1)}, bf16[528,512]{1,0:T(8,128)(2,1)S(1)}, u32[]{:S(2)}) copy-start(bf16[528,512]{1,0:T(8,128)(2,1)S(1)} %get-tuple-element.216.refs_8_) | copy-start | bytes 1622020
  148.3 20.3 %copy-start.19 = (bf16[528,512]{1,0:T(8,128)(2,1)}, bf16[528,512]{1,0:T(8,128)(2,1)S(1)}, u32[]{:S(2)}) copy-start(bf16[528,512]{1,0:T(8,128)(2,1)S(1)} %get-tuple-element.215.refs_7_) | copy-start | bytes 1622020
  148.3 20.3 %copy-start.20 = (bf16[528,512]{1,0:T(8,128)(2,1)}, bf16[528,512]{1,0:T(8,128)(2,1)S(1)}, u32[]{:S(2)}) copy-start(bf16[528,512]{1,0:T(8,128)(2,1)S(1)} %get-tuple-element.214.refs_6_) | copy-start | bytes 1622020
  148.3 32.5 %copy-start.16 = (bf16[528,512]{1,0:T(8,128)(2,1)}, bf16[528,512]{1,0:T(8,128)(2,1)S(1)}, u32[]{:S(2)}) copy-start(bf16[528,512]{1,0:T(8,128)(2,1)S(1)} %get-tuple-element.223.refs_5_) | copy-start | bytes 1622020
  148.4 20.2 %collective-permute-start.16 = (bf16[528,512]{1,0:T(8,128)(2,1)S(1)}, bf16[528,512]{1,0:T(8,128)(2,1)S(1)}, u32[]{:S(2)}, u32[]{:S(2)}) collective-permute-start(bf16[528,512]{1,0:T(8,128)(2,1)S(1)} %get-tuple-element.214.refs_6_), channel_id=1, source_target_pairs={{0,2},{2,0},{4,6},{6,4},{1,3},{3,1},{5,7},{7,5},{8,10},{10,8},{12,... | collective-permute-start | bytes 1622024 | tf_op jit(solution)/shard_map/expert_terms_ctx_1/ppermute | solution.py:870
  149.3 25.1 %collective-permute-start.17 = (bf16[528,512]{1,0:T(8,128)(2,1)S(1)}, bf16[528,512]{1,0:T(8,128)(2,1)S(1)}, u32[]{:S(2)}, u32[]{:S(2)}) collective-permute-start(bf16[528,512]{1,0:T(8,128)(2,1)S(1)} %get-tuple-element.215.refs_7_), channel_id=1, source_target_pairs={{0,4},{2,6},{4,0},{6,2},{1,5},{3,7},{5,1},{7,3},{8,12},{10,14},{12... | collective-permute-start | bytes 1622024 | tf_op jit(solution)/shard_map/expert_terms_ctx_2/ppermute | solution.py:870
  150.2 24.3 %collective-permute-start.18 = (bf16[528,512]{1,0:T(8,128)(2,1)S(1)}, bf16[528,512]{1,0:T(8,128)(2,1)S(1)}, u32[]{:S(2)}, u32[]{:S(2)}) collective-permute-start(bf16[528,512]{1,0:T(8,128)(2,1)S(1)} %get-tuple-element.216.refs_8_), channel_id=1, source_target_pairs={{0,6},{2,4},{4,2},{6,0},{1,7},{3,5},{5,3},{7,1},{8,14},{10,12},{12... | collective-permute-start | bytes 1622024 | tf_op jit(solution)/shard_map/expert_terms_ctx_3/ppermute | solution.py:870
  175.3 3.0 %collective-permute-start.19 = (bf16[4,272,512]{2,1,0:T(8,128)(2,1)}, bf16[4,272,512]{2,1,0:T(8,128)(2,1)S(1)}, u32[]{:S(2)}, u32[]{:S(2)}) collective-permute-start(bf16[4,272,512]{2,1,0:T(8,128)(2,1)} %get-tuple-element.203), channel_id=1, source_target_pairs={{0,1},{1,0},{2,3},{3,2},{4,5},{5,4},{6,7},{7,6},{8,9},{9,8},{10,11... | collective-permute-start | bytes 3342344 | tf_op jit(solution)/shard_map/shared_dp_1/ppermute | solution.py:870
  180.8 8.7 %collective-permute-start.20 = (bf16[4,272,128]{2,1,0:T(8,128)(2,1)S(1)}, bf16[4,272,128]{2,1,0:T(8,128)(2,1)S(1)}, u32[]{:S(2)}, u32[]{:S(2)}) collective-permute-start(bf16[4,272,128]{2,1,0:T(8,128)(2,1)S(1)} %get-tuple-element.277), channel_id=1, source_target_pairs={{0,8},{8,0},{16,24},{24,16},{1,9},{9,1},{17,25},{25,17},{2,10},{10... | collective-permute-start | bytes 835592 | tf_op jit(solution)/shard_map/shared_expert_1/ppermute | solution.py:870
  181.3 14.9 %collective-permute-start.21 = (bf16[528,512]{1,0:T(8,128)(2,1)S(1)}, bf16[528,512]{1,0:T(8,128)(2,1)}, u32[]{:S(2)}, u32[]{:S(2)}) collective-permute-start(bf16[528,512]{1,0:T(8,128)(2,1)S(1)} %add_convert_fusion.1), channel_id=1, source_target_pairs={{0,2},{2,0},{4,6},{6,4},{1,3},{3,1},{5,7},{7,5},{8,10},{10,8},{12,... | collective-permute-start | bytes 1622024 | tf_op jit(solution)/shard_map/expert_sums_ctx_1/ppermute | solution.py:870
  181.9 18.1 %collective-permute-start.22 = (bf16[528,512]{1,0:T(8,128)(2,1)S(1)}, bf16[528,512]{1,0:T(8,128)(2,1)}, u32[]{:S(2)}, u32[]{:S(2)}) collective-permute-start(bf16[528,512]{1,0:T(8,128)(2,1)S(1)} %add_convert_fusion.1), channel_id=1, source_target_pairs={{0,4},{2,6},{4,0},{6,2},{1,5},{3,7},{5,1},{7,3},{8,12},{10,14},{12... | collective-permute-start | bytes 1622024 | tf_op jit(solution)/shard_map/expert_sums_ctx_2/ppermute | solution.py:870
  189.5 34.1 %copy-start.17 = (bf16[4,272,128]{2,1,0:T(8,128)(2,1)}, bf16[4,272,128]{2,1,0:T(8,128)(2,1)S(1)}, u32[]{:S(2)}) copy-start(bf16[4,272,128]{2,1,0:T(8,128)(2,1)S(1)} %collective-permute-done.20.refs_14_.refs_16_.refs_17_) | copy-start | bytes 835588
  189.5 14.8 %all-to-all-start.2 = ((bf16[4,192,512]{2,1,0:T(8,128)(2,1)}), bf16[4,192,512]{2,1,0:T(8,128)(2,1)S(1)}, u32[]{:S(2)}, u32[]{:S(2)}) async-start(bf16[4,192,512]{2,1,0:T(8,128)(2,1)} %get-tuple-element.207), calls=%async_computation.2 | async-start | bytes 1572864 | tf_op jit(solution)/shard_map/input_grad/all_to_all | solution.py:875
  193.0 30.6 %collective-permute-start.23 = (bf16[4,272,128]{2,1,0:T(8,128)(2,1)}, bf16[4,272,128]{2,1,0:T(8,128)(2,1)S(1)}, u32[]{:S(2)}, u32[]{:S(2)}) collective-permute-start(bf16[4,272,128]{2,1,0:T(8,128)(2,1)} %get-tuple-element.275), channel_id=1, source_target_pairs={{0,16},{8,24},{16,0},{24,8},{1,17},{9,25},{17,1},{25,9},{2,18},{10... | collective-permute-start | bytes 835592 | tf_op jit(solution)/shard_map/shared_expert_2/ppermute | solution.py:870
  194.7 28.9 %collective-permute-start.24 = (bf16[4,272,128]{2,1,0:T(8,128)(2,1)}, bf16[4,272,128]{2,1,0:T(8,128)(2,1)}, u32[]{:S(2)}, u32[]{:S(2)}) collective-permute-start(bf16[4,272,128]{2,1,0:T(8,128)(2,1)} %get-tuple-element.274), channel_id=1, source_target_pairs={{0,24},{8,16},{16,8},{24,0},{1,25},{9,17},{17,9},{25,1},{2,26},{10... | collective-permute-start | bytes 835592 | tf_op jit(solution)/shard_map/shared_expert_3/ppermute | solution.py:870
  201.5 17.6 %collective-permute-start.25 = (bf16[3,528,512]{2,1,0:T(8,128)(2,1)S(1)}, bf16[3,528,512]{2,1,0:T(8,128)(2,1)}, u32[]{:S(2)}, u32[]{:S(2)}) collective-permute-start(bf16[3,528,512]{2,1,0:T(8,128)(2,1)S(1)} %pad_maximum_fusion.refs_0_), channel_id=1, source_target_pairs={{0,1},{1,0},{2,3},{3,2},{4,5},{5,4},{6,7},{7,6},{8,9},{9,8},{10,11... | collective-permute-start | bytes 4866056 | tf_op jit(solution)/shard_map/expert_sums_dp_1/ppermute | solution.py:870
  204.3 14.7 %collective-permute-start.32 = (bf16[528,512]{1,0:T(8,128)(2,1)S(1)}, bf16[528,512]{1,0:T(8,128)(2,1)S(1)}, u32[]{:S(2)}, u32[]{:S(2)}) collective-permute-start(bf16[528,512]{1,0:T(8,128)(2,1)S(1)} %add_convert_fusion.1), channel_id=1, source_target_pairs={{0,6},{2,4},{4,2},{6,0},{1,7},{3,5},{5,3},{7,1},{8,14},{10,12},{12... | collective-permute-start | bytes 1622024 | tf_op jit(solution)/shard_map/expert_sums_ctx_3/ppermute | solution.py:870
  219.0 16.3 %collective-permute-start.34 = (bf16[528,512]{1,0:T(8,128)(2,1)S(1)}, bf16[528,512]{1,0:T(8,128)(2,1)S(1)}, u32[]{:S(2)}, u32[]{:S(2)}) collective-permute-start(bf16[528,512]{1,0:T(8,128)(2,1)S(1)} %collective-permute-done.32.refs_21_), channel_id=1, source_target_pairs={{0,1},{1,0},{2,3},{3,2},{4,5},{5,4},{6,7},{7,6},{8,9},{9,8},{10,11... | collective-permute-start | bytes 1622024 | tf_op jit(solution)/shard_map/expert_sums_dp_1/ppermute | solution.py:870
  224.8 4.6 %collective-permute-start.26 = (bf16[272,128]{1,0:T(8,128)(2,1)S(1)}, bf16[272,128]{1,0:T(8,128)(2,1)S(1)}, u32[]{:S(2)}, u32[]{:S(2)}) collective-permute-start(bf16[272,128]{1,0:T(8,128)(2,1)S(1)} %get-tuple-element.278), channel_id=1, source_target_pairs={{0,2},{2,0},{4,6},{6,4},{1,3},{3,1},{5,7},{7,5},{8,10},{10,8},{12,... | collective-permute-start | bytes 208904 | tf_op jit(solution)/shard_map/shared_ctx_1/ppermute | solution.py:870
  225.6 4.3 %collective-permute-start.27 = (bf16[272,128]{1,0:T(8,128)(2,1)S(1)}, bf16[272,128]{1,0:T(8,128)(2,1)S(1)}, u32[]{:S(2)}, u32[]{:S(2)}) collective-permute-start(bf16[272,128]{1,0:T(8,128)(2,1)S(1)} %get-tuple-element.280), channel_id=1, source_target_pairs={{0,4},{2,6},{4,0},{6,2},{1,5},{3,7},{5,1},{7,3},{8,12},{10,14},{12... | collective-permute-start | bytes 208904 | tf_op jit(solution)/shard_map/shared_ctx_2/ppermute | solution.py:870
  226.5 5.2 %collective-permute-start.28 = (bf16[272,128]{1,0:T(8,128)(2,1)S(1)}, bf16[272,128]{1,0:T(8,128)(2,1)S(1)}, u32[]{:S(2)}, u32[]{:S(2)}) collective-permute-start(bf16[272,128]{1,0:T(8,128)(2,1)S(1)} %get-tuple-element.279), channel_id=1, source_target_pairs={{0,6},{2,4},{4,2},{6,0},{1,7},{3,5},{5,3},{7,1},{8,14},{10,12},{12... | collective-permute-start | bytes 208904 | tf_op jit(solution)/shard_map/shared_ctx_3/ppermute | solution.py:870
  231.8 7.7 %collective-permute-start.29 = (bf16[272,128]{1,0:T(8,128)(2,1)S(1)}, bf16[272,128]{1,0:T(8,128)(2,1)S(1)}, u32[]{:S(2)}, u32[]{:S(2)}) collective-permute-start(bf16[272,128]{1,0:T(8,128)(2,1)S(1)} %fusion.6), channel_id=1, source_target_pairs={{0,2},{2,0},{4,6},{6,4},{1,3},{3,1},{5,7},{7,5},{8,10},{10,8},{12,... | collective-permute-start | bytes 208904 | tf_op jit(solution)/shard_map/shared_sums_ctx_1/ppermute | solution.py:870
  233.2 6.4 %collective-permute-start.30 = (bf16[272,128]{1,0:T(8,128)(2,1)S(1)}, bf16[272,128]{1,0:T(8,128)(2,1)S(1)}, u32[]{:S(2)}, u32[]{:S(2)}) collective-permute-start(bf16[272,128]{1,0:T(8,128)(2,1)S(1)} %fusion.6), channel_id=1, source_target_pairs={{0,4},{2,6},{4,0},{6,2},{1,5},{3,7},{5,1},{7,3},{8,12},{10,14},{12... | collective-permute-start | bytes 208904 | tf_op jit(solution)/shard_map/shared_sums_ctx_2/ppermute | solution.py:870
  234.2 5.3 %collective-permute-start.31 = (bf16[272,128]{1,0:T(8,128)(2,1)S(1)}, bf16[272,128]{1,0:T(8,128)(2,1)S(1)}, u32[]{:S(2)}, u32[]{:S(2)}) collective-permute-start(bf16[272,128]{1,0:T(8,128)(2,1)S(1)} %fusion.6), channel_id=1, source_target_pairs={{0,6},{2,4},{4,2},{6,0},{1,7},{3,5},{5,3},{7,1},{8,14},{10,12},{12... | collective-permute-start | bytes 208904 | tf_op jit(solution)/shard_map/shared_sums_ctx_3/ppermute | solution.py:870
  239.6 2.7 %collective-permute-start.33 = (bf16[4,272,128]{2,1,0:T(8,128)(2,1)S(1)}, bf16[4,272,128]{2,1,0:T(8,128)(2,1)S(1)}, u32[]{:S(2)}, u32[]{:S(2)}) collective-permute-start(bf16[4,272,128]{2,1,0:T(8,128)(2,1)S(1)} %pad_maximum_fusion.1.refs_0_), channel_id=1, source_target_pairs={{0,1},{1,0},{2,3},{3,2},{4,5},{5,4},{6,7},{7,6},{8,9},{9,8},{10,11... | collective-permute-start | bytes 835592 | tf_op jit(solution)/shard_map/shared_sums_dp_1/ppermute | solution.py:870
  (34 other events, 140.5 us)
